TPU v7x, 128 devices: a whole 4x4x4 slice. The times are simulated.
128 devices in a mesh: blk: 16 (over y_lo, z, core), bin: 8 (over x, y_hi).
Axes of the slice: x: 4, y: 4 (y_hi: 2, y_lo: 2; y = y_hi * 2 + y_lo), z: 4, core: 2. Of those that a mesh axis runs over, the one named last changes fastest.
Arguments:
- spectra: bfloat16 [256, 8192, 2, 128], P('bin', 'blk'), may hold values from -48 to 48
- quality: bfloat16 [256, 8192], P('bin', 'blk'), may hold values from 0 to 1
- bins: int32 [32], replicated, may hold values from 0 to 127
Outputs:
- cross: bfloat16 [4, 2, 32, 8192, 512], P(None, None, 'bin', 'blk')
All inputs are finite; a program needn't handle non-finite values.
Results may differ from a plain program's by a relative error of at most 0.0057.
Values may be sent and summed in bfloat16 or wider, within the bound.
No kernel may reach another device: no remote copies, remote signals or barrier semaphores. Data moves between devices by JAX's collectives and lax.ppermute only.
A program may use at most 128 MiB of HBM per device.

v0:
```python
import jax
import jax.numpy as jnp
from jax import lax
from jax.sharding import PartitionSpec as P

FB = 128
HALF_SPAN = 4
ROUNDS = 4


def passed_along(value, axis, steps):
    count = lax.axis_size(axis)
    pairs = [(source, (source + steps) % count) for source in range(count)]
    return lax.ppermute(value, axis, pairs)


def whiten_local(spectra, quality, bins):
    values = spectra.astype(jnp.float32)
    power = values[:, :, 0, :] ** 2 + values[:, :, 1, :] ** 2
    offsets = jnp.arange(FB)
    band_kept = (jnp.abs(offsets[:, None] - bins[None, :]) <= HALF_SPAN).astype(jnp.float32)
    picker = (offsets[:, None] == bins[None, :]).astype(jnp.bfloat16)
    smooth_kept = jnp.einsum("wcf,fn->wnc", power, band_kept, precision=lax.Precision.HIGHEST)
    level = jnp.mean(power, axis=-1)
    picked = jnp.einsum("wcpf,fn->wpnc", spectra, picker, preferred_element_type=jnp.float32)
    scale = jnp.sqrt(smooth_kept / (2 * HALF_SPAN + 1) + 0.1 * level[:, None, :] + 1e-06)
    chosen = picked / scale[:, None, :, :] * quality.astype(jnp.float32)[:, None, None, :]
    return chosen.astype(jnp.bfloat16)


def shards(spectra, quality, bins):
    slab_windows = spectra.shape[0]
    block_channels = spectra.shape[1]
    bin_count = lax.axis_size("bin")
    chosen = whiten_local(spectra, quality, bins)
    marks = jnp.broadcast_to(
        quality[:, None, None, :], (slab_windows, 1, bin_count, block_channels)
    )
    mine, held = (
        lax.all_to_all(chosen, "bin", split_axis=2, concat_axis=0, tiled=True),
        lax.all_to_all(marks, "bin", split_axis=2, concat_axis=0, tiled=True),
    )
    held = held.reshape(slab_windows * bin_count, block_channels)
    left = jnp.stack(
        [jnp.stack([mine[:, 0], mine[:, 1]], 0), jnp.stack([mine[:, 1], -mine[:, 0]], 0)], 0
    )
    tiles = []
    for step in range(ROUNDS):
        other, other_marks = passed_along((mine, held), "blk", -(step + 1))
        product = jnp.einsum("opwfi,wpfk->ofik", left, other, preferred_element_type=jnp.float32)
        counts = jnp.einsum("wi,wk->ik", held, other_marks, preferred_element_type=jnp.float32)
        tiles.append((product * lax.rsqrt(jnp.maximum(counts, 1.0))).astype(jnp.bfloat16))
    return jnp.stack(tiles, 0)


def solution(mesh):
    return jax.shard_map(
        shards,
        mesh=mesh,
        in_specs=(P("bin", "blk", None, None), P("bin", "blk"), P()),
        out_specs=P(None, None, "bin", "blk", None),
        check_vma=False,
    )
```

profile of v0, /device:TPU:1, one launch (start us, length us, event | category | flops | bytes accessed | tf_op | source)
XLA Modules:
  0.0 427.9 jit_solution(2092063244482859667)
XLA Ops:
  0.0 1.5 broadcast_in_dim.2
  1.5 7.5 %all-to-all-start.1 = ((bf16[32,1,8,512]{3,0,1,2:T(8,128)(2,1)}), bf16[32,1,8,512]{3,0,1,2:T(8,128)(2,1)S(1)}, u32[]{:S(2)}, u32[]{:S(2)}) async-start(bf16[32,1,8,512]{3,0,1,2:T(8,128)(2,1)} %broadcast_in_dim.2), calls=%async_computation.1 | async-start | bytes 524288 | tf_op jit(solution)/shard_map/all_to_all | solution.py:41
  9.7 9.1 %convert_element_type.23 = f32[32,512,2,128]{3,2,1,0:T(2,128)} convert(bf16[32,512,2,128]{3,2,1,0:T(2,128)(2,1)} %param.3) | non-fusion elementwise | flops 4194304 | bytes 25165824 | tf_op jit(solution)/shard_map/convert_element_type | solution.py:18
  18.8 128.8 %fusion.32 = (f32[32,512]{1,0:T(8,128)S(1)}, f32[32,512,1,128]{3,2,1,0:T(1,128)}) fusion(f32[32,512,2,128]{3,2,1,0:T(2,128)} %convert_element_type.23), kind=kLoop, calls=%fused_computation.49 | loop fusion | flops 8372224 | bytes 25231360 | tf_op jit(solution)/shard_map/reduce_sum | solution.py:24
  147.6 8.4 %sqrt_bitcast_fusion = f32[32,32,512]{2,1,0:T(8,128)S(1)} fusion(f32[32,512,128]{2,1,0:T(8,128)} %bitcast.107, f32[32,512]{1,0:T(8,128)S(1)} %broadcast_multiply_fusion, s32[32]{0:T(128)S(1)} %copy-done.5), kind=kOutput, calls=%fused_computation.28 | convolution fusion | flops 806891520 | bytes 10551424 | tf_op jit(solution)/shard_map/wcf,fn->wnc/dot_general | solution.py:23
  156.0 6.4 %fusion.12 = bf16[32,2,32,512]{3,2,1,0:T(8,128)(2,1)S(1)} fusion(bf16[32,512,2,128]{3,2,1,0:T(2,128)(2,1)} %param.3, f32[32,512]{1,0:T(8,128)S(1)} %convert_element_type.24, f32[32,32,512]{2,1,0:T(8,128)S(1)} %sqrt_bitcast_fusion, s32[32]{0:T(128)S(1)} %copy-done.5), kind=kOutput, calls=%fused_computation.21 | convolution fusion | flops 271585280 | bytes 12648576 | tf_op jit(solution)/shard_map/wcpf,fn->wpnc/dot_general | solution.py:25
  162.4 3.5 copy.29
  165.8 6.6 %all-to-all-start = ((bf16[32,2,32,512]{3,1,0,2:T(2,128)(2,1)}), bf16[32,2,32,512]{3,1,0,2:T(2,128)(2,1)S(1)}, u32[]{:S(2)}, u32[]{:S(2)}) async-start(bf16[32,2,32,512]{3,1,0,2:T(2,128)(2,1)} %copy.29), calls=%async_computation | async-start | bytes 4194304 | tf_op jit(solution)/shard_map/all_to_all | solution.py:40
  172.5 1.5 collective-permute-start.1
  174.0 28.2 %all-to-all-done = bf16[32,2,32,512]{3,1,0,2:T(2,128)(2,1)S(1)} async-done(((bf16[32,2,32,512]{3,1,0,2:T(2,128)(2,1)}), bf16[32,2,32,512]{3,1,0,2:T(2,128)(2,1)S(1)}, u32[]{:S(2)}, u32[]{:S(2)}) %all-to-all-start) | async-done | bytes 2097184 | tf_op jit(solution)/shard_map/all_to_all | solution.py:40
  203.5 2.1 copy.30
  205.6 3.8 collective-permute-start.6
  209.4 6.2 %collective-permute-start.5 = (bf16[256,512]{1,0:T(8,128)(2,1)S(1)}, bf16[256,512]{1,0:T(8,128)(2,1)}, u32[]{:S(2)}, u32[]{:S(2)}) collective-permute-start(bf16[256,512]{1,0:T(8,128)(2,1)S(1)} %bitcast.117), channel_id=1, source_target_pairs={{0,104},{8,112},{16,120},{24,0},{32,8},{40,16},{48,24},{56,32},{64... | collective-permute-start | bytes 786440 | tf_op jit(solution)/shard_map/ppermute | solution.py:14
  217.0 1.4 copy.33
  218.4 55.3 %collective-permute-done.3 = bf16[256,512]{1,0:T(8,128)(2,1)} collective-permute-done((bf16[256,512]{1,0:T(8,128)(2,1)S(1)}, bf16[256,512]{1,0:T(8,128)(2,1)}, u32[]{:S(2)}, u32[]{:S(2)}) %collective-permute-start.3) | collective-permute-done | bytes 262176 | tf_op jit(solution)/shard_map/ppermute | solution.py:14
  276.3 3.3 collective-permute-start.4
  286.7 4.4 %fusion.10 = bf16[1,2,4,512,512]{3,4,1,2,0:T(8,128)(2,1)S(1)} fusion(f32[512,512]{0,1:T(8,128)S(1)} %copy-done.4, bf16[1,2,256,4,512]{4,2,1,0,3:T(8,128)(2,1)S(1)} %get-tuple-element.10, bf16[1,2,256,4,512]{4,2,1,0,3:T(8,128)(2,1)S(1)} %get-tuple-element.9, bf16[256,2,4,512]{3,0,2,1:T(8,128)(2,1)} %collective-permute-done.6), kind=kOutput, calls=%fused_computation.17 | convolution fusion | flops 2160066560 | bytes 11534336 | tf_op jit(solution)/shard_map/opwfi,wpfk->ofik/dot_general | solution.py:50
  291.1 37.6 %collective-permute-done.4 = bf16[256,2,4,512]{3,0,2,1:T(8,128)(2,1)} collective-permute-done((bf16[256,2,4,512]{3,0,2,1:T(8,128)(2,1)S(1)}, bf16[256,2,4,512]{3,0,2,1:T(8,128)(2,1)}, u32[]{:S(2)}, u32[]{:S(2)}) %collective-permute-start.4) | collective-permute-done | bytes 2097184 | tf_op jit(solution)/shard_map/ppermute | solution.py:14
  328.6 4.3 %fusion.9 = bf16[1,2,4,512,512]{3,4,1,2,0:T(8,128)(2,1)S(1)} fusion(f32[512,512]{0,1:T(8,128)S(1)} %copy-done.3, bf16[1,2,256,4,512]{4,2,1,0,3:T(8,128)(2,1)S(1)} %get-tuple-element.10, bf16[1,2,256,4,512]{4,2,1,0,3:T(8,128)(2,1)S(1)} %get-tuple-element.9, bf16[256,2,4,512]{3,0,2,1:T(8,128)(2,1)} %collective-permute-done.4), kind=kOutput, calls=%fused_computation.16 | convolution fusion | flops 2160066560 | bytes 11534336 | tf_op jit(solution)/shard_map/opwfi,wpfk->ofik/dot_general | solution.py:50
  332.9 54.3 %collective-permute-done.2 = bf16[256,2,4,512]{3,0,2,1:T(8,128)(2,1)} collective-permute-done((bf16[256,2,4,512]{3,0,2,1:T(8,128)(2,1)S(1)}, bf16[256,2,4,512]{3,0,2,1:T(8,128)(2,1)}, u32[]{:S(2)}, u32[]{:S(2)}) %collective-permute-start.2) | collective-permute-done | bytes 2097184 | tf_op jit(solution)/shard_map/ppermute | solution.py:14
  387.3 4.3 %fusion.8 = bf16[1,2,4,512,512]{3,4,1,2,0:T(8,128)(2,1)S(1)} fusion(f32[512,512]{0,1:T(8,128)S(1)} %copy-done.2, bf16[1,2,256,4,512]{4,2,1,0,3:T(8,128)(2,1)S(1)} %get-tuple-element.10, bf16[1,2,256,4,512]{4,2,1,0,3:T(8,128)(2,1)S(1)} %get-tuple-element.9, bf16[256,2,4,512]{3,0,2,1:T(8,128)(2,1)} %collective-permute-done.2), kind=kOutput, calls=%fused_computation.15 | convolution fusion | flops 2160066560 | bytes 11534336 | tf_op jit(solution)/shard_map/opwfi,wpfk->ofik/dot_general | solution.py:50
  391.6 4.3 %fusion.7 = bf16[1,2,4,512,512]{3,4,1,2,0:T(8,128)(2,1)S(1)} fusion(f32[512,512]{0,1:T(8,128)S(1)} %copy-done.1, bf16[1,2,256,4,512]{4,2,1,0,3:T(8,128)(2,1)S(1)} %get-tuple-element.10, bf16[1,2,256,4,512]{4,2,1,0,3:T(8,128)(2,1)S(1)} %get-tuple-element.9, bf16[256,2,4,512]{3,0,2,1:T(8,128)(2,1)} %collective-permute-done), kind=kOutput, calls=%fused_computation.14 | convolution fusion | flops 2160066560 | bytes 11534336 | tf_op jit(solution)/shard_map/opwfi,wpfk->ofik/dot_general | solution.py:50
  395.9 6.9 %pad_maximum_fusion = bf16[4,2,4,512,512]{3,4,1,2,0:T(8,128)(2,1)} fusion(bf16[1,2,4,512,512]{3,4,1,2,0:T(8,128)(2,1)S(1)} %fusion.10, bf16[1,2,4,512,512]{3,4,1,2,0:T(8,128)(2,1)S(1)} %fusion.9, bf16[1,2,4,512,512]{3,4,1,2,0:T(8,128)(2,1)S(1)} %fusion.8, bf16[1,2,4,512,512]{3,4,1,2,0:T(8,128)(2,1)S(1)} %fusion.7), kind=kLoop, calls=%fused_computation | loop fusion | flops 25165824 | bytes 33554432 | tf_op jit(solution)/shard_map/stack | solution.py:53
  402.8 25.1 %copy.40 = bf16[4,2,4,512,512]{4,3,2,1,0:T(8,128)(2,1)} copy(bf16[4,2,4,512,512]{3,4,1,2,0:T(8,128)(2,1)} %pad_maximum_fusion) | data formatting | bytes 33554432 | tf_op jit(solution)/shard_map/stack | solution.py:53
  (34 shorter events, 13.2 us)
Async XLA Ops:
  1.5 164.4 %all-to-all-start.1 = ((bf16[32,1,8,512]{3,0,1,2:T(8,128)(2,1)}), bf16[32,1,8,512]{3,0,1,2:T(8,128)(2,1)S(1)}, u32[]{:S(2)}, u32[]{:S(2)}) async-start(bf16[32,1,8,512]{3,0,1,2:T(8,128)(2,1)} %broadcast_in_dim.2), calls=%async_computation.1 | async-start | bytes 524288 | tf_op jit(solution)/shard_map/all_to_all | solution.py:41
  18.8 128.8 %copy-start.5 = (s32[32]{0:T(128)S(1)}, s32[32]{0:T(128)}, u32[]{:S(2)}) copy-start(s32[32]{0:T(128)} %param.5) | copy-start | bytes 388
  165.8 36.4 %all-to-all-start = ((bf16[32,2,32,512]{3,1,0,2:T(2,128)(2,1)}), bf16[32,2,32,512]{3,1,0,2:T(2,128)(2,1)S(1)}, u32[]{:S(2)}, u32[]{:S(2)}) async-start(bf16[32,2,32,512]{3,1,0,2:T(2,128)(2,1)} %copy.29), calls=%async_computation | async-start | bytes 4194304 | tf_op jit(solution)/shard_map/all_to_all | solution.py:40
  172.5 43.3 %collective-permute-start.1 = (bf16[256,512]{1,0:T(8,128)(2,1)S(1)}, bf16[256,512]{1,0:T(8,128)(2,1)}, u32[]{:S(2)}, u32[]{:S(2)}) collective-permute-start(bf16[256,512]{1,0:T(8,128)(2,1)S(1)} %bitcast.115), channel_id=1, source_target_pairs={{0,120},{8,0},{16,8},{24,16},{32,24},{40,32},{48,40},{56,48},{64,5... | collective-permute-start | bytes 786440 | tf_op jit(solution)/shard_map/ppermute | solution.py:14
  202.2 1.3 copy-start
  205.6 80.2 %collective-permute-start.6 = (bf16[256,2,4,512]{3,0,2,1:T(8,128)(2,1)S(1)}, bf16[256,2,4,512]{3,0,2,1:T(8,128)(2,1)}, u32[]{:S(2)}, u32[]{:S(2)}) collective-permute-start(bf16[256,2,4,512]{3,0,2,1:T(8,128)(2,1)S(1)} %bitcast.108), channel_id=1, source_target_pairs={{0,96},{8,104},{16,112},{24,120},{32,0},{40,8},{48,16},{56,24},{64... | collective-permute-start | bytes 6291464 | tf_op jit(solution)/shard_map/ppermute | solution.py:14
  209.4 72.9 %collective-permute-start.7 = (bf16[256,512]{1,0:T(8,128)(2,1)S(1)}, bf16[256,512]{1,0:T(8,128)(2,1)}, u32[]{:S(2)}, u32[]{:S(2)}) collective-permute-start(bf16[256,512]{1,0:T(8,128)(2,1)S(1)} %bitcast.116), channel_id=1, source_target_pairs={{0,96},{8,104},{16,112},{24,120},{32,0},{40,8},{48,16},{56,24},{64... | collective-permute-start | bytes 786440 | tf_op jit(solution)/shard_map/ppermute | solution.py:14
  209.4 70.2 %collective-permute-start.5 = (bf16[256,512]{1,0:T(8,128)(2,1)S(1)}, bf16[256,512]{1,0:T(8,128)(2,1)}, u32[]{:S(2)}, u32[]{:S(2)}) collective-permute-start(bf16[256,512]{1,0:T(8,128)(2,1)S(1)} %bitcast.117), channel_id=1, source_target_pairs={{0,104},{8,112},{16,120},{24,0},{32,8},{40,16},{48,24},{56,32},{64... | collective-permute-start | bytes 786440 | tf_op jit(solution)/shard_map/ppermute | solution.py:14
  215.6 58.1 %collective-permute-start.3 = (bf16[256,512]{1,0:T(8,128)(2,1)S(1)}, bf16[256,512]{1,0:T(8,128)(2,1)}, u32[]{:S(2)}, u32[]{:S(2)}) collective-permute-start(bf16[256,512]{1,0:T(8,128)(2,1)S(1)} %bitcast.118), channel_id=1, source_target_pairs={{0,112},{8,120},{16,0},{24,8},{32,16},{40,24},{48,32},{56,40},{64,... | collective-permute-start | bytes 786440 | tf_op jit(solution)/shard_map/ppermute | solution.py:14
  276.3 52.3 %collective-permute-start.4 = (bf16[256,2,4,512]{3,0,2,1:T(8,128)(2,1)S(1)}, bf16[256,2,4,512]{3,0,2,1:T(8,128)(2,1)}, u32[]{:S(2)}, u32[]{:S(2)}) collective-permute-start(bf16[256,2,4,512]{3,0,2,1:T(8,128)(2,1)S(1)} %bitcast.109), channel_id=1, source_target_pairs={{0,104},{8,112},{16,120},{24,0},{32,8},{40,16},{48,24},{56,32},{64... | collective-permute-start | bytes 6291464 | tf_op jit(solution)/shard_map/ppermute | solution.py:14
  284.8 102.4 %collective-permute-start.2 = (bf16[256,2,4,512]{3,0,2,1:T(8,128)(2,1)S(1)}, bf16[256,2,4,512]{3,0,2,1:T(8,128)(2,1)}, u32[]{:S(2)}, u32[]{:S(2)}) collective-permute-start(bf16[256,2,4,512]{3,0,2,1:T(8,128)(2,1)S(1)} %bitcast.110), channel_id=1, source_target_pairs={{0,112},{8,120},{16,0},{24,8},{32,16},{40,24},{48,32},{56,40},{64,... | collective-permute-start | bytes 6291464 | tf_op jit(solution)/shard_map/ppermute | solution.py:14
  284.8 106.7 %collective-permute-start = (bf16[256,2,4,512]{3,0,2,1:T(8,128)(2,1)S(1)}, bf16[256,2,4,512]{3,0,2,1:T(8,128)(2,1)}, u32[]{:S(2)}, u32[]{:S(2)}) collective-permute-start(bf16[256,2,4,512]{3,0,2,1:T(8,128)(2,1)S(1)} %bitcast.111), channel_id=1, source_target_pairs={{0,120},{8,0},{16,8},{24,16},{32,24},{40,32},{48,40},{56,48},{64,5... | collective-permute-start | bytes 6291464 | tf_op jit(solution)/shard_map/ppermute | solution.py:14
  285.4 1.2 copy-start.4
  286.7 42.0 %copy-start.3 = (f32[512,512]{0,1:T(8,128)S(1)}, f32[512,512]{0,1:T(8,128)}, u32[]{:S(2)}) copy-start(f32[512,512]{0,1:T(8,128)} %copy.37) | copy-start | bytes 3145732
  291.0 96.2 %copy-start.2 = (f32[512,512]{0,1:T(8,128)S(1)}, f32[512,512]{0,1:T(8,128)}, u32[]{:S(2)}) copy-start(f32[512,512]{0,1:T(8,128)} %copy.35) | copy-start | bytes 3145732
  332.9 58.6 %copy-start.1 = (f32[512,512]{0,1:T(8,128)S(1)}, f32[512,512]{0,1:T(8,128)}, u32[]{:S(2)}) copy-start(f32[512,512]{0,1:T(8,128)} %copy.33) | copy-start | bytes 3145732
where the time goes:
time: 430 us; the launch traced here: 428 us
  waiting for transfers between devices  175 us (41%)
  other arithmetic  146 us (34%)
  local copies, waits for them, and re-layouts  39.8 us (9%)
  matrix products  37.1 us (9%)
  starting transfers between devices  29.4 us (7%)
    ppermute x8, waiting for transfers between devices, passed_along(): return lax.ppermute(value, axis, pairs)  147 us
    reduce_sum x1, other arithmetic, whiten_local(): level = jnp.mean(power, axis=-1)  129 us
    all_to_all x1, waiting for transfers between devices, shards(): lax.all_to_all(chosen, 'bin', split_axis=2, concat_axis=0, tiled=True)  28.2 us
    another operation x1, local copies, waits for them, and re-layouts, shards(): return jnp.stack(tiles, 0)  25.1 us
    dot_general x4, matrix products, shards(): jnp.einsum('opwfi,wpfk->ofik', left, other, preferred_element_type=jnp.fl...  17.3 us
    ppermute x8, starting transfers between devices, passed_along(): return lax.ppermute(value, axis, pairs)  15.3 us
    convert_element_type x1, other arithmetic, whiten_local(): values = spectra.astype(jnp.float32)  9.06 us
  transfers between devices with their start and end apart: 10, of which 4 were waited for; matrix products, arithmetic and copies ran while one was open for 43% of the time, Pallas kernels for 0%

commit v1 on v0

v1 whole, which is shorter than its diff:
```python
import jax
import jax.numpy as jnp
from jax import lax
from jax.experimental import pallas as pl
from jax.experimental.pallas import tpu as pltpu
from jax.sharding import PartitionSpec as P

FB = 128
HALF_SPAN = 4
ROUNDS = 4
ROWS_Z = 4
WIN_STEP = 4
WIN_GROUP = 16
PIECES = 4
RELAYED = 2
MIB = 1024 * 1024


def whiten_kernel(bins_ref, x_ref, q_ref, *refs, channels, kept, shares, pieces):
    outs = refs[:pieces]
    parted, band, picker, staged = refs[pieces:]
    step = pl.program_id(0)

    @pl.when(step == 0)
    def _():
        lanes = lax.broadcasted_iota(jnp.int32, (kept, 2 * FB), 1)
        rows = lax.broadcasted_iota(jnp.int32, (kept, 2 * FB), 0)
        wanted = jnp.zeros((kept, 2 * FB), jnp.int32)
        for n in range(kept):
            wanted = jnp.where(rows == n, bins_ref[n], wanted)
        offset = jnp.where(lanes >= FB, lanes - FB, lanes)
        near = jnp.abs(offset - wanted) <= HALF_SPAN
        band[:kept] = jnp.where(near, 1.0, 0.0).astype(jnp.bfloat16)
        band[kept:] = jnp.ones((16, 2 * FB), jnp.bfloat16)
        exact = offset == wanted
        picker[:kept] = jnp.where(exact & (lanes < FB), 1.0, 0.0).astype(jnp.bfloat16)
        picker[kept:] = jnp.where(exact & (lanes >= FB), 1.0, 0.0).astype(jnp.bfloat16)

    along = (((1,), (1,)), ((), ()))
    for k in range(WIN_STEP):
        parted[k] = x_ref[k].astype(jnp.float32)
        real = parted[k, pl.ds(0, channels, stride=2), :]
        imag = parted[k, pl.ds(1, channels, stride=2), :]
        power = real * real + imag * imag
        high = power.astype(jnp.bfloat16)
        low = (power - high.astype(jnp.float32)).astype(jnp.bfloat16)
        sums = lax.dot_general(
            band[...], jnp.concatenate([high, low], 1), along, preferred_element_type=jnp.float32
        )
        both = jnp.concatenate([real.astype(jnp.bfloat16), imag.astype(jnp.bfloat16)], 1)
        picked = lax.dot_general(picker[...], both, along, preferred_element_type=jnp.float32)
        level = sums[kept:kept + 1] * (0.1 / FB) + 1e-06
        scale = lax.rsqrt(sums[:kept] * (1.0 / (2 * HALF_SPAN + 1)) + level)
        window = step * WIN_STEP + k
        gain = q_ref[pl.ds(window, 1), :] * scale
        local = lax.rem(window, WIN_GROUP)
        value = jnp.concatenate([picked[:kept] * gain, picked[kept:] * gain], 0)
        for c in range(0, channels, 128):
            staged[c // 128, pl.ds(local, 2 * kept, stride=WIN_GROUP), :] = value[:, c:c + 128]

    @pl.when(lax.rem(step, WIN_GROUP // WIN_STEP) == WIN_GROUP // WIN_STEP - 1)
    def _():
        for n in range(kept):
            share, place = n // (kept // shares), n % (kept // shares)
            for part in range(2):
                row = (part * kept + n) * WIN_GROUP
                for c in range(0, channels, 128):
                    outs[place][share, part, :, c:c + 128] = staged[c // 128, row:row + WIN_GROUP, :].astype(
                        jnp.bfloat16
                    )


def whiten(spectra, quality, bins, shares):
    windows, channels = quality.shape
    kept = bins.shape[0]
    rows = spectra.reshape(windows, channels * 2, FB)
    group = WIN_GROUP // WIN_STEP
    piece = jax.ShapeDtypeStruct((shares, 2, windows, channels), jnp.bfloat16)
    return pl.pallas_call(
        lambda *refs: whiten_kernel(*refs, channels=channels, kept=kept, shares=shares, pieces=PIECES),
        grid=(windows // WIN_STEP,),
        in_specs=[
            pl.BlockSpec(memory_space=pltpu.SMEM),
            pl.BlockSpec((WIN_STEP, channels * 2, FB), lambda i: (i, 0, 0)),
            pl.BlockSpec((windows, channels), lambda i: (0, 0)),
        ],
        out_specs=[pl.BlockSpec((shares, 2, WIN_GROUP, channels), lambda i: (0, 0, i // group, 0))] * PIECES,
        out_shape=[piece] * PIECES,
        scratch_shapes=[
            pltpu.VMEM((WIN_STEP, channels * 2, FB), jnp.float32),
            pltpu.VMEM((kept + 16, 2 * FB), jnp.bfloat16),
            pltpu.VMEM((2 * kept, 2 * FB), jnp.bfloat16),
            pltpu.VMEM((channels // 128, 2 * kept * WIN_GROUP, 128), jnp.float32),
        ],
        compiler_params=pltpu.CompilerParams(vmem_limit_bytes=40 * MIB),
        cost_estimate=pl.CostEstimate(flops=4 * 10**9, bytes_accessed=11 * 10**6, transcendentals=524288),
    )(bins, rows, quality.astype(jnp.float32))


def turn_kernel(own_ref, out_ref):
    channels = own_ref.shape[-1]
    depth = out_ref.shape[-1]
    own = own_ref[...]
    out_ref[:channels] = own.reshape(depth, channels).T
    turned = jnp.concatenate([own[:, 1:], -own[:, :1]], 1)
    out_ref[channels:] = turned.reshape(depth, channels).T


def turn(own):
    shares, _, windows, channels = own.shape
    depth = shares * 2 * windows
    return pl.pallas_call(
        turn_kernel,
        out_shape=jax.ShapeDtypeStruct((2 * channels, depth), jnp.bfloat16),
        compiler_params=pltpu.CompilerParams(vmem_limit_bytes=24 * MIB),
        cost_estimate=pl.CostEstimate(flops=0, bytes_accessed=3 * 10**6, transcendentals=0),
    )(own)


def weight_kernel(own_ref, other_ref, out_ref):
    counts = lax.dot_general(
        own_ref[...], other_ref[...], (((0,), (0,)), ((), ())), preferred_element_type=jnp.float32
    )
    out_ref[...] = lax.rsqrt(jnp.maximum(counts, 1.0))


def weights(marks):
    depth, channels = marks.shape[1:]
    return pl.pallas_call(
        weight_kernel,
        grid=(ROUNDS,),
        in_specs=[
            pl.BlockSpec((None, depth, channels), lambda r: (0, 0, 0)),
            pl.BlockSpec((None, depth, channels), lambda r: (r + 1, 0, 0)),
        ],
        out_specs=pl.BlockSpec((None, channels, channels), lambda r: (r, 0, 0)),
        out_shape=jax.ShapeDtypeStruct((ROUNDS, channels, channels), jnp.float32),
        compiler_params=pltpu.CompilerParams(vmem_limit_bytes=24 * MIB),
        cost_estimate=pl.CostEstimate(flops=5 * 10**8, bytes_accessed=5 * 10**6, transcendentals=10**6),
    )(marks, marks)


def cross_kernel(left_ref, near_ref, far_ref, weight_ref, *refs):
    out_ref = refs[-1]
    channels = out_ref.shape[-1]
    depth = left_ref.shape[-1]

    def products(other_ref):
        other = other_ref[...].reshape(depth, channels)
        for part in range(2):
            product = jnp.dot(
                left_ref[part * channels:(part + 1) * channels], other, preferred_element_type=jnp.float32
            )
            out_ref[part] = (product * weight_ref[...]).astype(jnp.bfloat16)

    @pl.when(pl.program_id(0) == 0)
    def _():
        products(near_ref)

    @pl.when(pl.program_id(0) == 1)
    def _():
        products(far_ref)


def cross(left, near, far, weight, first_round, place, held):
    depth, channels = left.shape[1], left.shape[0] // 2
    block = pl.BlockSpec(near.shape, lambda r: (0, 0, 0, 0))
    shape = jax.ShapeDtypeStruct((ROUNDS, 2, PIECES, channels, channels), jnp.bfloat16)
    extra = [] if held is None else [held]
    return pl.pallas_call(
        cross_kernel,
        grid=(2,),
        in_specs=[
            pl.BlockSpec(left.shape, lambda r: (0, 0)),
            block,
            block,
            pl.BlockSpec((None, channels, channels), lambda r: (first_round + r, 0, 0)),
        ]
        + [pl.BlockSpec(memory_space=pl.ANY)] * len(extra),
        out_specs=pl.BlockSpec((None, 2, None, channels, channels), lambda r: (first_round + r, 0, place, 0, 0)),
        out_shape=shape,
        input_output_aliases={} if held is None else {4: 0},
        compiler_params=pltpu.CompilerParams(vmem_limit_bytes=32 * MIB),
        cost_estimate=pl.CostEstimate(flops=2 * 10**9, bytes_accessed=6 * 10**6, transcendentals=0),
    )(left, near, far, weight, *extra)


def shards(spectra, quality, bins):
    blocks = lax.axis_size("blk")
    shares = lax.axis_size("bin")
    windows, channels = quality.shape
    chips = blocks // 2
    core = lax.rem(lax.axis_index("blk"), 2)

    def moved(value, pairs):
        return lax.ppermute(value, "blk", [(2 * s + c, 2 * t + c) for s, t in pairs for c in range(2)])

    def back(value):
        return moved(value, [((t + 1) % chips, t) for t in range(chips)])

    def chip(row, z):
        return (row % (chips // ROWS_Z)) * ROWS_Z + z % ROWS_Z

    every = [(row, z) for row in range(chips // ROWS_Z) for z in range(ROWS_Z)]

    def forth(value):
        return moved(value, [(chip(row, z - 1), chip(row, z)) for row, z in every])

    def forth_last(value):
        return moved(value, [(chip(row + (z + 2) // ROWS_Z, z - 1), chip(row, z)) for row, z in every])

    def swapped(value):
        return lax.ppermute(value, "blk", [(i, i ^ 1) for i in range(blocks)])

    def shifted(value, steps):
        return lax.ppermute(value, "blk", [((i + steps) % blocks, i) for i in range(blocks)])

    marks = jnp.stack([quality] + [shifted(quality, r + 1) for r in range(ROUNDS)], 0)
    marks = lax.all_gather(marks, "bin", axis=0, tiled=False)
    marks = marks.transpose(1, 0, 2, 3).reshape(ROUNDS + 1, shares * windows, channels)
    weight = weights(marks)

    sent = whiten(spectra, quality, bins, shares)
    own = [lax.all_to_all(value, "bin", split_axis=0, concat_axis=0, tiled=True) for value in sent]
    out = None
    near = [back(value) for value in own]
    left = [turn(value) for value in own]
    far = [
        back(near[place]) if place < RELAYED else forth_last(forth(own[place])) for place in range(PIECES)
    ]
    for place in range(PIECES):
        first = swapped(jnp.where(core == 1, own[place], near[place]))
        out = cross(left[place], first, near[place], weight, 0, place, out)
    for place in range(PIECES):
        third = swapped(jnp.where(core == 1, near[place], far[place]))
        out = cross(left[place], third, far[place], weight, 2, place, out)
    return out


def solution(mesh):
    return jax.shard_map(
        shards,
        mesh=mesh,
        in_specs=(P("bin", "blk", None, None), P("bin", "blk"), P()),
        out_specs=P(None, None, "bin", "blk", None),
        check_vma=False,
    )
```

time: 430 us -> 190 us (0.44)
  other arithmetic: 146 us -> 9.92 us
  waiting for transfers between devices: 175 us -> 65.9 us
  Pallas kernels: 0 us -> 41.1 us
  matrix products: 37.1 us -> 0 us
  local copies, waits for them, and re-layouts: 39.8 us -> 8.85 us
  starting transfers between devices: 29.4 us -> 49.2 us
  between operations: 0.19 us -> 13.7 us
    reduce_sum x1 -> x0, other arithmetic: 129 us -> none  [whiten_local(): level = jnp.mean(power, axis=-1)]
    ppermute x8 -> x22, waiting for transfers between devices: 147 us -> 36.6 us  [the longest x10 36.5 us: moved(): lax.ppermute(value, 'blk', [(2 * s + c, 2 * t + c) for s, t in pairs for...]
    pallas_call x0 -> x14, Pallas kernels: none -> 41.1 us  [the longest x8 26.2 us: cross(): pl.pallas_call(cross_kernel, grid=(2,), in_specs=[pl.BlockSpec(left.shape...]
    dot_general x10 -> x0, matrix products: 37.1 us -> none  [the longest x4 17.3 us: shards(): jnp.einsum('opwfi,wpfk->ofik', left, other, preferred_element_type=jnp.fl...]
    another operation x2 -> x1, local copies, waits for them, and re-layouts: 25.3 us -> 0.01 us  [shards(): jnp.stack([quality] + [shifted(quality, r + 1) for r in range(ROUNDS)], 0)]
    ppermute x8 -> x22, starting transfers between devices: 15.3 us -> 26.9 us  [the longest x10 14.2 us: moved(): lax.ppermute(value, 'blk', [(2 * s + c, 2 * t + c) for s, t in pairs for...]
    select_n x0 -> x4, other arithmetic: none -> 9.09 us  [shards(): first = swapped(jnp.where(core == 1, own[place], near[place]))]
    convert_element_type x2 -> x1, other arithmetic: 9.82 us -> 0.84 us  [whiten(): quality.astype(jnp.float32)]
  transfers between devices with their start and end apart: 10 -> 27, of which waited for: 4 -> 9; matrix products, arithmetic and copies ran while one was open for 43% -> 6% of each run, Pallas kernels for 0% -> 15%
where the time goes in v1:
time: 190 us; the launch traced here: 189 us
  waiting for transfers between devices  65.9 us (35%)
  starting transfers between devices  49.2 us (26%)
  Pallas kernels  41.1 us (22%)
  between operations  13.7 us (7%)
  other arithmetic  9.92 us (5%)
  local copies, waits for them, and re-layouts  8.85 us (5%)
    ppermute x10, waiting for transfers between devices, moved(): lax.ppermute(value, 'blk', [(2 * s + c, 2 * t + c) for s, t in pairs for...  36.5 us
    all_to_all x4, waiting for transfers between devices, shards(): lax.all_to_all(value, 'bin', split_axis=0, concat_axis=0, tiled=True)  29.3 us
    pallas_call x8, Pallas kernels, cross(): pl.pallas_call(cross_kernel, grid=(2,), in_specs=[pl.BlockSpec(left.shape...  26.2 us
    all_to_all x4, starting transfers between devices, shards(): lax.all_to_all(value, 'bin', split_axis=0, concat_axis=0, tiled=True)  22.2 us
    ppermute x10, starting transfers between devices, moved(): lax.ppermute(value, 'blk', [(2 * s + c, 2 * t + c) for s, t in pairs for...  14.2 us
    pallas_call x1, Pallas kernels, whiten(): pl.pallas_call(lambda *refs: whiten_kernel(*refs, channels=channels, kept...  10.2 us
    select_n x4, other arithmetic, shards(): first = swapped(jnp.where(core == 1, own[place], near[place]))  9.09 us
    ppermute x4, starting transfers between devices, shifted(): lax.ppermute(value, 'blk', [((i + steps) % blocks, i) for i in range(bloc...  8.47 us
  transfers between devices with their start and end apart: 27, of which 9 were waited for; matrix products, arithmetic and copies ran while one was open for 6% of the time, Pallas kernels for 15%

profile of v1, /device:TPU:1, one launch (start us, length us, event | category | flops | bytes accessed | tf_op | source)
XLA Modules:
  0.0 188.6 jit_solution(9132814930351949167)
XLA Ops:
  7.4 3.4 %copy-done.12 = bf16[32,512,2,128]{3,2,1,0:T(2,128)(2,1)S(1)} copy-done((bf16[32,512,2,128]{3,2,1,0:T(2,128)(2,1)S(1)}, bf16[32,512,2,128]{3,2,1,0:T(2,128)(2,1)}, u32[]{:S(2)}) %copy-start.12) | copy-done | bytes 8388632
  11.4 10.2 %shard_map.37 = (bf16[8,2,32,512]{3,2,1,0:T(8,128)(2,1)}, bf16[8,2,32,512]{3,2,1,0:T(8,128)(2,1)}, bf16[8,2,32,512]{3,2,1,0:T(8,128)(2,1)}, bf16[8,2,32,512]{3,2,1,0:T(8,128)(2,1)}) custom-call(s32[32]{0:T(128)S(1)} %copy-done.13, bf16[32,1024,128]{2,1,0:T(8,128)(2,1)S(1)} %bitcast.17, f32[32,512]{1,0:T(8,128)S(1)} %convert_element_type.3.refs_2_), custom_call_target="tpu_custom_call" | custom-call | flops 4000000000 | bytes 11000000 | tf_op jit(solution)/shard_map/pallas_call | solution.py:79
  21.6 7.5 %all-to-all-start.3 = ((bf16[8,2,32,512]{3,2,1,0:T(8,128)(2,1)}), bf16[8,2,32,512]{3,2,1,0:T(8,128)(2,1)S(1)}, u32[]{:S(2)}, u32[]{:S(2)}) async-start(bf16[8,2,32,512]{3,2,1,0:T(8,128)(2,1)} %get-tuple-element.12), calls=%async_computation.3 | async-start | bytes 1048576 | tf_op jit(solution)/shard_map/all_to_all | solution.py:224
  30.0 3.9 %collective-permute-start.5 = (bf16[32,512]{1,0:T(8,128)(2,1)}, bf16[32,512]{1,0:T(8,128)(2,1)S(1)}, u32[]{:S(2)}, u32[]{:S(2)}) collective-permute-start(bf16[32,512]{1,0:T(8,128)(2,1)} %param.4), channel_id=1, source_target_pairs={{16,0},{24,8},{32,16},{40,24},{48,32},{56,40},{64,48},{72,56},{80,... | collective-permute-start | bytes 98312 | tf_op jit(solution)/shard_map/ppermute | solution.py:216
  34.3 3.3 %collective-permute-start.7 = (bf16[32,512]{1,0:T(8,128)(2,1)}, bf16[32,512]{1,0:T(8,128)(2,1)S(1)}, u32[]{:S(2)}, u32[]{:S(2)}) collective-permute-start(bf16[32,512]{1,0:T(8,128)(2,1)} %param.4), channel_id=1, source_target_pairs={{32,0},{40,8},{48,16},{56,24},{64,32},{72,40},{80,48},{88,56},{96,... | collective-permute-start | bytes 98312 | tf_op jit(solution)/shard_map/ppermute | solution.py:216
  39.3 4.8 %all-to-all-start.2 = ((bf16[8,2,32,512]{3,2,1,0:T(8,128)(2,1)}), bf16[8,2,32,512]{3,2,1,0:T(8,128)(2,1)S(1)}, u32[]{:S(2)}, u32[]{:S(2)}) async-start(bf16[8,2,32,512]{3,2,1,0:T(8,128)(2,1)} %get-tuple-element.11), calls=%async_computation.2 | async-start | bytes 1048576 | tf_op jit(solution)/shard_map/all_to_all | solution.py:224
  44.2 9.0 %all-to-all-done.2.own_ref = bf16[8,2,32,512]{3,2,1,0:T(8,128)(2,1)S(1)} async-done(((bf16[8,2,32,512]{3,2,1,0:T(8,128)(2,1)}), bf16[8,2,32,512]{3,2,1,0:T(8,128)(2,1)S(1)}, u32[]{:S(2)}, u32[]{:S(2)}) %all-to-all-start.2) | async-done | bytes 524320 | tf_op jit(solution)/shard_map/all_to_all | solution.py:224
  53.2 4.9 %all-to-all-start.1 = ((bf16[8,2,32,512]{3,2,1,0:T(8,128)(2,1)}), bf16[8,2,32,512]{3,2,1,0:T(8,128)(2,1)}, u32[]{:S(2)}, u32[]{:S(2)}) async-start(bf16[8,2,32,512]{3,2,1,0:T(8,128)(2,1)} %get-tuple-element.10), calls=%async_computation.1 | async-start | bytes 1048576 | tf_op jit(solution)/shard_map/all_to_all | solution.py:224
  61.6 5.2 %all-to-all-done.1.own_ref = bf16[8,2,32,512]{3,2,1,0:T(8,128)(2,1)} async-done(((bf16[8,2,32,512]{3,2,1,0:T(8,128)(2,1)}), bf16[8,2,32,512]{3,2,1,0:T(8,128)(2,1)}, u32[]{:S(2)}, u32[]{:S(2)}) %all-to-all-start.1) | async-done | bytes 524320 | tf_op jit(solution)/shard_map/all_to_all | solution.py:224
  66.8 5.0 %all-to-all-start = ((bf16[8,2,32,512]{3,2,1,0:T(8,128)(2,1)}), bf16[8,2,32,512]{3,2,1,0:T(8,128)(2,1)}, u32[]{:S(2)}, u32[]{:S(2)}) async-start(bf16[8,2,32,512]{3,2,1,0:T(8,128)(2,1)} %get-tuple-element.9), calls=%async_computation | async-start | bytes 1048576 | tf_op jit(solution)/shard_map/all_to_all | solution.py:224
  74.5 13.3 %all-to-all-done.own_ref = bf16[8,2,32,512]{3,2,1,0:T(8,128)(2,1)} async-done(((bf16[8,2,32,512]{3,2,1,0:T(8,128)(2,1)}), bf16[8,2,32,512]{3,2,1,0:T(8,128)(2,1)}, u32[]{:S(2)}, u32[]{:S(2)}) %all-to-all-start) | async-done | bytes 524320 | tf_op jit(solution)/shard_map/all_to_all | solution.py:224
  87.8 2.8 %collective-permute-start.16 = (bf16[8,2,32,512]{3,2,1,0:T(8,128)(2,1)}, bf16[8,2,32,512]{3,2,1,0:T(8,128)(2,1)}, u32[]{:S(2)}, u32[]{:S(2)}) collective-permute-start(bf16[8,2,32,512]{3,2,1,0:T(8,128)(2,1)} %collective-permute-done.15.far_ref), channel_id=1, source_target_pairs={{16,0},{24,8},{32,16},{40,24},{48,32},{56,40},{64,48},{72,56},{80,... | collective-permute-start | bytes 1572872 | tf_op jit(solution)/shard_map/ppermute | solution.py:196
  90.6 4.0 %collective-permute-done.12.far_ref = bf16[8,2,32,512]{3,2,1,0:T(8,128)(2,1)} collective-permute-done((bf16[8,2,32,512]{3,2,1,0:T(8,128)(2,1)S(1)}, bf16[8,2,32,512]{3,2,1,0:T(8,128)(2,1)}, u32[]{:S(2)}, u32[]{:S(2)}) %collective-permute-start.12) | collective-permute-done | bytes 524320 | tf_op jit(solution)/shard_map/ppermute | solution.py:196
  94.6 4.4 %collective-permute-start.13 = (bf16[8,2,32,512]{3,2,1,0:T(8,128)(2,1)}, bf16[8,2,32,512]{3,2,1,0:T(8,128)(2,1)}, u32[]{:S(2)}, u32[]{:S(2)}) collective-permute-start(bf16[8,2,32,512]{3,2,1,0:T(8,128)(2,1)} %collective-permute-done.12.far_ref), channel_id=1, source_target_pairs={{16,0},{24,8},{32,16},{40,24},{48,32},{56,40},{64,48},{72,56},{80,... | collective-permute-start | bytes 1572872 | tf_op jit(solution)/shard_map/ppermute | solution.py:196
  104.6 8.4 %collective-permute-done.16.far_ref = bf16[8,2,32,512]{3,2,1,0:T(8,128)(2,1)} collective-permute-done((bf16[8,2,32,512]{3,2,1,0:T(8,128)(2,1)}, bf16[8,2,32,512]{3,2,1,0:T(8,128)(2,1)}, u32[]{:S(2)}, u32[]{:S(2)}) %collective-permute-start.16) | collective-permute-done | bytes 524320 | tf_op jit(solution)/shard_map/ppermute | solution.py:196
  115.2 9.0 %collective-permute-done.13.far_ref = bf16[8,2,32,512]{3,2,1,0:T(8,128)(2,1)} collective-permute-done((bf16[8,2,32,512]{3,2,1,0:T(8,128)(2,1)}, bf16[8,2,32,512]{3,2,1,0:T(8,128)(2,1)}, u32[]{:S(2)}, u32[]{:S(2)}) %collective-permute-start.13) | collective-permute-done | bytes 524320 | tf_op jit(solution)/shard_map/ppermute | solution.py:196
  127.9 7.6 %collective-permute-done.8.far_ref = bf16[8,2,32,512]{3,2,1,0:T(8,128)(2,1)S(1)} collective-permute-done((bf16[8,2,32,512]{3,2,1,0:T(8,128)(2,1)}, bf16[8,2,32,512]{3,2,1,0:T(8,128)(2,1)S(1)}, u32[]{:S(2)}, u32[]{:S(2)}) %collective-permute-start.8) | collective-permute-done | bytes 524320 | tf_op jit(solution)/shard_map/ppermute | solution.py:196
  139.1 7.6 %collective-permute-done.far_ref = bf16[8,2,32,512]{3,2,1,0:T(8,128)(2,1)S(1)} collective-permute-done((bf16[8,2,32,512]{3,2,1,0:T(8,128)(2,1)}, bf16[8,2,32,512]{3,2,1,0:T(8,128)(2,1)S(1)}, u32[]{:S(2)}, u32[]{:S(2)}) %collective-permute-start) | collective-permute-done | bytes 524320 | tf_op jit(solution)/shard_map/ppermute | solution.py:196
  154.6 3.6 %shard_map.43.refs_0_ = bf16[4,2,4,512,512]{4,3,2,1,0:T(8,128)(2,1)} custom-call(bf16[1024,512]{1,0:T(8,128)(2,1)S(1)} %copy-done.1, bf16[8,2,32,512]{3,2,1,0:T(8,128)(2,1)} %collective-permute-done.21.near_ref, bf16[8,2,32,512]{3,2,1,0:T(8,128)(2,1)} %collective-permute-done.15.far_ref, f32[4,512,512]{2,1,0:T(8,128)S(1)} %shard_map.39.weight_ref), custom_call_target="tpu_custom_call" | custom-call | flops 2000000000 | bytes 6000000 | tf_op jit(solution)/shard_map/pallas_call | solution.py:170
  159.0 3.6 %shard_map.44.refs_0_ = bf16[4,2,4,512,512]{4,3,2,1,0:T(8,128)(2,1)} custom-call(bf16[1024,512]{1,0:T(8,128)(2,1)S(1)} %shard_map.41.left_ref, bf16[8,2,32,512]{3,2,1,0:T(8,128)(2,1)} %collective-permute-done.20.near_ref, bf16[8,2,32,512]{3,2,1,0:T(8,128)(2,1)} %collective-permute-done.12.far_ref, ...), custom_call_target="tpu_custom_call", output_to_operand_aliasing={{}: (4, {})} | custom-call | flops 2000000000 | bytes 6000000 | tf_op jit(solution)/shard_map/pallas_call | solution.py:170
  162.8 3.5 %shard_map.45.refs_0_ = bf16[4,2,4,512,512]{4,3,2,1,0:T(8,128)(2,1)} custom-call(bf16[1024,512]{1,0:T(8,128)(2,1)S(1)} %shard_map.40.left_ref, bf16[8,2,32,512]{3,2,1,0:T(8,128)(2,1)} %collective-permute-done.19.near_ref, bf16[8,2,32,512]{3,2,1,0:T(8,128)(2,1)S(1)} %copy-done.9, ...), custom_call_target="tpu_custom_call", output_to_operand_aliasing={{}: (4, {})} | custom-call | flops 2000000000 | bytes 6000000 | tf_op jit(solution)/shard_map/pallas_call | solution.py:170
  166.3 3.5 %shard_map.46.refs_0_ = bf16[4,2,4,512,512]{4,3,2,1,0:T(8,128)(2,1)} custom-call(bf16[1024,512]{1,0:T(8,128)(2,1)S(1)} %shard_map.38.left_ref, bf16[8,2,32,512]{3,2,1,0:T(8,128)(2,1)} %collective-permute-done.18.near_ref, bf16[8,2,32,512]{3,2,1,0:T(8,128)(2,1)S(1)} %copy-done.11, ...), custom_call_target="tpu_custom_call", output_to_operand_aliasing={{}: (4, {})} | custom-call | flops 2000000000 | bytes 6000000 | tf_op jit(solution)/shard_map/pallas_call | solution.py:170
  169.7 3.6 %shard_map.47.refs_0_ = bf16[4,2,4,512,512]{4,3,2,1,0:T(8,128)(2,1)} custom-call(bf16[1024,512]{1,0:T(8,128)(2,1)S(1)} %copy-done.1, bf16[8,2,32,512]{3,2,1,0:T(8,128)(2,1)} %collective-permute-done.17.near_ref, bf16[8,2,32,512]{3,2,1,0:T(8,128)(2,1)} %collective-permute-done.16.far_ref, ...), custom_call_target="tpu_custom_call", output_to_operand_aliasing={{}: (4, {})} | custom-call | flops 2000000000 | bytes 6000000 | tf_op jit(solution)/shard_map/pallas_call | solution.py:170
  173.4 3.5 %shard_map.48.refs_0_ = bf16[4,2,4,512,512]{4,3,2,1,0:T(8,128)(2,1)} custom-call(bf16[1024,512]{1,0:T(8,128)(2,1)S(1)} %shard_map.41.left_ref, bf16[8,2,32,512]{3,2,1,0:T(8,128)(2,1)S(1)} %collective-permute-done.14.near_ref, bf16[8,2,32,512]{3,2,1,0:T(8,128)(2,1)} %collective-permute-done.13.far_ref, ...), custom_call_target="tpu_custom_call", output_to_operand_aliasing={{}: (4, {})} | custom-call | flops 2000000000 | bytes 6000000 | tf_op jit(solution)/shard_map/pallas_call | solution.py:170
  (92 shorter events, 39.5 us)
Async XLA Ops:
  21.6 17.8 %all-to-all-start.3 = ((bf16[8,2,32,512]{3,2,1,0:T(8,128)(2,1)}), bf16[8,2,32,512]{3,2,1,0:T(8,128)(2,1)S(1)}, u32[]{:S(2)}, u32[]{:S(2)}) async-start(bf16[8,2,32,512]{3,2,1,0:T(8,128)(2,1)} %get-tuple-element.12), calls=%async_computation.3 | async-start | bytes 1048576 | tf_op jit(solution)/shard_map/all_to_all | solution.py:224
  29.1 15.1 %collective-permute-start.4 = (bf16[32,512]{1,0:T(8,128)(2,1)}, bf16[32,512]{1,0:T(8,128)(2,1)S(1)}, u32[]{:S(2)}, u32[]{:S(2)}) collective-permute-start(bf16[32,512]{1,0:T(8,128)(2,1)} %param.4), channel_id=1, source_target_pairs={{8,0},{16,8},{24,16},{32,24},{40,32},{48,40},{56,48},{64,56},{72,6... | collective-permute-start | bytes 98312 | tf_op jit(solution)/shard_map/ppermute | solution.py:216
  33.9 24.2 %collective-permute-start.6 = (bf16[32,512]{1,0:T(8,128)(2,1)}, bf16[32,512]{1,0:T(8,128)(2,1)S(1)}, u32[]{:S(2)}, u32[]{:S(2)}) collective-permute-start(bf16[32,512]{1,0:T(8,128)(2,1)} %param.4), channel_id=1, source_target_pairs={{24,0},{32,8},{40,16},{48,24},{56,32},{64,40},{72,48},{80,56},{88,... | collective-permute-start | bytes 98312 | tf_op jit(solution)/shard_map/ppermute | solution.py:216
  34.3 23.9 %collective-permute-start.7 = (bf16[32,512]{1,0:T(8,128)(2,1)}, bf16[32,512]{1,0:T(8,128)(2,1)S(1)}, u32[]{:S(2)}, u32[]{:S(2)}) collective-permute-start(bf16[32,512]{1,0:T(8,128)(2,1)} %param.4), channel_id=1, source_target_pairs={{32,0},{40,8},{48,16},{56,24},{64,32},{72,40},{80,48},{88,56},{96,... | collective-permute-start | bytes 98312 | tf_op jit(solution)/shard_map/ppermute | solution.py:216
  58.1 92.3 %all-gather.3.cloned.1.call-start = ((), (), s32[]{:S(2)}) async-start(), calls=%async_computation.4 | async-start | bytes 1474560 | tf_op jit(solution)/shard_map/all_gather | solution.py:219
  58.9 29.0 %collective-permute-start.15 = (bf16[8,2,32,512]{3,2,1,0:T(8,128)(2,1)S(1)}, bf16[8,2,32,512]{3,2,1,0:T(8,128)(2,1)}, u32[]{:S(2)}, u32[]{:S(2)}) collective-permute-start(bf16[8,2,32,512]{3,2,1,0:T(8,128)(2,1)S(1)} %all-to-all-done.3.own_ref), channel_id=1, source_target_pairs={{16,0},{24,8},{32,16},{40,24},{48,32},{56,40},{64,48},{72,56},{80,... | collective-permute-start | bytes 1572872 | tf_op jit(solution)/shard_map/ppermute | solution.py:196
  66.8 21.0 %all-to-all-start = ((bf16[8,2,32,512]{3,2,1,0:T(8,128)(2,1)}), bf16[8,2,32,512]{3,2,1,0:T(8,128)(2,1)}, u32[]{:S(2)}, u32[]{:S(2)}) async-start(bf16[8,2,32,512]{3,2,1,0:T(8,128)(2,1)} %get-tuple-element.9), calls=%async_computation | async-start | bytes 1048576 | tf_op jit(solution)/shard_map/all_to_all | solution.py:224
  71.8 22.8 %collective-permute-start.12 = (bf16[8,2,32,512]{3,2,1,0:T(8,128)(2,1)S(1)}, bf16[8,2,32,512]{3,2,1,0:T(8,128)(2,1)}, u32[]{:S(2)}, u32[]{:S(2)}) collective-permute-start(bf16[8,2,32,512]{3,2,1,0:T(8,128)(2,1)S(1)} %all-to-all-done.2.own_ref), channel_id=1, source_target_pairs={{16,0},{24,8},{32,16},{40,24},{48,32},{56,40},{64,48},{72,56},{80,... | collective-permute-start | bytes 1572872 | tf_op jit(solution)/shard_map/ppermute | solution.py:196
  74.5 28.6 %collective-permute-start.9 = (bf16[8,2,32,512]{3,2,1,0:T(8,128)(2,1)}, bf16[8,2,32,512]{3,2,1,0:T(8,128)(2,1)}, u32[]{:S(2)}, u32[]{:S(2)}) collective-permute-start(bf16[8,2,32,512]{3,2,1,0:T(8,128)(2,1)} %all-to-all-done.1.own_ref), channel_id=1, source_target_pairs={{48,0},{56,8},{0,16},{8,24},{16,32},{24,40},{32,48},{40,56},{112,6... | collective-permute-start | bytes 1572872 | tf_op jit(solution)/shard_map/ppermute | solution.py:196
  87.8 15.3 %collective-permute-start.1 = (bf16[8,2,32,512]{3,2,1,0:T(8,128)(2,1)}, bf16[8,2,32,512]{3,2,1,0:T(8,128)(2,1)}, u32[]{:S(2)}, u32[]{:S(2)}) collective-permute-start(bf16[8,2,32,512]{3,2,1,0:T(8,128)(2,1)} %all-to-all-done.own_ref), channel_id=1, source_target_pairs={{48,0},{56,8},{0,16},{8,24},{16,32},{24,40},{32,48},{40,56},{112,6... | collective-permute-start | bytes 1572872 | tf_op jit(solution)/shard_map/ppermute | solution.py:196
  87.8 25.1 %collective-permute-start.16 = (bf16[8,2,32,512]{3,2,1,0:T(8,128)(2,1)}, bf16[8,2,32,512]{3,2,1,0:T(8,128)(2,1)}, u32[]{:S(2)}, u32[]{:S(2)}) collective-permute-start(bf16[8,2,32,512]{3,2,1,0:T(8,128)(2,1)} %collective-permute-done.15.far_ref), channel_id=1, source_target_pairs={{16,0},{24,8},{32,16},{40,24},{48,32},{56,40},{64,48},{72,56},{80,... | collective-permute-start | bytes 1572872 | tf_op jit(solution)/shard_map/ppermute | solution.py:196
  94.6 29.6 %collective-permute-start.13 = (bf16[8,2,32,512]{3,2,1,0:T(8,128)(2,1)}, bf16[8,2,32,512]{3,2,1,0:T(8,128)(2,1)}, u32[]{:S(2)}, u32[]{:S(2)}) collective-permute-start(bf16[8,2,32,512]{3,2,1,0:T(8,128)(2,1)} %collective-permute-done.12.far_ref), channel_id=1, source_target_pairs={{16,0},{24,8},{32,16},{40,24},{48,32},{56,40},{64,48},{72,56},{80,... | collective-permute-start | bytes 1572872 | tf_op jit(solution)/shard_map/ppermute | solution.py:196
  99.7 35.7 %collective-permute-start.8 = (bf16[8,2,32,512]{3,2,1,0:T(8,128)(2,1)}, bf16[8,2,32,512]{3,2,1,0:T(8,128)(2,1)S(1)}, u32[]{:S(2)}, u32[]{:S(2)}) collective-permute-start(bf16[8,2,32,512]{3,2,1,0:T(8,128)(2,1)} %all-to-all-done.1.own_ref), channel_id=1, source_target_pairs={{16,0},{24,8},{32,16},{40,24},{48,32},{56,40},{64,48},{72,56},{80,... | collective-permute-start | bytes 1572872 | tf_op jit(solution)/shard_map/ppermute | solution.py:196
  103.1 43.6 %collective-permute-start = (bf16[8,2,32,512]{3,2,1,0:T(8,128)(2,1)}, bf16[8,2,32,512]{3,2,1,0:T(8,128)(2,1)S(1)}, u32[]{:S(2)}, u32[]{:S(2)}) collective-permute-start(bf16[8,2,32,512]{3,2,1,0:T(8,128)(2,1)} %all-to-all-done.own_ref), channel_id=1, source_target_pairs={{16,0},{24,8},{32,16},{40,24},{48,32},{56,40},{64,48},{72,56},{80,... | collective-permute-start | bytes 1572872 | tf_op jit(solution)/shard_map/ppermute | solution.py:196
  103.2 33.7 %collective-permute-start.10 = (bf16[8,2,32,512]{3,2,1,0:T(8,128)(2,1)}, bf16[8,2,32,512]{3,2,1,0:T(8,128)(2,1)S(1)}, u32[]{:S(2)}, u32[]{:S(2)}) collective-permute-start(bf16[8,2,32,512]{3,2,1,0:T(8,128)(2,1)} %collective-permute-done.9), channel_id=1, source_target_pairs={{48,0},{56,8},{0,16},{8,24},{80,32},{88,40},{96,48},{104,56},{112,... | collective-permute-start | bytes 1572872 | tf_op jit(solution)/shard_map/ppermute | solution.py:196
  113.0 33.7 %collective-permute-start.2 = (bf16[8,2,32,512]{3,2,1,0:T(8,128)(2,1)}, bf16[8,2,32,512]{3,2,1,0:T(8,128)(2,1)S(1)}, u32[]{:S(2)}, u32[]{:S(2)}) collective-permute-start(bf16[8,2,32,512]{3,2,1,0:T(8,128)(2,1)} %collective-permute-done.1), channel_id=1, source_target_pairs={{48,0},{56,8},{0,16},{8,24},{80,32},{88,40},{96,48},{104,56},{112,... | collective-permute-start | bytes 1572872 | tf_op jit(solution)/shard_map/ppermute | solution.py:196
  124.2 29.0 %collective-permute-start.21 = (bf16[8,2,32,512]{3,2,1,0:T(8,128)(2,1)}, bf16[8,2,32,512]{3,2,1,0:T(8,128)(2,1)}, u32[]{:S(2)}, u32[]{:S(2)}) collective-permute-start(bf16[8,2,32,512]{3,2,1,0:T(8,128)(2,1)} %get-tuple-element.13), channel_id=1, source_target_pairs={{0,8},{8,0},{16,24},{24,16},{32,40},{40,32},{48,56},{56,48},{64,72... | collective-permute-start | bytes 1572872 | tf_op jit(solution)/shard_map/ppermute | solution.py:213
  135.4 22.8 %collective-permute-start.20 = (bf16[8,2,32,512]{3,2,1,0:T(8,128)(2,1)}, bf16[8,2,32,512]{3,2,1,0:T(8,128)(2,1)}, u32[]{:S(2)}, u32[]{:S(2)}) collective-permute-start(bf16[8,2,32,512]{3,2,1,0:T(8,128)(2,1)} %get-tuple-element.15), channel_id=1, source_target_pairs={{0,8},{8,0},{16,24},{24,16},{32,40},{40,32},{48,56},{56,48},{64,72... | collective-permute-start | bytes 1572872 | tf_op jit(solution)/shard_map/ppermute | solution.py:213
  139.1 23.5 %collective-permute-start.19 = (bf16[8,2,32,512]{3,2,1,0:T(8,128)(2,1)}, bf16[8,2,32,512]{3,2,1,0:T(8,128)(2,1)}, u32[]{:S(2)}, u32[]{:S(2)}) collective-permute-start(bf16[8,2,32,512]{3,2,1,0:T(8,128)(2,1)} %get-tuple-element.17), channel_id=1, source_target_pairs={{0,8},{8,0},{16,24},{24,16},{32,40},{40,32},{48,56},{56,48},{64,72... | collective-permute-start | bytes 1572872 | tf_op jit(solution)/shard_map/ppermute | solution.py:213
  149.8 16.4 %collective-permute-start.18 = (bf16[8,2,32,512]{3,2,1,0:T(8,128)(2,1)}, bf16[8,2,32,512]{3,2,1,0:T(8,128)(2,1)}, u32[]{:S(2)}, u32[]{:S(2)}) collective-permute-start(bf16[8,2,32,512]{3,2,1,0:T(8,128)(2,1)} %get-tuple-element.19), channel_id=1, source_target_pairs={{0,8},{8,0},{16,24},{24,16},{32,40},{40,32},{48,56},{56,48},{64,72... | collective-permute-start | bytes 1572872 | tf_op jit(solution)/shard_map/ppermute | solution.py:213
  149.8 19.9 %collective-permute-start.17 = (bf16[8,2,32,512]{3,2,1,0:T(8,128)(2,1)}, bf16[8,2,32,512]{3,2,1,0:T(8,128)(2,1)}, u32[]{:S(2)}, u32[]{:S(2)}) collective-permute-start(bf16[8,2,32,512]{3,2,1,0:T(8,128)(2,1)} %get-tuple-element.14), channel_id=1, source_target_pairs={{0,8},{8,0},{16,24},{24,16},{32,40},{40,32},{48,56},{56,48},{64,72... | collective-permute-start | bytes 1572872 | tf_op jit(solution)/shard_map/ppermute | solution.py:213
  153.3 20.1 %collective-permute-start.14 = (bf16[8,2,32,512]{3,2,1,0:T(8,128)(2,1)}, bf16[8,2,32,512]{3,2,1,0:T(8,128)(2,1)S(1)}, u32[]{:S(2)}, u32[]{:S(2)}) collective-permute-start(bf16[8,2,32,512]{3,2,1,0:T(8,128)(2,1)} %get-tuple-element.16), channel_id=1, source_target_pairs={{0,8},{8,0},{16,24},{24,16},{32,40},{40,32},{48,56},{56,48},{64,72... | collective-permute-start | bytes 1572872 | tf_op jit(solution)/shard_map/ppermute | solution.py:213
  158.3 18.6 %collective-permute-start.11 = (bf16[8,2,32,512]{3,2,1,0:T(8,128)(2,1)S(1)}, bf16[8,2,32,512]{3,2,1,0:T(8,128)(2,1)S(1)}, u32[]{:S(2)}, u32[]{:S(2)}) collective-permute-start(bf16[8,2,32,512]{3,2,1,0:T(8,128)(2,1)S(1)} %copy-done.14), channel_id=1, source_target_pairs={{0,8},{8,0},{16,24},{24,16},{32,40},{40,32},{48,56},{56,48},{64,72... | collective-permute-start | bytes 1572872 | tf_op jit(solution)/shard_map/ppermute | solution.py:213
  162.6 16.8 %collective-permute-start.3 = (bf16[8,2,32,512]{3,2,1,0:T(8,128)(2,1)S(1)}, bf16[8,2,32,512]{3,2,1,0:T(8,128)(2,1)S(1)}, u32[]{:S(2)}, u32[]{:S(2)}) collective-permute-start(bf16[8,2,32,512]{3,2,1,0:T(8,128)(2,1)S(1)} %copy-done.15), channel_id=1, source_target_pairs={{0,8},{8,0},{16,24},{24,16},{32,40},{40,32},{48,56},{56,48},{64,72... | collective-permute-start | bytes 1572872 | tf_op jit(solution)/shard_map/ppermute | solution.py:213
  (21 other events, 250.1 us)
Sparse Core Ops, SparseCore 0:
  61.2 60.7 all-gather.2

commit v2 on v1

v2 whole, which is shorter than its diff:
```python
import jax
import jax.numpy as jnp
from jax import lax
from jax.experimental import pallas as pl
from jax.experimental.pallas import tpu as pltpu
from jax.sharding import PartitionSpec as P

FB = 128
HALF_SPAN = 4
ROUNDS = 4
ROWS_Z = 4
WIN_STEP = 8
WIN_GROUP = 16
PIECES = 2
CHUNKS = 2
MIB = 1024 * 1024
COST = 1000


def taking(micros):
    return pl.CostEstimate(flops=int(micros * COST), bytes_accessed=1000, transcendentals=0)


def whiten_kernel(bins_ref, x_ref, q_ref, *refs, channels, kept, shares, pieces):
    outs = refs[:pieces]
    parted, band, picker, staged, quality = refs[pieces:]
    depth = kept // shares // pieces
    step = pl.program_id(0)
    group = pl.multiple_of(step * WIN_STEP // WIN_GROUP * WIN_GROUP, WIN_GROUP)

    @pl.when(step == 0)
    def _():
        quality[...] = q_ref[...].astype(jnp.float32)
        lanes = lax.broadcasted_iota(jnp.int32, (kept, 2 * FB), 1)
        rows = lax.broadcasted_iota(jnp.int32, (kept, 2 * FB), 0)
        wanted = jnp.zeros((kept, 2 * FB), jnp.int32)
        for n in range(kept):
            wanted = jnp.where(rows == n, bins_ref[n], wanted)
        offset = jnp.where(lanes >= FB, lanes - FB, lanes)
        near = jnp.abs(offset - wanted) <= HALF_SPAN
        band[:kept] = jnp.where(near, 1.0, 0.0).astype(jnp.bfloat16)
        band[kept:] = jnp.ones((16, 2 * FB), jnp.bfloat16)
        exact = offset == wanted
        picker[:kept] = jnp.where(exact & (lanes < FB), 1.0, 0.0).astype(jnp.bfloat16)
        picker[kept:] = jnp.where(exact & (lanes >= FB), 1.0, 0.0).astype(jnp.bfloat16)

    along = (((1,), (1,)), ((), ()))
    for k in range(WIN_STEP):
        parted[k] = x_ref[k].astype(jnp.float32)
        real = parted[k, pl.ds(0, channels, stride=2), :]
        imag = parted[k, pl.ds(1, channels, stride=2), :]
        power = real * real + imag * imag
        high = power.astype(jnp.bfloat16)
        low = (power - high.astype(jnp.float32)).astype(jnp.bfloat16)
        sums = lax.dot_general(
            band[...], jnp.concatenate([high, low], 1), along, preferred_element_type=jnp.float32
        )
        both = jnp.concatenate([real.astype(jnp.bfloat16), imag.astype(jnp.bfloat16)], 1)
        picked = lax.dot_general(picker[...], both, along, preferred_element_type=jnp.float32)
        level = sums[kept:kept + 1] * (0.1 / FB) + 1e-06
        scale = lax.rsqrt(sums[:kept] * (1.0 / (2 * HALF_SPAN + 1)) + level)
        window = step * WIN_STEP + k
        gain = quality[pl.ds(window, 1), :] * scale
        local = lax.rem(window, WIN_GROUP)
        value = jnp.concatenate([picked[:kept] * gain, picked[kept:] * gain], 0)
        for c in range(0, channels, 128):
            staged[c // 128, pl.ds(local, 2 * kept, stride=WIN_GROUP), :] = value[:, c:c + 128]

    @pl.when(lax.rem(step, WIN_GROUP // WIN_STEP) == WIN_GROUP // WIN_STEP - 1)
    def _():
        for n in range(kept):
            share, place = n // (kept // shares), n % (kept // shares)
            for part in range(2):
                row = (part * kept + n) * WIN_GROUP
                for c in range(0, channels, 128):
                    value = staged[c // 128, row:row + WIN_GROUP, :].astype(jnp.bfloat16)
                    outs[place // depth][share, place % depth * 2 + part, :, c:c + 128] = value
        for share in range(shares):
            outs[-1][share, 2 * depth] = q_ref[pl.ds(group, WIN_GROUP), :]


def whiten(spectra, quality, bins, shares):
    windows, channels = quality.shape
    kept = bins.shape[0]
    paired = spectra.reshape(windows, channels * 2, FB)
    group = WIN_GROUP // WIN_STEP
    depth = kept // shares // PIECES
    rows = [2 * depth + (place == PIECES - 1) for place in range(PIECES)]
    return pl.pallas_call(
        lambda *refs: whiten_kernel(*refs, channels=channels, kept=kept, shares=shares, pieces=PIECES),
        grid=(windows // WIN_STEP,),
        in_specs=[
            pl.BlockSpec(memory_space=pltpu.SMEM),
            pl.BlockSpec((WIN_STEP, channels * 2, FB), lambda i: (i, 0, 0)),
            pl.BlockSpec((windows, channels), lambda i: (0, 0)),
        ],
        out_specs=[pl.BlockSpec((shares, r, WIN_GROUP, channels), lambda i: (0, 0, i // group, 0)) for r in rows],
        out_shape=[jax.ShapeDtypeStruct((shares, r, windows, channels), jnp.bfloat16) for r in rows],
        scratch_shapes=[
            pltpu.VMEM((WIN_STEP, channels * 2, FB), jnp.float32),
            pltpu.VMEM((kept + 16, 2 * FB), jnp.bfloat16),
            pltpu.VMEM((2 * kept, 2 * FB), jnp.bfloat16),
            pltpu.VMEM((channels // 128, 2 * kept * WIN_GROUP, 128), jnp.float32),
            pltpu.VMEM((windows, channels), jnp.float32),
        ],
        compiler_params=pltpu.CompilerParams(vmem_limit_bytes=60 * MIB),
        cost_estimate=taking(11),
    )(bins, paired, quality)


def turn_kernel(own_ref, out_ref):
    channels = own_ref.shape[-1]
    depth = out_ref.shape[-1]
    own = own_ref[...]
    out_ref[:channels] = own.reshape(depth, channels).T
    turned = jnp.concatenate([own[:, 1:], -own[:, :1]], 1)
    out_ref[channels:] = turned.reshape(depth, channels).T


def turn(own):
    shares, rows, windows, channels = own.shape
    deep = rows // 2
    depth = shares * 2 * windows
    return pl.pallas_call(
        turn_kernel,
        grid=(deep,),
        in_specs=[pl.BlockSpec((shares, 2, windows, channels), lambda n: (0, n, 0, 0))],
        out_specs=pl.BlockSpec((None, 2 * channels, depth), lambda n: (n, 0, 0)),
        out_shape=jax.ShapeDtypeStruct((deep, 2 * channels, depth), jnp.bfloat16),
        compiler_params=pltpu.CompilerParams(vmem_limit_bytes=63 * MIB),
        cost_estimate=taking(1.5),
    )(own)


def weight_kernel(where_ref, own_ref, first_ref, second_ref, both_ref, out_ref):
    shares, _, windows, channels = own_ref.shape
    depth = shares * windows
    own = own_ref[...].reshape(depth, channels).T
    for r, other in enumerate([jnp.where(where_ref[0] == 0, first_ref[...], second_ref[...]), both_ref[...]]):
        counts = jnp.dot(own, other.reshape(depth, channels), preferred_element_type=jnp.float32)
        out_ref[r] = lax.rsqrt(jnp.maximum(counts, 1.0))


def weights(where, *marks):
    channels = marks[0].shape[-1]
    return pl.pallas_call(
        weight_kernel,
        grid=(1,),
        in_specs=[pl.BlockSpec(memory_space=pltpu.SMEM)]
        + [pl.BlockSpec(value.shape, lambda g: (0, 0, 0, 0)) for value in marks],
        out_specs=pl.BlockSpec((2, channels, channels), lambda g: (0, 0, 0)),
        out_shape=jax.ShapeDtypeStruct((2, channels, channels), jnp.float32),
        compiler_params=pltpu.CompilerParams(vmem_limit_bytes=16 * MIB),
        cost_estimate=taking(1),
    )(where, *marks)


def cross_kernel(where_ref, weight_ref, *refs, jobs, deep, rounds):
    out_ref = refs[-1]
    channels = out_ref.shape[-1]
    depth = refs[jobs[0][0]].shape[-1]
    job, n = pl.program_id(0) // deep, lax.rem(pl.program_id(0), deep)
    rows = channels // CHUNKS

    def products(left_ref, other_ref, r):
        other = other_ref[...].reshape(depth, channels)
        for part in range(2):
            for i in range(CHUNKS):
                left = left_ref[n, part * channels + i * rows:part * channels + (i + 1) * rows]
                product = jnp.dot(left, other, preferred_element_type=jnp.float32)
                weight = weight_ref[r, i * rows:(i + 1) * rows]
                out_ref[part, i * rows:(i + 1) * rows] = (product * weight).astype(jnp.bfloat16)

    for at, (left, _, r, sources) in enumerate(jobs):
        for place, (source, core, last) in enumerate(sources):
            wanted = job == at
            if core is not None:
                wanted = wanted & (where_ref[0] == core)
            if last is not None:
                wanted = wanted & (where_ref[1] == last)

            @pl.when(wanted)
            def _(left=left, source=source, r=r):
                products(refs[left], refs[source], r - rounds[0])


def cross(where, weight, jobs, kept, held):
    arrays, plan, first_job = [], [], []

    def put(value, job):
        for at, other in enumerate(arrays):
            if other is value:
                return at
        arrays.append(value)
        first_job.append(job)
        return len(arrays) - 1

    lefts = []
    for at, (left, place, r, choices) in enumerate(jobs):
        lefts.append(put(left, None))
    for at, (left, place, r, choices) in enumerate(jobs):
        plan.append((lefts[at], place, r, [(put(value, at), core, last) for value, core, last in choices]))
    deep, double, depth = jobs[0][0].shape
    channels = double // 2
    extra = [] if held is None else [held]
    used = sorted({r for _, _, r, _ in plan})
    rounds = (used[0] // 2 * 2, 2) if len(used) > 1 else (used[0], 1)

    def spec(value, job):
        if job is None:
            return pl.BlockSpec(value.shape, lambda g: (0, 0, 0), pipeline_mode=pl.Buffered(1))
        shares, _, windows, _ = value.shape
        return pl.BlockSpec(
            (shares, 2, windows, channels), lambda g: (0, jnp.clip(g - job * deep, 0, deep - 1), 0, 0)
        )

    def chosen(job, values):
        result = values[0]
        for at in range(1, len(values)):
            result = jnp.where(job == at, values[at], result)
        return result

    def target(g):
        job = g // deep
        place = chosen(job, [p[1] for p in plan]) + lax.rem(g, deep)
        return chosen(job, [p[2] for p in plan]), 0, place, 0, 0

    return pl.pallas_call(
        lambda *refs: cross_kernel(*refs, jobs=plan, deep=deep, rounds=rounds),
        grid=(len(plan) * deep,),
        in_specs=[pl.BlockSpec(memory_space=pltpu.SMEM)]
        + [
            pl.BlockSpec(
                (rounds[1], channels, channels), lambda g: (rounds[0] % 2 // rounds[1], 0, 0), pipeline_mode=pl.Buffered(1)
            )
        ]
        + [spec(value, job) for value, job in zip(arrays, first_job)]
        + [pl.BlockSpec(memory_space=pl.ANY)] * len(extra),
        out_specs=pl.BlockSpec((None, 2, None, channels, channels), target),
        out_shape=jax.ShapeDtypeStruct((ROUNDS, 2, kept, channels, channels), jnp.bfloat16),
        input_output_aliases={} if held is None else {2 + len(arrays): 0},
        compiler_params=pltpu.CompilerParams(vmem_limit_bytes=32 * MIB),
        cost_estimate=taking(1),
    )(where, weight, *arrays, *extra)


def tied(*values):
    return lax.optimization_barrier(values)


def gate_kernel(value_ref, *refs):
    del value_ref, refs


def gated(value, *others):
    anywhere = pl.BlockSpec(memory_space=pl.ANY)
    return pl.pallas_call(
        gate_kernel,
        in_specs=[anywhere] * (1 + len(others)),
        out_specs=anywhere,
        out_shape=jax.ShapeDtypeStruct(value.shape, value.dtype),
        input_output_aliases={0: 0},
        cost_estimate=taking(0.1),
    )(value, *others)


def shards(spectra, quality, bins):
    blocks = lax.axis_size("blk")
    shares = lax.axis_size("bin")
    chips = blocks // 2
    block = lax.axis_index("blk")
    where = jnp.stack([block % 2, (block // 2 % ROWS_Z == ROWS_Z - 1).astype(jnp.int32)])

    def moved(value, pairs):
        return lax.ppermute(value, "blk", [(2 * s + c, 2 * t + c) for s, t in pairs for c in range(2)])

    def back(value):
        return moved(value, [((t + 1) % chips, t) for t in range(chips)])

    def chip(row, z):
        return (row % (chips // ROWS_Z)) * ROWS_Z + z % ROWS_Z

    every = [(row, z) for row in range(chips // ROWS_Z) for z in range(ROWS_Z)]

    def forth(value):
        return moved(value, [(chip(row, z - 1), chip(row, z)) for row, z in every])

    def forth_last(value):
        return moved(value, [(chip(row + (z + 2) // ROWS_Z, z - 1), chip(row, z)) for row, z in every])

    def swapped(value):
        return lax.ppermute(value, "blk", [(i, i ^ 1) for i in range(blocks)])

    def back_inside(value):
        return moved(value, [(chip(row, z + 1), chip(row, z)) for row, z in every])

    def last_crossed(value):
        rows = chips // ROWS_Z
        return moved(value, [(chip(row + 1, -1), chip(row, -1)) for row in range(rows)])

    def far_back(value):
        return moved(value, [((t + 2) % chips, t) for t in range(chips)])

    def to_bins(value):
        return lax.all_to_all(value, "bin", split_axis=0, concat_axis=0, tiled=True)

    kept = bins.shape[0] // shares
    deep = kept // PIECES
    sent_a, sent_b = whiten(spectra, quality, bins, shares)
    own_a = to_bins(sent_a)
    sent_b, own_a = tied(sent_b, own_a)
    own_all = to_bins(sent_b)
    own_b, own_marks = own_all[:, :2 * deep], own_all[:, 2 * deep:]
    inside_a, forth_a, forth_marks = back_inside(own_a), forth(own_a), forth(own_marks)
    left_a = turn(own_a)
    own_b, inside_a, forth_a, forth_marks, left_a = tied(own_b, inside_a, forth_a, forth_marks, left_a)
    near_b, crossed_a, far_a = back(own_b), last_crossed(inside_a), forth_last(forth_a)
    near_marks, far_marks = back(own_marks), forth_last(forth_marks)
    left_b = turn(own_b)
    near_b, crossed_a, far_a, left_b = tied(near_b, crossed_a, far_a, left_b)
    far_b = back(near_b)
    near_marks_pair = swapped(near_marks)
    own_pair_a, own_pair_b, inside_pair_a = swapped(own_a), swapped(own_b), swapped(inside_a)
    own_marks_pair, far_marks_pair = swapped(own_marks), swapped(far_marks)
    crossed_pair_a, near_pair_b, far_pair_a = swapped(crossed_a), swapped(near_b), swapped(far_a)
    weight = weights(where, own_marks, own_marks_pair, near_marks_pair, near_marks)
    far_weight = weights(where, own_marks, near_marks_pair, far_marks_pair, far_marks)
    jobs = [
        (left_b, deep, 1, [(near_b, None, None)]),
        (left_b, deep, 0, [(own_pair_b, 0, None), (near_pair_b, 1, None)]),
        (left_a, 0, 1, [(inside_a, None, 0), (crossed_a, None, 1)]),
        (left_a, 0, 0, [(own_pair_a, 0, None), (inside_pair_a, 1, 0), (crossed_pair_a, 1, 1)]),
    ]
    out = cross(where, weight, jobs, kept, None)
    jobs = [
        (left_a, 0, 3, [(far_a, None, None)]),
        (left_a, 0, 2, [(inside_pair_a, 0, 0), (crossed_pair_a, 0, 1), (far_pair_a, 1, None)]),
    ]
    out = cross(where, far_weight, jobs, kept, out)
    far_b, out = tied(far_b, out)
    far_pair_b = swapped(far_b)
    out = cross(where, far_weight, [(left_b, deep, 3, [(far_b, None, None)])], kept, out)
    return cross(where, far_weight, [(left_b, deep, 2, [(near_pair_b, 0, None), (far_pair_b, 1, None)])], kept, out)


def solution(mesh):
    return jax.shard_map(
        shards,
        mesh=mesh,
        in_specs=(P("bin", "blk", None, None), P("bin", "blk"), P()),
        out_specs=P(None, None, "bin", "blk", None),
        check_vma=False,
    )
```

time: 190 us -> 140 us (0.74)
  waiting for transfers between devices: 65.9 us -> 38.5 us
  blocking collectives: 0 us -> 22.8 us
  starting transfers between devices: 49.2 us -> 28.2 us
  between operations: 13.7 us -> 0.1 us
  other arithmetic: 9.92 us -> 0.07 us
  local copies, waits for them, and re-layouts: 8.85 us -> 5.95 us
  Pallas kernels: 41.1 us -> 43.3 us
    all_to_all x0 -> x1, blocking collectives: none -> 22.8 us  [to_bins(): return lax.all_to_all(value, 'bin', split_axis=0, concat_axis=0, tiled=True)]
    all_to_all x4 -> x1, starting transfers between devices: 22.2 us -> 4.26 us  [to_bins(): return lax.all_to_all(value, 'bin', split_axis=0, concat_axis=0, tiled=True)]
    all_to_all x4 -> x1, waiting for transfers between devices: 29.3 us -> 13.3 us  [to_bins(): return lax.all_to_all(value, 'bin', split_axis=0, concat_axis=0, tiled=True)]
    ppermute x10 -> x9, waiting for transfers between devices: 36.5 us -> 25.1 us  [moved(): lax.ppermute(value, 'blk', [(2 * s + c, 2 * t + c) for s, t in pairs for...]
    select_n x4 -> x0, other arithmetic: 9.09 us -> none  [shards(): first = swapped(jnp.where(core == 1, own[place], near[place]))]
    ppermute x4 -> x0, starting transfers between devices: 8.47 us -> none  [shifted(): lax.ppermute(value, 'blk', [((i + steps) % blocks, i) for i in range(bloc...]
    ppermute x8 -> x10, starting transfers between devices: 4.3 us -> 10.5 us  [swapped(): return lax.ppermute(value, 'blk', [(i, i ^ 1) for i in range(blocks)])]
    unnamed x40 -> x12, local copies, waits for them, and re-layouts: 7.33 us -> 2.67 us
  transfers between devices with their start and end apart: 27 -> 20, of which waited for: 9 -> 4; matrix products, arithmetic and copies ran while one was open for 6% -> 2% of each run, Pallas kernels for 15% -> 21%
where the time goes in v2:
time: 140 us; the launch traced here: 139 us
  Pallas kernels  43.3 us (31%)
  waiting for transfers between devices  38.5 us (28%)
  starting transfers between devices  28.2 us (20%)
  blocking collectives  22.8 us (16%)
  local copies, waits for them, and re-layouts  5.95 us (4%)
    ppermute x9, waiting for transfers between devices, moved(): lax.ppermute(value, 'blk', [(2 * s + c, 2 * t + c) for s, t in pairs for...  25.1 us
    pallas_call x4, Pallas kernels, cross(): pl.pallas_call(lambda *refs: cross_kernel(*refs, jobs=plan, deep=deep, ro...  24 us
    all_to_all x1, blocking collectives, to_bins(): return lax.all_to_all(value, 'bin', split_axis=0, concat_axis=0, tiled=True)  22.8 us
    ppermute x9, starting transfers between devices, moved(): lax.ppermute(value, 'blk', [(2 * s + c, 2 * t + c) for s, t in pairs for...  13.5 us
    all_to_all x1, waiting for transfers between devices, to_bins(): return lax.all_to_all(value, 'bin', split_axis=0, concat_axis=0, tiled=True)  13.3 us
    pallas_call x1, Pallas kernels, whiten(): pl.pallas_call(lambda *refs: whiten_kernel(*refs, channels=channels, kept...  10.6 us
    ppermute x10, starting transfers between devices, swapped(): return lax.ppermute(value, 'blk', [(i, i ^ 1) for i in range(blocks)])  10.5 us
    pallas_call x2, Pallas kernels, turn(): pl.pallas_call(turn_kernel, grid=(deep,), in_specs=[pl.BlockSpec((shares,...  5.38 us
  transfers between devices with their start and end apart: 20, of which 4 were waited for; matrix products, arithmetic and copies ran while one was open for 2% of the time, Pallas kernels for 21%

profile of v2, /device:TPU:1, one launch (start us, length us, event | category | flops | bytes accessed | tf_op | source)
XLA Modules:
  0.0 138.9 jit_solution(3819987353914136253)
XLA Ops:
  0.0 10.6 %shard_map.37 = (bf16[8,4,32,512]{3,2,1,0:T(8,128)(2,1)}, bf16[8,5,32,512]{3,2,1,0:T(8,128)(2,1)}) custom-call(s32[32]{0:T(128)} %refs_0_.1, bf16[32,1024,128]{2,1,0:T(8,128)(2,1)} %bitcast.3, bf16[32,512]{1,0:T(8,128)(2,1)} %refs_2_.1), custom_call_target="tpu_custom_call" | custom-call | flops 11000 | bytes 1000 | tf_op jit(solution)/shard_map/pallas_call | solution.py:89
  10.6 22.8 %all_to_all.10.own_ref = bf16[8,4,32,512]{3,2,1,0:T(8,128)(2,1)} all-to-all(bf16[8,4,32,512]{3,2,1,0:T(8,128)(2,1)} %get-tuple-element.21), channel_id=1, replica_groups=mesh['blk'=16,'bin'=8] {'bin'}, dimensions={0} | all-to-all | bytes 2097152 | tf_op jit(solution)/shard_map/all_to_all | solution.py:305
  33.5 4.3 %all-to-all-start.1 = ((bf16[8,5,32,512]{3,2,1,0:T(8,128)(2,1)}), bf16[8,5,32,512]{3,2,1,0:T(8,128)(2,1)}, u32[]{:S(2)}, u32[]{:S(2)}) async-start(bf16[8,5,32,512]{3,2,1,0:T(8,128)(2,1)} %get-tuple-element.22), calls=%async_computation.1 | async-start | bytes 2621440 | tf_op jit(solution)/shard_map/all_to_all | solution.py:305
  37.7 1.7 %collective-permute-start.3 = (bf16[8,4,32,512]{3,2,1,0:T(8,128)(2,1)}, bf16[8,4,32,512]{3,2,1,0:T(8,128)(2,1)}, u32[]{:S(2)}, u32[]{:S(2)}) collective-permute-start(bf16[8,4,32,512]{3,2,1,0:T(8,128)(2,1)} %all_to_all.10.own_ref), channel_id=1, source_target_pairs={{48,0},{56,8},{0,16},{8,24},{16,32},{24,40},{32,48},{40,56},{112,6... | collective-permute-start | bytes 3145736 | tf_op jit(solution)/shard_map/ppermute | solution.py:275
  39.4 2.2 %collective-permute-start.2 = (bf16[8,4,32,512]{3,2,1,0:T(8,128)(2,1)}, bf16[8,4,32,512]{3,2,1,0:T(8,128)(2,1)}, u32[]{:S(2)}, u32[]{:S(2)}) collective-permute-start(bf16[8,4,32,512]{3,2,1,0:T(8,128)(2,1)} %all_to_all.10.own_ref), channel_id=1, source_target_pairs={{16,0},{24,8},{32,16},{40,24},{48,32},{56,40},{0,48},{8,56},{80,64... | collective-permute-start | bytes 3145736 | tf_op jit(solution)/shard_map/ppermute | solution.py:275
  41.6 13.3 %all-to-all-done.1 = bf16[8,5,32,512]{3,2,1,0:T(8,128)(2,1)} async-done(((bf16[8,5,32,512]{3,2,1,0:T(8,128)(2,1)}), bf16[8,5,32,512]{3,2,1,0:T(8,128)(2,1)}, u32[]{:S(2)}, u32[]{:S(2)}) %all-to-all-start.1) | async-done | bytes 1310752 | tf_op jit(solution)/shard_map/all_to_all | solution.py:305
  55.9 1.7 %collective-permute-start.4 = (bf16[8,1,32,512]{3,2,1,0:T(8,128)(2,1)S(1)}, bf16[8,1,32,512]{3,2,1,0:T(8,128)(2,1)S(1)}, u32[]{:S(2)}, u32[]{:S(2)}) collective-permute-start(bf16[8,1,32,512]{3,2,1,0:T(8,128)(2,1)S(1)} %slice.8.own_ref), channel_id=1, source_target_pairs={{48,0},{56,8},{0,16},{8,24},{16,32},{24,40},{32,48},{40,56},{112,6... | collective-permute-start | bytes 786440 | tf_op jit(solution)/shard_map/ppermute | solution.py:275
  57.6 2.7 %shard_map.38.refs_3_.refs_2_ = bf16[2,1024,512]{2,1,0:T(8,128)(2,1)} custom-call(bf16[8,4,32,512]{3,2,1,0:T(8,128)(2,1)} %all_to_all.10.own_ref), custom_call_target="tpu_custom_call" | custom-call | flops 1500 | bytes 1000 | tf_op jit(solution)/shard_map/pallas_call | solution.py:124
  60.3 2.3 %collective-permute-start = (bf16[8,1,32,512]{3,2,1,0:T(8,128)(2,1)S(1)}, bf16[8,1,32,512]{3,2,1,0:T(8,128)(2,1)S(1)}, u32[]{:S(2)}, u32[]{:S(2)}) collective-permute-start(bf16[8,1,32,512]{3,2,1,0:T(8,128)(2,1)S(1)} %slice.8.own_ref), channel_id=1, source_target_pairs={{16,0},{24,8},{32,16},{40,24},{48,32},{56,40},{64,48},{72,56},{80,... | collective-permute-start | bytes 786440 | tf_op jit(solution)/shard_map/ppermute | solution.py:275
  62.6 2.3 %slice.9.own_ref = bf16[8,4,32,512]{3,2,1,0:T(8,128)(2,1)} slice(bf16[8,5,32,512]{3,2,1,0:T(8,128)(2,1)} %all-to-all-done.1), slice={[0:8], [0:4], [0:32], [0:512]} | slice | bytes 2097152 | tf_op jit(solution)/shard_map/slice | solution.py:313
  64.9 3.5 %collective-permute-done.4 = bf16[8,1,32,512]{3,2,1,0:T(8,128)(2,1)S(1)} collective-permute-done((bf16[8,1,32,512]{3,2,1,0:T(8,128)(2,1)S(1)}, bf16[8,1,32,512]{3,2,1,0:T(8,128)(2,1)S(1)}, u32[]{:S(2)}, u32[]{:S(2)}) %collective-permute-start.4) | collective-permute-done | bytes 262176 | tf_op jit(solution)/shard_map/ppermute | solution.py:275
  68.4 2.8 %collective-permute-start.7 = (bf16[8,4,32,512]{3,2,1,0:T(8,128)(2,1)}, bf16[8,4,32,512]{3,2,1,0:T(8,128)(2,1)}, u32[]{:S(2)}, u32[]{:S(2)}) collective-permute-start(bf16[8,4,32,512]{3,2,1,0:T(8,128)(2,1)} %slice.9.own_ref), channel_id=1, source_target_pairs={{16,0},{24,8},{32,16},{40,24},{48,32},{56,40},{64,48},{72,56},{80,... | collective-permute-start | bytes 3145736 | tf_op jit(solution)/shard_map/ppermute | solution.py:275
  71.2 1.6 %collective-permute-start.8 = (bf16[8,4,32,512]{3,2,1,0:T(8,128)(2,1)}, bf16[8,4,32,512]{3,2,1,0:T(8,128)(2,1)}, u32[]{:S(2)}, u32[]{:S(2)}) collective-permute-start(bf16[8,4,32,512]{3,2,1,0:T(8,128)(2,1)} %collective-permute-done.2.refs_7_), channel_id=1, source_target_pairs={{112,48},{120,56},{48,112},{56,120},{113,49},{121,57},{49,113},{57... | collective-permute-start | bytes 3145736 | tf_op jit(solution)/shard_map/ppermute | solution.py:275
  72.8 3.7 %collective-permute-start.17 = (bf16[8,4,32,512]{3,2,1,0:T(8,128)(2,1)}, bf16[8,4,32,512]{3,2,1,0:T(8,128)(2,1)}, u32[]{:S(2)}, u32[]{:S(2)}) collective-permute-start(bf16[8,4,32,512]{3,2,1,0:T(8,128)(2,1)} %all_to_all.10.own_ref), channel_id=1, source_target_pairs={{0,8},{8,0},{16,24},{24,16},{32,40},{40,32},{48,56},{56,48},{64,72... | collective-permute-start | bytes 3145736 | tf_op jit(solution)/shard_map/ppermute | solution.py:292
  76.6 20.5 %collective-permute-done.5.both_ref = bf16[8,1,32,512]{3,2,1,0:T(8,128)(2,1)} collective-permute-done((bf16[8,1,32,512]{3,2,1,0:T(8,128)(2,1)S(1)}, bf16[8,1,32,512]{3,2,1,0:T(8,128)(2,1)}, u32[]{:S(2)}, u32[]{:S(2)}) %collective-permute-start.5) | collective-permute-done | bytes 262176 | tf_op jit(solution)/shard_map/ppermute | solution.py:275
  97.1 4.0 %collective-permute-start.16 = (bf16[8,4,32,512]{3,2,1,0:T(8,128)(2,1)}, bf16[8,4,32,512]{3,2,1,0:T(8,128)(2,1)}, u32[]{:S(2)}, u32[]{:S(2)}) collective-permute-start(bf16[8,4,32,512]{3,2,1,0:T(8,128)(2,1)} %slice.9.own_ref), channel_id=1, source_target_pairs={{0,8},{8,0},{16,24},{24,16},{32,40},{40,32},{48,56},{56,48},{64,72... | collective-permute-start | bytes 3145736 | tf_op jit(solution)/shard_map/ppermute | solution.py:292
  101.7 2.7 %shard_map.40.refs_2_ = bf16[2,1024,512]{2,1,0:T(8,128)(2,1)} custom-call(bf16[8,4,32,512]{3,2,1,0:T(8,128)(2,1)} %slice.9.own_ref), custom_call_target="tpu_custom_call" | custom-call | flops 1500 | bytes 1000 | tf_op jit(solution)/shard_map/pallas_call | solution.py:124
  106.2 1.2 collective-permute-start.11
  109.3 1.6 %shard_map.41.refs_1_ = f32[2,512,512]{2,1,0:T(8,128)S(1)} custom-call(s32[2]{0:T(128)S(1)} %pad_add_fusion.where_ref.refs_0_, bf16[8,1,32,512]{3,2,1,0:T(8,128)(2,1)S(1)} %slice.8.own_ref, bf16[8,1,32,512]{3,2,1,0:T(8,128)(2,1)} %collective-permute-done.15.first_ref, bf16[8,1,32,512]{3,2,1,0:T(8,128)(2,1)S(1)} %copy-done.3, ...), custom_call_target="tpu_custom_call" | custom-call | flops 1000 | bytes 1000 | tf_op jit(solution)/shard_map/pallas_call | solution.py:146
  110.9 1.7 %shard_map.39.refs_1_ = f32[2,512,512]{2,1,0:T(8,128)S(1)} custom-call(s32[2]{0:T(128)S(1)} %pad_add_fusion.where_ref.refs_0_, bf16[8,1,32,512]{3,2,1,0:T(8,128)(2,1)S(1)} %slice.8.own_ref, bf16[8,1,32,512]{3,2,1,0:T(8,128)(2,1)S(1)} %copy-done.3, bf16[8,1,32,512]{3,2,1,0:T(8,128)(2,1)} %collective-permute-done.6.second_ref, ...), custom_call_target="tpu_custom_call" | custom-call | flops 1000 | bytes 1000 | tf_op jit(solution)/shard_map/pallas_call | solution.py:146
  112.7 11.3 %shard_map.42.refs_7_ = bf16[4,2,4,512,512]{4,3,2,1,0:T(8,128)(2,1)} custom-call(s32[2]{0:T(128)S(1)} %pad_add_fusion.where_ref.refs_0_, f32[2,512,512]{2,1,0:T(8,128)S(1)} %shard_map.41.refs_1_, bf16[2,1024,512]{2,1,0:T(8,128)(2,1)S(1)} %copy-done, bf16[2,1024,512]{2,1,0:T(8,128)(2,1)S(1)} %copy-done.1, ...), custom_call_target="tpu_custom_call" | custom-call | flops 1000 | bytes 1000 | tf_op jit(solution)/shard_map/pallas_call | solution.py:228
  124.0 6.0 %shard_map.43.refs_4_ = bf16[4,2,4,512,512]{4,3,2,1,0:T(8,128)(2,1)} custom-call(s32[2]{0:T(128)S(1)} %pad_add_fusion.where_ref.refs_0_, f32[2,512,512]{2,1,0:T(8,128)S(1)} %shard_map.39.refs_1_, bf16[2,1024,512]{2,1,0:T(8,128)(2,1)S(1)} %copy-done.1, bf16[8,4,32,512]{3,2,1,0:T(8,128)(2,1)} %collective-permute-done.9.refs_3_, ...), custom_call_target="tpu_custom_call", output_to_operand_aliasing={{}: (7, {})} | custom-call | flops 1000 | bytes 1000 | tf_op jit(solution)/shard_map/pallas_call | solution.py:228
  132.2 3.5 %shard_map.44.refs_5_ = bf16[4,2,4,512,512]{4,3,2,1,0:T(8,128)(2,1)} custom-call(s32[2]{0:T(128)S(1)} %pad_add_fusion.where_ref.refs_0_, f32[2,512,512]{2,1,0:T(8,128)S(1)} %shard_map.39.refs_1_, bf16[2,1024,512]{2,1,0:T(8,128)(2,1)S(1)} %copy-done, bf16[8,4,32,512]{3,2,1,0:T(8,128)(2,1)} %collective-permute-done.11.refs_3_, ...), custom_call_target="tpu_custom_call", output_to_operand_aliasing={{}: (4, {})} | custom-call | flops 1000 | bytes 1000 | tf_op jit(solution)/shard_map/pallas_call | solution.py:228
  135.8 3.1 %shard_map.45 = bf16[4,2,4,512,512]{4,3,2,1,0:T(8,128)(2,1)} custom-call(s32[2]{0:T(128)S(1)} %pad_add_fusion.where_ref.refs_0_, f32[2,512,512]{2,1,0:T(8,128)S(1)} %shard_map.39.refs_1_, bf16[2,1024,512]{2,1,0:T(8,128)(2,1)S(1)} %copy-done, bf16[8,4,32,512]{3,2,1,0:T(8,128)(2,1)S(1)} %collective-permute-done.10.refs_6_.refs_3_, ...), custom_call_target="tpu_custom_call", output_to_operand_aliasing={{}: (5, {})} | custom-call | flops 1000 | bytes 1000 | tf_op jit(solution)/shard_map/pallas_call | solution.py:228
  (41 shorter events, 7.5 us)
Async XLA Ops:
  33.5 21.5 %all-to-all-start.1 = ((bf16[8,5,32,512]{3,2,1,0:T(8,128)(2,1)}), bf16[8,5,32,512]{3,2,1,0:T(8,128)(2,1)}, u32[]{:S(2)}, u32[]{:S(2)}) async-start(bf16[8,5,32,512]{3,2,1,0:T(8,128)(2,1)} %get-tuple-element.22), calls=%async_computation.1 | async-start | bytes 2621440 | tf_op jit(solution)/shard_map/all_to_all | solution.py:305
  37.7 27.2 %collective-permute-start.3 = (bf16[8,4,32,512]{3,2,1,0:T(8,128)(2,1)}, bf16[8,4,32,512]{3,2,1,0:T(8,128)(2,1)}, u32[]{:S(2)}, u32[]{:S(2)}) collective-permute-start(bf16[8,4,32,512]{3,2,1,0:T(8,128)(2,1)} %all_to_all.10.own_ref), channel_id=1, source_target_pairs={{48,0},{56,8},{0,16},{8,24},{16,32},{24,40},{32,48},{40,56},{112,6... | collective-permute-start | bytes 3145736 | tf_op jit(solution)/shard_map/ppermute | solution.py:275
  39.4 25.5 %collective-permute-start.2 = (bf16[8,4,32,512]{3,2,1,0:T(8,128)(2,1)}, bf16[8,4,32,512]{3,2,1,0:T(8,128)(2,1)}, u32[]{:S(2)}, u32[]{:S(2)}) collective-permute-start(bf16[8,4,32,512]{3,2,1,0:T(8,128)(2,1)} %all_to_all.10.own_ref), channel_id=1, source_target_pairs={{16,0},{24,8},{32,16},{40,24},{48,32},{56,40},{0,48},{8,56},{80,64... | collective-permute-start | bytes 3145736 | tf_op jit(solution)/shard_map/ppermute | solution.py:275
  55.9 12.5 %collective-permute-start.4 = (bf16[8,1,32,512]{3,2,1,0:T(8,128)(2,1)S(1)}, bf16[8,1,32,512]{3,2,1,0:T(8,128)(2,1)S(1)}, u32[]{:S(2)}, u32[]{:S(2)}) collective-permute-start(bf16[8,1,32,512]{3,2,1,0:T(8,128)(2,1)S(1)} %slice.8.own_ref), channel_id=1, source_target_pairs={{48,0},{56,8},{0,16},{8,24},{16,32},{24,40},{32,48},{40,56},{112,6... | collective-permute-start | bytes 786440 | tf_op jit(solution)/shard_map/ppermute | solution.py:275
  60.3 12.5 %collective-permute-start = (bf16[8,1,32,512]{3,2,1,0:T(8,128)(2,1)S(1)}, bf16[8,1,32,512]{3,2,1,0:T(8,128)(2,1)S(1)}, u32[]{:S(2)}, u32[]{:S(2)}) collective-permute-start(bf16[8,1,32,512]{3,2,1,0:T(8,128)(2,1)S(1)} %slice.8.own_ref), channel_id=1, source_target_pairs={{16,0},{24,8},{32,16},{40,24},{48,32},{56,40},{64,48},{72,56},{80,... | collective-permute-start | bytes 786440 | tf_op jit(solution)/shard_map/ppermute | solution.py:275
  68.4 32.7 %collective-permute-start.9 = (bf16[8,4,32,512]{3,2,1,0:T(8,128)(2,1)}, bf16[8,4,32,512]{3,2,1,0:T(8,128)(2,1)}, u32[]{:S(2)}, u32[]{:S(2)}) collective-permute-start(bf16[8,4,32,512]{3,2,1,0:T(8,128)(2,1)} %collective-permute-done.3), channel_id=1, source_target_pairs={{48,0},{56,8},{0,16},{8,24},{80,32},{88,40},{96,48},{104,56},{112,... | collective-permute-start | bytes 3145736 | tf_op jit(solution)/shard_map/ppermute | solution.py:275
  68.4 32.7 %collective-permute-start.7 = (bf16[8,4,32,512]{3,2,1,0:T(8,128)(2,1)}, bf16[8,4,32,512]{3,2,1,0:T(8,128)(2,1)}, u32[]{:S(2)}, u32[]{:S(2)}) collective-permute-start(bf16[8,4,32,512]{3,2,1,0:T(8,128)(2,1)} %slice.9.own_ref), channel_id=1, source_target_pairs={{16,0},{24,8},{32,16},{40,24},{48,32},{56,40},{64,48},{72,56},{80,... | collective-permute-start | bytes 3145736 | tf_op jit(solution)/shard_map/ppermute | solution.py:275
  71.2 30.4 %collective-permute-start.8 = (bf16[8,4,32,512]{3,2,1,0:T(8,128)(2,1)}, bf16[8,4,32,512]{3,2,1,0:T(8,128)(2,1)}, u32[]{:S(2)}, u32[]{:S(2)}) collective-permute-start(bf16[8,4,32,512]{3,2,1,0:T(8,128)(2,1)} %collective-permute-done.2.refs_7_), channel_id=1, source_target_pairs={{112,48},{120,56},{48,112},{56,120},{113,49},{121,57},{49,113},{57... | collective-permute-start | bytes 3145736 | tf_op jit(solution)/shard_map/ppermute | solution.py:275
  72.8 24.3 %collective-permute-start.5 = (bf16[8,1,32,512]{3,2,1,0:T(8,128)(2,1)S(1)}, bf16[8,1,32,512]{3,2,1,0:T(8,128)(2,1)}, u32[]{:S(2)}, u32[]{:S(2)}) collective-permute-start(bf16[8,1,32,512]{3,2,1,0:T(8,128)(2,1)S(1)} %collective-permute-done.4), channel_id=1, source_target_pairs={{48,0},{56,8},{0,16},{8,24},{80,32},{88,40},{96,48},{104,56},{112,... | collective-permute-start | bytes 786440 | tf_op jit(solution)/shard_map/ppermute | solution.py:275
  72.8 32.1 %copy-start.4 = (bf16[8,1,32,512]{3,2,1,0:T(8,128)(2,1)}, bf16[8,1,32,512]{3,2,1,0:T(8,128)(2,1)S(1)}, u32[]{:S(2)}) copy-start(bf16[8,1,32,512]{3,2,1,0:T(8,128)(2,1)S(1)} %collective-permute-done.both_ref) | copy-start | bytes 786436
  72.8 31.6 %collective-permute-start.17 = (bf16[8,4,32,512]{3,2,1,0:T(8,128)(2,1)}, bf16[8,4,32,512]{3,2,1,0:T(8,128)(2,1)}, u32[]{:S(2)}, u32[]{:S(2)}) collective-permute-start(bf16[8,4,32,512]{3,2,1,0:T(8,128)(2,1)} %all_to_all.10.own_ref), channel_id=1, source_target_pairs={{0,8},{8,0},{16,24},{24,16},{32,40},{40,32},{48,56},{56,48},{64,72... | collective-permute-start | bytes 3145736 | tf_op jit(solution)/shard_map/ppermute | solution.py:292
  97.1 9.1 %collective-permute-start.16 = (bf16[8,4,32,512]{3,2,1,0:T(8,128)(2,1)}, bf16[8,4,32,512]{3,2,1,0:T(8,128)(2,1)}, u32[]{:S(2)}, u32[]{:S(2)}) collective-permute-start(bf16[8,4,32,512]{3,2,1,0:T(8,128)(2,1)} %slice.9.own_ref), channel_id=1, source_target_pairs={{0,8},{8,0},{16,24},{24,16},{32,40},{40,32},{48,56},{56,48},{64,72... | collective-permute-start | bytes 3145736 | tf_op jit(solution)/shard_map/ppermute | solution.py:292
  101.1 3.7 %collective-permute-start.15 = (bf16[8,1,32,512]{3,2,1,0:T(8,128)(2,1)S(1)}, bf16[8,1,32,512]{3,2,1,0:T(8,128)(2,1)}, u32[]{:S(2)}, u32[]{:S(2)}) collective-permute-start(bf16[8,1,32,512]{3,2,1,0:T(8,128)(2,1)S(1)} %slice.8.own_ref), channel_id=1, source_target_pairs={{0,8},{8,0},{16,24},{24,16},{32,40},{40,32},{48,56},{56,48},{64,72... | collective-permute-start | bytes 786440 | tf_op jit(solution)/shard_map/ppermute | solution.py:292
  101.1 3.8 %collective-permute-start.1 = (bf16[8,1,32,512]{3,2,1,0:T(8,128)(2,1)S(1)}, bf16[8,1,32,512]{3,2,1,0:T(8,128)(2,1)S(1)}, u32[]{:S(2)}, u32[]{:S(2)}) collective-permute-start(bf16[8,1,32,512]{3,2,1,0:T(8,128)(2,1)S(1)} %collective-permute-done.both_ref), channel_id=1, source_target_pairs={{0,8},{8,0},{16,24},{24,16},{32,40},{40,32},{48,56},{56,48},{64,72... | collective-permute-start | bytes 786440 | tf_op jit(solution)/shard_map/ppermute | solution.py:292
  101.6 4.4 %collective-permute-start.6 = (bf16[8,1,32,512]{3,2,1,0:T(8,128)(2,1)}, bf16[8,1,32,512]{3,2,1,0:T(8,128)(2,1)}, u32[]{:S(2)}, u32[]{:S(2)}) collective-permute-start(bf16[8,1,32,512]{3,2,1,0:T(8,128)(2,1)} %collective-permute-done.5.both_ref), channel_id=1, source_target_pairs={{0,8},{8,0},{16,24},{24,16},{32,40},{40,32},{48,56},{56,48},{64,72... | collective-permute-start | bytes 786440 | tf_op jit(solution)/shard_map/ppermute | solution.py:292
  104.4 8.2 %collective-permute-start.12 = (bf16[8,4,32,512]{3,2,1,0:T(8,128)(2,1)}, bf16[8,4,32,512]{3,2,1,0:T(8,128)(2,1)S(1)}, u32[]{:S(2)}, u32[]{:S(2)}) collective-permute-start(bf16[8,4,32,512]{3,2,1,0:T(8,128)(2,1)} %collective-permute-done.2.refs_7_), channel_id=1, source_target_pairs={{0,8},{8,0},{16,24},{24,16},{32,40},{40,32},{48,56},{56,48},{64,72... | collective-permute-start | bytes 3145736 | tf_op jit(solution)/shard_map/ppermute | solution.py:292
  104.8 7.8 %collective-permute-start.13 = (bf16[8,4,32,512]{3,2,1,0:T(8,128)(2,1)}, bf16[8,4,32,512]{3,2,1,0:T(8,128)(2,1)S(1)}, u32[]{:S(2)}, u32[]{:S(2)}) collective-permute-start(bf16[8,4,32,512]{3,2,1,0:T(8,128)(2,1)} %collective-permute-done.8.refs_8_), channel_id=1, source_target_pairs={{0,8},{8,0},{16,24},{24,16},{32,40},{40,32},{48,56},{56,48},{64,72... | collective-permute-start | bytes 3145736 | tf_op jit(solution)/shard_map/ppermute | solution.py:292
  105.6 7.0 %collective-permute-start.10 = (bf16[8,4,32,512]{3,2,1,0:T(8,128)(2,1)}, bf16[8,4,32,512]{3,2,1,0:T(8,128)(2,1)S(1)}, u32[]{:S(2)}, u32[]{:S(2)}) collective-permute-start(bf16[8,4,32,512]{3,2,1,0:T(8,128)(2,1)} %collective-permute-done.7.refs_4_), channel_id=1, source_target_pairs={{0,8},{8,0},{16,24},{24,16},{32,40},{40,32},{48,56},{56,48},{64,72... | collective-permute-start | bytes 3145736 | tf_op jit(solution)/shard_map/ppermute | solution.py:292
  106.1 17.9 %collective-permute-start.14 = (bf16[8,4,32,512]{3,2,1,0:T(8,128)(2,1)}, bf16[8,4,32,512]{3,2,1,0:T(8,128)(2,1)}, u32[]{:S(2)}, u32[]{:S(2)}) collective-permute-start(bf16[8,4,32,512]{3,2,1,0:T(8,128)(2,1)} %collective-permute-done.9.refs_3_), channel_id=1, source_target_pairs={{0,8},{8,0},{16,24},{24,16},{32,40},{40,32},{48,56},{56,48},{64,72... | collective-permute-start | bytes 3145736 | tf_op jit(solution)/shard_map/ppermute | solution.py:292
  106.2 25.0 %collective-permute-start.11 = (bf16[8,4,32,512]{3,2,1,0:T(8,128)(2,1)}, bf16[8,4,32,512]{3,2,1,0:T(8,128)(2,1)}, u32[]{:S(2)}, u32[]{:S(2)}) collective-permute-start(bf16[8,4,32,512]{3,2,1,0:T(8,128)(2,1)} %collective-permute-done.7.refs_4_), channel_id=1, source_target_pairs={{16,0},{24,8},{32,16},{40,24},{48,32},{56,40},{64,48},{72,56},{80,... | collective-permute-start | bytes 3145736 | tf_op jit(solution)/shard_map/ppermute | solution.py:275
  107.4 0.9 copy-start.3
  109.3 3.3 %copy-start.1 = (bf16[2,1024,512]{2,1,0:T(8,128)(2,1)S(1)}, bf16[2,1024,512]{2,1,0:T(8,128)(2,1)}, u32[]{:S(2)}) copy-start(bf16[2,1024,512]{2,1,0:T(8,128)(2,1)} %shard_map.38.refs_3_.refs_2_) | copy-start | bytes 6291460
  110.9 1.8 %copy-start = (bf16[2,1024,512]{2,1,0:T(8,128)(2,1)S(1)}, bf16[2,1024,512]{2,1,0:T(8,128)(2,1)}, u32[]{:S(2)}) copy-start(bf16[2,1024,512]{2,1,0:T(8,128)(2,1)} %shard_map.40.refs_2_) | copy-start | bytes 6291460
  131.2 4.6 %collective-permute-start.18 = (bf16[8,4,32,512]{3,2,1,0:T(8,128)(2,1)}, bf16[8,4,32,512]{3,2,1,0:T(8,128)(2,1)S(1)}, u32[]{:S(2)}, u32[]{:S(2)}) collective-permute-start(bf16[8,4,32,512]{3,2,1,0:T(8,128)(2,1)} %collective-permute-done.11.refs_3_), channel_id=1, source_target_pairs={{0,8},{8,0},{16,24},{24,16},{32,40},{40,32},{48,56},{56,48},{64,72... | collective-permute-start | bytes 3145736 | tf_op jit(solution)/shard_map/ppermute | solution.py:292
  (2 other events, 1.7 us)

commit v3 on v2

--- a/solution.py
+++ b/solution.py
@@ -244,6 +244,23 @@
     )(where, weight, *arrays, *extra)
 
 
+def copied_kernel(value_ref, out_ref):
+    for at in range(value_ref.shape[0]):
+        out_ref[at] = value_ref[at]
+
+
+def copied(value):
+    scalars = pl.BlockSpec(memory_space=pltpu.SMEM)
+    return pl.pallas_call(
+        copied_kernel,
+        in_specs=[scalars],
+        out_specs=scalars,
+        out_shape=jax.ShapeDtypeStruct(value.shape, value.dtype),
+        compiler_params=pltpu.CompilerParams(vmem_limit_bytes=63 * MIB),
+        cost_estimate=taking(0.1),
+    )(value)
+
+
 def tied(*values):
     return lax.optimization_barrier(values)
 
@@ -315,9 +332,10 @@
     left_a = turn(own_a)
     own_b, inside_a, forth_a, forth_marks, left_a = tied(own_b, inside_a, forth_a, forth_marks, left_a)
     near_b, crossed_a, far_a = back(own_b), last_crossed(inside_a), forth_last(forth_a)
+    left_b = turn(own_b)
+    forth_marks, left_b = tied(forth_marks, left_b)
     near_marks, far_marks = back(own_marks), forth_last(forth_marks)
-    left_b = turn(own_b)
-    near_b, crossed_a, far_a, left_b = tied(near_b, crossed_a, far_a, left_b)
+    near_b, crossed_a, far_a, where = tied(near_b, crossed_a, far_a, copied(where))
     far_b = back(near_b)
     near_marks_pair = swapped(near_marks)
     own_pair_a, own_pair_b, inside_pair_a = swapped(own_a), swapped(own_b), swapped(inside_a)

time: 140 us -> 137 us (0.979)
  local copies, waits for them, and re-layouts: 5.95 us -> 4.11 us
  transfers between devices with their start and end apart: 20 -> 20, of which waited for: 4 -> 5; matrix products, arithmetic and copies ran while one was open for 2% -> 2% of each run, Pallas kernels for 21% -> 22%
where the time goes in v3:
time: 137 us
  Pallas kernels  43.3 us (32%)
  waiting for transfers between devices  38.1 us (28%)
  starting transfers between devices  27.5 us (20%)
  blocking collectives  22.8 us (17%)
  local copies, waits for them, and re-layouts  4.11 us (3%)
    ppermute x9, waiting for transfers between devices, moved(): lax.ppermute(value, 'blk', [(2 * s + c, 2 * t + c) for s, t in pairs for...  24.3 us
    pallas_call x4, Pallas kernels, cross(): pl.pallas_call(lambda *refs: cross_kernel(*refs, jobs=plan, deep=deep, ro...  22.8 us
    all_to_all x1, blocking collectives, to_bins(): return lax.all_to_all(value, 'bin', split_axis=0, concat_axis=0, tiled=True)  22.8 us
    ppermute x9, starting transfers between devices, moved(): lax.ppermute(value, 'blk', [(2 * s + c, 2 * t + c) for s, t in pairs for...  13.3 us
    all_to_all x1, waiting for transfers between devices, to_bins(): return lax.all_to_all(value, 'bin', split_axis=0, concat_axis=0, tiled=True)  13.3 us
    pallas_call x1, Pallas kernels, whiten(): pl.pallas_call(lambda *refs: whiten_kernel(*refs, channels=channels, kept...  10.6 us
    ppermute x10, starting transfers between devices, swapped(): return lax.ppermute(value, 'blk', [(i, i ^ 1) for i in range(blocks)])  10.6 us
    pallas_call x2, Pallas kernels, turn(): pl.pallas_call(turn_kernel, grid=(deep,), in_specs=[pl.BlockSpec((shares,...  5.41 us
  transfers between devices with their start and end apart: 20, of which 5 were waited for; matrix products, arithmetic and copies ran while one was open for 2% of the time, Pallas kernels for 22%

profile of v3, /device:TPU:1, one launch (start us, length us, event | category | flops | bytes accessed | tf_op | source)
XLA Modules:
  0.0 136.5 jit_solution(12015553256924895664)
XLA Ops:
  0.0 10.6 %shard_map.37 = (bf16[8,4,32,512]{3,2,1,0:T(8,128)(2,1)}, bf16[8,5,32,512]{3,2,1,0:T(8,128)(2,1)}) custom-call(s32[32]{0:T(128)} %refs_0_.1, bf16[32,1024,128]{2,1,0:T(8,128)(2,1)} %bitcast.3, bf16[32,512]{1,0:T(8,128)(2,1)} %refs_2_.1), custom_call_target="tpu_custom_call" | custom-call | flops 11000 | bytes 1000 | tf_op jit(solution)/shard_map/pallas_call | solution.py:89
  10.6 22.8 %all_to_all.10.own_ref = bf16[8,4,32,512]{3,2,1,0:T(8,128)(2,1)} all-to-all(bf16[8,4,32,512]{3,2,1,0:T(8,128)(2,1)} %get-tuple-element.23), channel_id=1, replica_groups=mesh['blk'=16,'bin'=8] {'bin'}, dimensions={0} | all-to-all | bytes 2097152 | tf_op jit(solution)/shard_map/all_to_all | solution.py:322
  33.5 3.6 %all-to-all-start.1 = ((bf16[8,5,32,512]{3,2,1,0:T(8,128)(2,1)}), bf16[8,5,32,512]{3,2,1,0:T(8,128)(2,1)S(1)}, u32[]{:S(2)}, u32[]{:S(2)}) async-start(bf16[8,5,32,512]{3,2,1,0:T(8,128)(2,1)} %get-tuple-element.24), calls=%async_computation.1 | async-start | bytes 2621440 | tf_op jit(solution)/shard_map/all_to_all | solution.py:322
  37.0 1.7 %collective-permute-start.1 = (bf16[8,4,32,512]{3,2,1,0:T(8,128)(2,1)}, bf16[8,4,32,512]{3,2,1,0:T(8,128)(2,1)}, u32[]{:S(2)}, u32[]{:S(2)}) collective-permute-start(bf16[8,4,32,512]{3,2,1,0:T(8,128)(2,1)} %all_to_all.10.own_ref), channel_id=1, source_target_pairs={{48,0},{56,8},{0,16},{8,24},{16,32},{24,40},{32,48},{40,56},{112,6... | collective-permute-start | bytes 3145736 | tf_op jit(solution)/shard_map/ppermute | solution.py:292
  38.7 2.2 %collective-permute-start = (bf16[8,4,32,512]{3,2,1,0:T(8,128)(2,1)}, bf16[8,4,32,512]{3,2,1,0:T(8,128)(2,1)}, u32[]{:S(2)}, u32[]{:S(2)}) collective-permute-start(bf16[8,4,32,512]{3,2,1,0:T(8,128)(2,1)} %all_to_all.10.own_ref), channel_id=1, source_target_pairs={{16,0},{24,8},{32,16},{40,24},{48,32},{56,40},{0,48},{8,56},{80,64... | collective-permute-start | bytes 3145736 | tf_op jit(solution)/shard_map/ppermute | solution.py:292
  40.9 13.3 %all-to-all-done.1 = bf16[8,5,32,512]{3,2,1,0:T(8,128)(2,1)S(1)} async-done(((bf16[8,5,32,512]{3,2,1,0:T(8,128)(2,1)}), bf16[8,5,32,512]{3,2,1,0:T(8,128)(2,1)S(1)}, u32[]{:S(2)}, u32[]{:S(2)}) %all-to-all-start.1) | async-done | bytes 1310752 | tf_op jit(solution)/shard_map/all_to_all | solution.py:322
  55.3 1.7 %collective-permute-start.2 = (bf16[8,1,32,512]{3,2,1,0:T(8,128)(2,1)S(1)}, bf16[8,1,32,512]{3,2,1,0:T(8,128)(2,1)S(1)}, u32[]{:S(2)}, u32[]{:S(2)}) collective-permute-start(bf16[8,1,32,512]{3,2,1,0:T(8,128)(2,1)S(1)} %slice.9.own_ref), channel_id=1, source_target_pairs={{48,0},{56,8},{0,16},{8,24},{16,32},{24,40},{32,48},{40,56},{112,6... | collective-permute-start | bytes 786440 | tf_op jit(solution)/shard_map/ppermute | solution.py:292
  57.0 2.7 %shard_map.38.refs_3_.refs_2_ = bf16[2,1024,512]{2,1,0:T(8,128)(2,1)} custom-call(bf16[8,4,32,512]{3,2,1,0:T(8,128)(2,1)} %all_to_all.10.own_ref), custom_call_target="tpu_custom_call" | custom-call | flops 1500 | bytes 1000 | tf_op jit(solution)/shard_map/pallas_call | solution.py:124
  59.7 2.3 %collective-permute-start.6 = (bf16[8,1,32,512]{3,2,1,0:T(8,128)(2,1)S(1)}, bf16[8,1,32,512]{3,2,1,0:T(8,128)(2,1)S(1)}, u32[]{:S(2)}, u32[]{:S(2)}) collective-permute-start(bf16[8,1,32,512]{3,2,1,0:T(8,128)(2,1)S(1)} %slice.9.own_ref), channel_id=1, source_target_pairs={{16,0},{24,8},{32,16},{40,24},{48,32},{56,40},{64,48},{72,56},{80,... | collective-permute-start | bytes 786440 | tf_op jit(solution)/shard_map/ppermute | solution.py:292
  62.0 2.3 %slice.8.own_ref = bf16[8,4,32,512]{3,2,1,0:T(8,128)(2,1)} slice(bf16[8,5,32,512]{3,2,1,0:T(8,128)(2,1)} %copy-done.4), slice={[0:8], [0:4], [0:32], [0:512]} | slice | bytes 2097152 | tf_op jit(solution)/shard_map/slice | solution.py:330
  64.3 3.4 %collective-permute-done.2 = bf16[8,1,32,512]{3,2,1,0:T(8,128)(2,1)S(1)} collective-permute-done((bf16[8,1,32,512]{3,2,1,0:T(8,128)(2,1)S(1)}, bf16[8,1,32,512]{3,2,1,0:T(8,128)(2,1)S(1)}, u32[]{:S(2)}, u32[]{:S(2)}) %collective-permute-start.2) | collective-permute-done | bytes 262176 | tf_op jit(solution)/shard_map/ppermute | solution.py:292
  67.7 2.8 %collective-permute-start.3 = (bf16[8,4,32,512]{3,2,1,0:T(8,128)(2,1)}, bf16[8,4,32,512]{3,2,1,0:T(8,128)(2,1)}, u32[]{:S(2)}, u32[]{:S(2)}) collective-permute-start(bf16[8,4,32,512]{3,2,1,0:T(8,128)(2,1)} %slice.8.own_ref), channel_id=1, source_target_pairs={{16,0},{24,8},{32,16},{40,24},{48,32},{56,40},{64,48},{72,56},{80,... | collective-permute-start | bytes 3145736 | tf_op jit(solution)/shard_map/ppermute | solution.py:292
  70.5 2.7 %shard_map.40.refs_2_ = bf16[2,1024,512]{2,1,0:T(8,128)(2,1)} custom-call(bf16[8,4,32,512]{3,2,1,0:T(8,128)(2,1)} %slice.8.own_ref), custom_call_target="tpu_custom_call" | custom-call | flops 1500 | bytes 1000 | tf_op jit(solution)/shard_map/pallas_call | solution.py:124
  73.2 1.6 %collective-permute-start.4 = (bf16[8,4,32,512]{3,2,1,0:T(8,128)(2,1)}, bf16[8,4,32,512]{3,2,1,0:T(8,128)(2,1)}, u32[]{:S(2)}, u32[]{:S(2)}) collective-permute-start(bf16[8,4,32,512]{3,2,1,0:T(8,128)(2,1)} %collective-permute-done.refs_7_), channel_id=1, source_target_pairs={{112,48},{120,56},{48,112},{56,120},{113,49},{121,57},{49,113},{57... | collective-permute-start | bytes 3145736 | tf_op jit(solution)/shard_map/ppermute | solution.py:292
  74.8 3.7 %collective-permute-start.17 = (bf16[8,4,32,512]{3,2,1,0:T(8,128)(2,1)}, bf16[8,4,32,512]{3,2,1,0:T(8,128)(2,1)}, u32[]{:S(2)}, u32[]{:S(2)}) collective-permute-start(bf16[8,4,32,512]{3,2,1,0:T(8,128)(2,1)} %all_to_all.10.own_ref), channel_id=1, source_target_pairs={{0,8},{8,0},{16,24},{24,16},{32,40},{40,32},{48,56},{56,48},{64,72... | collective-permute-start | bytes 3145736 | tf_op jit(solution)/shard_map/ppermute | solution.py:309
  78.5 17.9 %collective-permute-done.8.both_ref = bf16[8,1,32,512]{3,2,1,0:T(8,128)(2,1)} collective-permute-done((bf16[8,1,32,512]{3,2,1,0:T(8,128)(2,1)S(1)}, bf16[8,1,32,512]{3,2,1,0:T(8,128)(2,1)}, u32[]{:S(2)}, u32[]{:S(2)}) %collective-permute-start.8) | collective-permute-done | bytes 262176 | tf_op jit(solution)/shard_map/ppermute | solution.py:292
  96.4 4.0 %collective-permute-start.16 = (bf16[8,4,32,512]{3,2,1,0:T(8,128)(2,1)}, bf16[8,4,32,512]{3,2,1,0:T(8,128)(2,1)}, u32[]{:S(2)}, u32[]{:S(2)}) collective-permute-start(bf16[8,4,32,512]{3,2,1,0:T(8,128)(2,1)} %slice.8.own_ref), channel_id=1, source_target_pairs={{0,8},{8,0},{16,24},{24,16},{32,40},{40,32},{48,56},{56,48},{64,72... | collective-permute-start | bytes 3145736 | tf_op jit(solution)/shard_map/ppermute | solution.py:309
  106.2 1.6 %shard_map.42.refs_1_ = f32[2,512,512]{2,1,0:T(8,128)S(1)} custom-call(s32[2]{0:T(128)S(1)} %copy-done.2, bf16[8,1,32,512]{3,2,1,0:T(8,128)(2,1)S(1)} %slice.9.own_ref, bf16[8,1,32,512]{3,2,1,0:T(8,128)(2,1)} %collective-permute-done.15.first_ref, bf16[8,1,32,512]{3,2,1,0:T(8,128)(2,1)S(1)} %collective-permute-done.7.first_ref.second_ref, ...), custom_call_target="tpu_custom_call" | custom-call | flops 1000 | bytes 1000 | tf_op jit(solution)/shard_map/pallas_call | solution.py:146
  107.8 1.6 %shard_map.41.refs_1_ = f32[2,512,512]{2,1,0:T(8,128)S(1)} custom-call(s32[2]{0:T(128)S(1)} %copy-done.2, bf16[8,1,32,512]{3,2,1,0:T(8,128)(2,1)S(1)} %slice.9.own_ref, bf16[8,1,32,512]{3,2,1,0:T(8,128)(2,1)S(1)} %collective-permute-done.7.first_ref.second_ref, bf16[8,1,32,512]{3,2,1,0:T(8,128)(2,1)} %collective-permute-done.9.second_ref, ...), custom_call_target="tpu_custom_call" | custom-call | flops 1000 | bytes 1000 | tf_op jit(solution)/shard_map/pallas_call | solution.py:146
  109.6 11.3 %shard_map.43.refs_7_ = bf16[4,2,4,512,512]{4,3,2,1,0:T(8,128)(2,1)} custom-call(s32[2]{0:T(128)S(1)} %copy-done.3, f32[2,512,512]{2,1,0:T(8,128)S(1)} %shard_map.42.refs_1_, bf16[2,1024,512]{2,1,0:T(8,128)(2,1)S(1)} %copy-done, bf16[2,1024,512]{2,1,0:T(8,128)(2,1)S(1)} %copy-done.1, bf16[8,4,32,512]{3,2,1,0:T(8,128)(2,1)} %collective-permute-done.3.refs_4_, ...), custom_call_target="tpu_custom_call" | custom-call | flops 1000 | bytes 1000 | tf_op jit(solution)/shard_map/pallas_call | solution.py:228
  120.9 5.4 %shard_map.44.refs_4_ = bf16[4,2,4,512,512]{4,3,2,1,0:T(8,128)(2,1)} custom-call(s32[2]{0:T(128)S(1)} %copy-done.3, f32[2,512,512]{2,1,0:T(8,128)S(1)} %shard_map.41.refs_1_, bf16[2,1024,512]{2,1,0:T(8,128)(2,1)S(1)} %copy-done.1, bf16[8,4,32,512]{3,2,1,0:T(8,128)(2,1)} %collective-permute-done.5.refs_3_, ...), custom_call_target="tpu_custom_call", output_to_operand_aliasing={{}: (7, {})} | custom-call | flops 1000 | bytes 1000 | tf_op jit(solution)/shard_map/pallas_call | solution.py:228
  126.3 3.0 %collective-permute-done.11.refs_3_ = bf16[8,4,32,512]{3,2,1,0:T(8,128)(2,1)S(1)} collective-permute-done((bf16[8,4,32,512]{3,2,1,0:T(8,128)(2,1)}, bf16[8,4,32,512]{3,2,1,0:T(8,128)(2,1)S(1)}, u32[]{:S(2)}, u32[]{:S(2)}) %collective-permute-start.11) | collective-permute-done | bytes 1048608 | tf_op jit(solution)/shard_map/ppermute | solution.py:292
  130.4 3.0 %shard_map.45.refs_5_ = bf16[4,2,4,512,512]{4,3,2,1,0:T(8,128)(2,1)} custom-call(s32[2]{0:T(128)S(1)} %copy-done.3, f32[2,512,512]{2,1,0:T(8,128)S(1)} %shard_map.41.refs_1_, bf16[2,1024,512]{2,1,0:T(8,128)(2,1)S(1)} %copy-done, bf16[8,4,32,512]{3,2,1,0:T(8,128)(2,1)S(1)} %collective-permute-done.11.refs_3_, ...), custom_call_target="tpu_custom_call", output_to_operand_aliasing={{}: (4, {})} | custom-call | flops 1000 | bytes 1000 | tf_op jit(solution)/shard_map/pallas_call | solution.py:228
  133.4 3.1 %shard_map.46 = bf16[4,2,4,512,512]{4,3,2,1,0:T(8,128)(2,1)} custom-call(s32[2]{0:T(128)S(1)} %copy-done.3, f32[2,512,512]{2,1,0:T(8,128)S(1)} %shard_map.41.refs_1_, bf16[2,1024,512]{2,1,0:T(8,128)(2,1)S(1)} %copy-done, bf16[8,4,32,512]{3,2,1,0:T(8,128)(2,1)S(1)} %collective-permute-done.10.refs_6_.refs_3_, ...), custom_call_target="tpu_custom_call", output_to_operand_aliasing={{}: (5, {})} | custom-call | flops 1000 | bytes 1000 | tf_op jit(solution)/shard_map/pallas_call | solution.py:228
  (40 shorter events, 8.0 us)
Async XLA Ops:
  33.5 20.8 %all-to-all-start.1 = ((bf16[8,5,32,512]{3,2,1,0:T(8,128)(2,1)}), bf16[8,5,32,512]{3,2,1,0:T(8,128)(2,1)S(1)}, u32[]{:S(2)}, u32[]{:S(2)}) async-start(bf16[8,5,32,512]{3,2,1,0:T(8,128)(2,1)} %get-tuple-element.24), calls=%async_computation.1 | async-start | bytes 2621440 | tf_op jit(solution)/shard_map/all_to_all | solution.py:322
  37.0 27.3 %collective-permute-start.1 = (bf16[8,4,32,512]{3,2,1,0:T(8,128)(2,1)}, bf16[8,4,32,512]{3,2,1,0:T(8,128)(2,1)}, u32[]{:S(2)}, u32[]{:S(2)}) collective-permute-start(bf16[8,4,32,512]{3,2,1,0:T(8,128)(2,1)} %all_to_all.10.own_ref), channel_id=1, source_target_pairs={{48,0},{56,8},{0,16},{8,24},{16,32},{24,40},{32,48},{40,56},{112,6... | collective-permute-start | bytes 3145736 | tf_op jit(solution)/shard_map/ppermute | solution.py:292
  38.7 25.6 %collective-permute-start = (bf16[8,4,32,512]{3,2,1,0:T(8,128)(2,1)}, bf16[8,4,32,512]{3,2,1,0:T(8,128)(2,1)}, u32[]{:S(2)}, u32[]{:S(2)}) collective-permute-start(bf16[8,4,32,512]{3,2,1,0:T(8,128)(2,1)} %all_to_all.10.own_ref), channel_id=1, source_target_pairs={{16,0},{24,8},{32,16},{40,24},{48,32},{56,40},{0,48},{8,56},{80,64... | collective-permute-start | bytes 3145736 | tf_op jit(solution)/shard_map/ppermute | solution.py:292
  54.2 1.1 copy-start.4
  55.3 12.4 %collective-permute-start.2 = (bf16[8,1,32,512]{3,2,1,0:T(8,128)(2,1)S(1)}, bf16[8,1,32,512]{3,2,1,0:T(8,128)(2,1)S(1)}, u32[]{:S(2)}, u32[]{:S(2)}) collective-permute-start(bf16[8,1,32,512]{3,2,1,0:T(8,128)(2,1)S(1)} %slice.9.own_ref), channel_id=1, source_target_pairs={{48,0},{56,8},{0,16},{8,24},{16,32},{24,40},{32,48},{40,56},{112,6... | collective-permute-start | bytes 786440 | tf_op jit(solution)/shard_map/ppermute | solution.py:292
  59.7 15.1 %collective-permute-start.6 = (bf16[8,1,32,512]{3,2,1,0:T(8,128)(2,1)S(1)}, bf16[8,1,32,512]{3,2,1,0:T(8,128)(2,1)S(1)}, u32[]{:S(2)}, u32[]{:S(2)}) collective-permute-start(bf16[8,1,32,512]{3,2,1,0:T(8,128)(2,1)S(1)} %slice.9.own_ref), channel_id=1, source_target_pairs={{16,0},{24,8},{32,16},{40,24},{48,32},{56,40},{64,48},{72,56},{80,... | collective-permute-start | bytes 786440 | tf_op jit(solution)/shard_map/ppermute | solution.py:292
  67.7 32.7 %collective-permute-start.5 = (bf16[8,4,32,512]{3,2,1,0:T(8,128)(2,1)}, bf16[8,4,32,512]{3,2,1,0:T(8,128)(2,1)}, u32[]{:S(2)}, u32[]{:S(2)}) collective-permute-start(bf16[8,4,32,512]{3,2,1,0:T(8,128)(2,1)} %collective-permute-done.1), channel_id=1, source_target_pairs={{48,0},{56,8},{0,16},{8,24},{80,32},{88,40},{96,48},{104,56},{112,... | collective-permute-start | bytes 3145736 | tf_op jit(solution)/shard_map/ppermute | solution.py:292
  67.7 32.7 %collective-permute-start.3 = (bf16[8,4,32,512]{3,2,1,0:T(8,128)(2,1)}, bf16[8,4,32,512]{3,2,1,0:T(8,128)(2,1)}, u32[]{:S(2)}, u32[]{:S(2)}) collective-permute-start(bf16[8,4,32,512]{3,2,1,0:T(8,128)(2,1)} %slice.8.own_ref), channel_id=1, source_target_pairs={{16,0},{24,8},{32,16},{40,24},{48,32},{56,40},{64,48},{72,56},{80,... | collective-permute-start | bytes 3145736 | tf_op jit(solution)/shard_map/ppermute | solution.py:292
  73.2 27.7 %collective-permute-start.4 = (bf16[8,4,32,512]{3,2,1,0:T(8,128)(2,1)}, bf16[8,4,32,512]{3,2,1,0:T(8,128)(2,1)}, u32[]{:S(2)}, u32[]{:S(2)}) collective-permute-start(bf16[8,4,32,512]{3,2,1,0:T(8,128)(2,1)} %collective-permute-done.refs_7_), channel_id=1, source_target_pairs={{112,48},{120,56},{48,112},{56,120},{113,49},{121,57},{49,113},{57... | collective-permute-start | bytes 3145736 | tf_op jit(solution)/shard_map/ppermute | solution.py:292
  74.8 21.6 %collective-permute-start.8 = (bf16[8,1,32,512]{3,2,1,0:T(8,128)(2,1)S(1)}, bf16[8,1,32,512]{3,2,1,0:T(8,128)(2,1)}, u32[]{:S(2)}, u32[]{:S(2)}) collective-permute-start(bf16[8,1,32,512]{3,2,1,0:T(8,128)(2,1)S(1)} %collective-permute-done.2), channel_id=1, source_target_pairs={{48,0},{56,8},{0,16},{8,24},{80,32},{88,40},{96,48},{104,56},{112,... | collective-permute-start | bytes 786440 | tf_op jit(solution)/shard_map/ppermute | solution.py:292
  74.8 28.0 %collective-permute-start.17 = (bf16[8,4,32,512]{3,2,1,0:T(8,128)(2,1)}, bf16[8,4,32,512]{3,2,1,0:T(8,128)(2,1)}, u32[]{:S(2)}, u32[]{:S(2)}) collective-permute-start(bf16[8,4,32,512]{3,2,1,0:T(8,128)(2,1)} %all_to_all.10.own_ref), channel_id=1, source_target_pairs={{0,8},{8,0},{16,24},{24,16},{32,40},{40,32},{48,56},{56,48},{64,72... | collective-permute-start | bytes 3145736 | tf_op jit(solution)/shard_map/ppermute | solution.py:309
  96.4 8.2 %collective-permute-start.16 = (bf16[8,4,32,512]{3,2,1,0:T(8,128)(2,1)}, bf16[8,4,32,512]{3,2,1,0:T(8,128)(2,1)}, u32[]{:S(2)}, u32[]{:S(2)}) collective-permute-start(bf16[8,4,32,512]{3,2,1,0:T(8,128)(2,1)} %slice.8.own_ref), channel_id=1, source_target_pairs={{0,8},{8,0},{16,24},{24,16},{32,40},{40,32},{48,56},{56,48},{64,72... | collective-permute-start | bytes 3145736 | tf_op jit(solution)/shard_map/ppermute | solution.py:309
  100.4 3.4 %collective-permute-start.15 = (bf16[8,1,32,512]{3,2,1,0:T(8,128)(2,1)S(1)}, bf16[8,1,32,512]{3,2,1,0:T(8,128)(2,1)}, u32[]{:S(2)}, u32[]{:S(2)}) collective-permute-start(bf16[8,1,32,512]{3,2,1,0:T(8,128)(2,1)S(1)} %slice.9.own_ref), channel_id=1, source_target_pairs={{0,8},{8,0},{16,24},{24,16},{32,40},{40,32},{48,56},{56,48},{64,72... | collective-permute-start | bytes 786440 | tf_op jit(solution)/shard_map/ppermute | solution.py:309
  100.4 3.5 %collective-permute-start.7 = (bf16[8,1,32,512]{3,2,1,0:T(8,128)(2,1)S(1)}, bf16[8,1,32,512]{3,2,1,0:T(8,128)(2,1)S(1)}, u32[]{:S(2)}, u32[]{:S(2)}) collective-permute-start(bf16[8,1,32,512]{3,2,1,0:T(8,128)(2,1)S(1)} %collective-permute-done.6.both_ref), channel_id=1, source_target_pairs={{0,8},{8,0},{16,24},{24,16},{32,40},{40,32},{48,56},{56,48},{64,72... | collective-permute-start | bytes 786440 | tf_op jit(solution)/shard_map/ppermute | solution.py:309
  100.9 3.4 %collective-permute-start.9 = (bf16[8,1,32,512]{3,2,1,0:T(8,128)(2,1)}, bf16[8,1,32,512]{3,2,1,0:T(8,128)(2,1)}, u32[]{:S(2)}, u32[]{:S(2)}) collective-permute-start(bf16[8,1,32,512]{3,2,1,0:T(8,128)(2,1)} %collective-permute-done.8.both_ref), channel_id=1, source_target_pairs={{0,8},{8,0},{16,24},{24,16},{32,40},{40,32},{48,56},{56,48},{64,72... | collective-permute-start | bytes 786440 | tf_op jit(solution)/shard_map/ppermute | solution.py:309
  102.9 6.6 %collective-permute-start.12 = (bf16[8,4,32,512]{3,2,1,0:T(8,128)(2,1)}, bf16[8,4,32,512]{3,2,1,0:T(8,128)(2,1)S(1)}, u32[]{:S(2)}, u32[]{:S(2)}) collective-permute-start(bf16[8,4,32,512]{3,2,1,0:T(8,128)(2,1)} %collective-permute-done.refs_7_), channel_id=1, source_target_pairs={{0,8},{8,0},{16,24},{24,16},{32,40},{40,32},{48,56},{56,48},{64,72... | collective-permute-start | bytes 3145736 | tf_op jit(solution)/shard_map/ppermute | solution.py:309
  103.8 5.7 %collective-permute-start.13 = (bf16[8,4,32,512]{3,2,1,0:T(8,128)(2,1)}, bf16[8,4,32,512]{3,2,1,0:T(8,128)(2,1)S(1)}, u32[]{:S(2)}, u32[]{:S(2)}) collective-permute-start(bf16[8,4,32,512]{3,2,1,0:T(8,128)(2,1)} %collective-permute-done.4.refs_8_), channel_id=1, source_target_pairs={{0,8},{8,0},{16,24},{24,16},{32,40},{40,32},{48,56},{56,48},{64,72... | collective-permute-start | bytes 3145736 | tf_op jit(solution)/shard_map/ppermute | solution.py:309
  104.0 5.5 %collective-permute-start.10 = (bf16[8,4,32,512]{3,2,1,0:T(8,128)(2,1)}, bf16[8,4,32,512]{3,2,1,0:T(8,128)(2,1)S(1)}, u32[]{:S(2)}, u32[]{:S(2)}) collective-permute-start(bf16[8,4,32,512]{3,2,1,0:T(8,128)(2,1)} %collective-permute-done.3.refs_4_), channel_id=1, source_target_pairs={{0,8},{8,0},{16,24},{24,16},{32,40},{40,32},{48,56},{56,48},{64,72... | collective-permute-start | bytes 3145736 | tf_op jit(solution)/shard_map/ppermute | solution.py:309
  104.3 16.5 %collective-permute-start.14 = (bf16[8,4,32,512]{3,2,1,0:T(8,128)(2,1)}, bf16[8,4,32,512]{3,2,1,0:T(8,128)(2,1)S(1)}, u32[]{:S(2)}, u32[]{:S(2)}) collective-permute-start(bf16[8,4,32,512]{3,2,1,0:T(8,128)(2,1)} %collective-permute-done.5.refs_3_), channel_id=1, source_target_pairs={{0,8},{8,0},{16,24},{24,16},{32,40},{40,32},{48,56},{56,48},{64,72... | collective-permute-start | bytes 3145736 | tf_op jit(solution)/shard_map/ppermute | solution.py:309
  104.6 24.8 %collective-permute-start.11 = (bf16[8,4,32,512]{3,2,1,0:T(8,128)(2,1)}, bf16[8,4,32,512]{3,2,1,0:T(8,128)(2,1)S(1)}, u32[]{:S(2)}, u32[]{:S(2)}) collective-permute-start(bf16[8,4,32,512]{3,2,1,0:T(8,128)(2,1)} %collective-permute-done.3.refs_4_), channel_id=1, source_target_pairs={{16,0},{24,8},{32,16},{40,24},{48,32},{56,40},{64,48},{72,56},{80,... | collective-permute-start | bytes 3145736 | tf_op jit(solution)/shard_map/ppermute | solution.py:292
  106.2 3.3 %copy-start.1 = (bf16[2,1024,512]{2,1,0:T(8,128)(2,1)S(1)}, bf16[2,1024,512]{2,1,0:T(8,128)(2,1)}, u32[]{:S(2)}) copy-start(bf16[2,1024,512]{2,1,0:T(8,128)(2,1)} %shard_map.38.refs_3_.refs_2_) | copy-start | bytes 6291460
  107.8 1.8 %copy-start = (bf16[2,1024,512]{2,1,0:T(8,128)(2,1)S(1)}, bf16[2,1024,512]{2,1,0:T(8,128)(2,1)}, u32[]{:S(2)}) copy-start(bf16[2,1024,512]{2,1,0:T(8,128)(2,1)} %shard_map.40.refs_2_) | copy-start | bytes 6291460
  107.8 1.8 %copy-start.3 = (s32[2]{0:T(128)S(1)}, s32[2]{0:T(128)}, u32[]{:S(2)}) copy-start(s32[2]{0:T(128)} %shard_map.39.where_ref.refs_0_) | copy-start | bytes 28
  129.3 4.1 %collective-permute-start.18 = (bf16[8,4,32,512]{3,2,1,0:T(8,128)(2,1)S(1)}, bf16[8,4,32,512]{3,2,1,0:T(8,128)(2,1)S(1)}, u32[]{:S(2)}, u32[]{:S(2)}) collective-permute-start(bf16[8,4,32,512]{3,2,1,0:T(8,128)(2,1)S(1)} %collective-permute-done.11.refs_3_), channel_id=1, source_target_pairs={{0,8},{8,0},{16,24},{24,16},{32,40},{40,32},{48,56},{56,48},{64,72... | collective-permute-start | bytes 3145736 | tf_op jit(solution)/shard_map/ppermute | solution.py:309
  (1 other events, 0.6 us)

commit v4 on v3

--- a/solution.py
+++ b/solution.py
@@ -166,7 +166,7 @@
         other = other_ref[...].reshape(depth, channels)
         for part in range(2):
             for i in range(CHUNKS):
-                left = left_ref[n, part * channels + i * rows:part * channels + (i + 1) * rows]
+                left = left_ref[n if left_ref.shape[0] > 1 else 0, part * channels + i * rows:part * channels + (i + 1) * rows]
                 product = jnp.dot(left, other, preferred_element_type=jnp.float32)
                 weight = weight_ref[r, i * rows:(i + 1) * rows]
                 out_ref[part, i * rows:(i + 1) * rows] = (product * weight).astype(jnp.bfloat16)
@@ -208,6 +208,8 @@
 
     def spec(value, job):
         if job is None:
+            if len(plan) == 1:
+                return pl.BlockSpec((1, double, depth), lambda g: (g, 0, 0))
             return pl.BlockSpec(value.shape, lambda g: (0, 0, 0), pipeline_mode=pl.Buffered(1))
         shares, _, windows, _ = value.shape
         return pl.BlockSpec(

time: 137 us -> 137 us (level)
  no operation moved by 1% of the time
where the time goes in v4:
time: 137 us
  Pallas kernels  43.3 us (32%)
  waiting for transfers between devices  38.1 us (28%)
  starting transfers between devices  27.5 us (20%)
  blocking collectives  22.8 us (17%)
  local copies, waits for them, and re-layouts  4.11 us (3%)
    ppermute x9, waiting for transfers between devices, moved(): lax.ppermute(value, 'blk', [(2 * s + c, 2 * t + c) for s, t in pairs for...  24.3 us
    pallas_call x4, Pallas kernels, cross(): pl.pallas_call(lambda *refs: cross_kernel(*refs, jobs=plan, deep=deep, ro...  22.8 us
    all_to_all x1, blocking collectives, to_bins(): return lax.all_to_all(value, 'bin', split_axis=0, concat_axis=0, tiled=True)  22.8 us
    ppermute x9, starting transfers between devices, moved(): lax.ppermute(value, 'blk', [(2 * s + c, 2 * t + c) for s, t in pairs for...  13.3 us
    all_to_all x1, waiting for transfers between devices, to_bins(): return lax.all_to_all(value, 'bin', split_axis=0, concat_axis=0, tiled=True)  13.3 us
    pallas_call x1, Pallas kernels, whiten(): pl.pallas_call(lambda *refs: whiten_kernel(*refs, channels=channels, kept...  10.6 us
    ppermute x10, starting transfers between devices, swapped(): return lax.ppermute(value, 'blk', [(i, i ^ 1) for i in range(blocks)])  10.6 us
    pallas_call x2, Pallas kernels, turn(): pl.pallas_call(turn_kernel, grid=(deep,), in_specs=[pl.BlockSpec((shares,...  5.41 us
  transfers between devices with their start and end apart: 20, of which 5 were waited for; matrix products, arithmetic and copies ran while one was open for 2% of the time, Pallas kernels for 22%

profile of v4, /device:TPU:1, one launch (start us, length us, event | category | flops | bytes accessed | tf_op | source)
XLA Modules:
  0.0 136.5 jit_solution(4814822050395780640)
XLA Ops:
  0.0 10.6 %shard_map.37 = (bf16[8,4,32,512]{3,2,1,0:T(8,128)(2,1)}, bf16[8,5,32,512]{3,2,1,0:T(8,128)(2,1)}) custom-call(s32[32]{0:T(128)} %refs_0_.1, bf16[32,1024,128]{2,1,0:T(8,128)(2,1)} %bitcast.3, bf16[32,512]{1,0:T(8,128)(2,1)} %refs_2_.1), custom_call_target="tpu_custom_call" | custom-call | flops 11000 | bytes 1000 | tf_op jit(solution)/shard_map/pallas_call | solution.py:89
  10.6 22.8 %all_to_all.10.own_ref = bf16[8,4,32,512]{3,2,1,0:T(8,128)(2,1)} all-to-all(bf16[8,4,32,512]{3,2,1,0:T(8,128)(2,1)} %get-tuple-element.23), channel_id=1, replica_groups=mesh['blk'=16,'bin'=8] {'bin'}, dimensions={0} | all-to-all | bytes 2097152 | tf_op jit(solution)/shard_map/all_to_all | solution.py:324
  33.5 3.6 %all-to-all-start.1 = ((bf16[8,5,32,512]{3,2,1,0:T(8,128)(2,1)}), bf16[8,5,32,512]{3,2,1,0:T(8,128)(2,1)S(1)}, u32[]{:S(2)}, u32[]{:S(2)}) async-start(bf16[8,5,32,512]{3,2,1,0:T(8,128)(2,1)} %get-tuple-element.24), calls=%async_computation.1 | async-start | bytes 2621440 | tf_op jit(solution)/shard_map/all_to_all | solution.py:324
  37.0 1.7 %collective-permute-start.1 = (bf16[8,4,32,512]{3,2,1,0:T(8,128)(2,1)}, bf16[8,4,32,512]{3,2,1,0:T(8,128)(2,1)}, u32[]{:S(2)}, u32[]{:S(2)}) collective-permute-start(bf16[8,4,32,512]{3,2,1,0:T(8,128)(2,1)} %all_to_all.10.own_ref), channel_id=1, source_target_pairs={{48,0},{56,8},{0,16},{8,24},{16,32},{24,40},{32,48},{40,56},{112,6... | collective-permute-start | bytes 3145736 | tf_op jit(solution)/shard_map/ppermute | solution.py:294
  38.7 2.2 %collective-permute-start = (bf16[8,4,32,512]{3,2,1,0:T(8,128)(2,1)}, bf16[8,4,32,512]{3,2,1,0:T(8,128)(2,1)}, u32[]{:S(2)}, u32[]{:S(2)}) collective-permute-start(bf16[8,4,32,512]{3,2,1,0:T(8,128)(2,1)} %all_to_all.10.own_ref), channel_id=1, source_target_pairs={{16,0},{24,8},{32,16},{40,24},{48,32},{56,40},{0,48},{8,56},{80,64... | collective-permute-start | bytes 3145736 | tf_op jit(solution)/shard_map/ppermute | solution.py:294
  40.9 13.3 %all-to-all-done.1 = bf16[8,5,32,512]{3,2,1,0:T(8,128)(2,1)S(1)} async-done(((bf16[8,5,32,512]{3,2,1,0:T(8,128)(2,1)}), bf16[8,5,32,512]{3,2,1,0:T(8,128)(2,1)S(1)}, u32[]{:S(2)}, u32[]{:S(2)}) %all-to-all-start.1) | async-done | bytes 1310752 | tf_op jit(solution)/shard_map/all_to_all | solution.py:324
  55.3 1.7 %collective-permute-start.2 = (bf16[8,1,32,512]{3,2,1,0:T(8,128)(2,1)S(1)}, bf16[8,1,32,512]{3,2,1,0:T(8,128)(2,1)S(1)}, u32[]{:S(2)}, u32[]{:S(2)}) collective-permute-start(bf16[8,1,32,512]{3,2,1,0:T(8,128)(2,1)S(1)} %slice.9.own_ref), channel_id=1, source_target_pairs={{48,0},{56,8},{0,16},{8,24},{16,32},{24,40},{32,48},{40,56},{112,6... | collective-permute-start | bytes 786440 | tf_op jit(solution)/shard_map/ppermute | solution.py:294
  57.0 2.7 %shard_map.38.refs_3_.refs_2_ = bf16[2,1024,512]{2,1,0:T(8,128)(2,1)} custom-call(bf16[8,4,32,512]{3,2,1,0:T(8,128)(2,1)} %all_to_all.10.own_ref), custom_call_target="tpu_custom_call" | custom-call | flops 1500 | bytes 1000 | tf_op jit(solution)/shard_map/pallas_call | solution.py:124
  59.7 2.3 %collective-permute-start.6 = (bf16[8,1,32,512]{3,2,1,0:T(8,128)(2,1)S(1)}, bf16[8,1,32,512]{3,2,1,0:T(8,128)(2,1)S(1)}, u32[]{:S(2)}, u32[]{:S(2)}) collective-permute-start(bf16[8,1,32,512]{3,2,1,0:T(8,128)(2,1)S(1)} %slice.9.own_ref), channel_id=1, source_target_pairs={{16,0},{24,8},{32,16},{40,24},{48,32},{56,40},{64,48},{72,56},{80,... | collective-permute-start | bytes 786440 | tf_op jit(solution)/shard_map/ppermute | solution.py:294
  62.0 2.3 %slice.8.own_ref = bf16[8,4,32,512]{3,2,1,0:T(8,128)(2,1)} slice(bf16[8,5,32,512]{3,2,1,0:T(8,128)(2,1)} %copy-done.4), slice={[0:8], [0:4], [0:32], [0:512]} | slice | bytes 2097152 | tf_op jit(solution)/shard_map/slice | solution.py:332
  64.3 3.4 %collective-permute-done.2 = bf16[8,1,32,512]{3,2,1,0:T(8,128)(2,1)S(1)} collective-permute-done((bf16[8,1,32,512]{3,2,1,0:T(8,128)(2,1)S(1)}, bf16[8,1,32,512]{3,2,1,0:T(8,128)(2,1)S(1)}, u32[]{:S(2)}, u32[]{:S(2)}) %collective-permute-start.2) | collective-permute-done | bytes 262176 | tf_op jit(solution)/shard_map/ppermute | solution.py:294
  67.7 2.8 %collective-permute-start.3 = (bf16[8,4,32,512]{3,2,1,0:T(8,128)(2,1)}, bf16[8,4,32,512]{3,2,1,0:T(8,128)(2,1)}, u32[]{:S(2)}, u32[]{:S(2)}) collective-permute-start(bf16[8,4,32,512]{3,2,1,0:T(8,128)(2,1)} %slice.8.own_ref), channel_id=1, source_target_pairs={{16,0},{24,8},{32,16},{40,24},{48,32},{56,40},{64,48},{72,56},{80,... | collective-permute-start | bytes 3145736 | tf_op jit(solution)/shard_map/ppermute | solution.py:294
  70.5 2.7 %shard_map.40.refs_2_ = bf16[2,1024,512]{2,1,0:T(8,128)(2,1)} custom-call(bf16[8,4,32,512]{3,2,1,0:T(8,128)(2,1)} %slice.8.own_ref), custom_call_target="tpu_custom_call" | custom-call | flops 1500 | bytes 1000 | tf_op jit(solution)/shard_map/pallas_call | solution.py:124
  73.2 1.6 %collective-permute-start.4 = (bf16[8,4,32,512]{3,2,1,0:T(8,128)(2,1)}, bf16[8,4,32,512]{3,2,1,0:T(8,128)(2,1)}, u32[]{:S(2)}, u32[]{:S(2)}) collective-permute-start(bf16[8,4,32,512]{3,2,1,0:T(8,128)(2,1)} %collective-permute-done.refs_7_), channel_id=1, source_target_pairs={{112,48},{120,56},{48,112},{56,120},{113,49},{121,57},{49,113},{57... | collective-permute-start | bytes 3145736 | tf_op jit(solution)/shard_map/ppermute | solution.py:294
  74.8 3.7 %collective-permute-start.17 = (bf16[8,4,32,512]{3,2,1,0:T(8,128)(2,1)}, bf16[8,4,32,512]{3,2,1,0:T(8,128)(2,1)}, u32[]{:S(2)}, u32[]{:S(2)}) collective-permute-start(bf16[8,4,32,512]{3,2,1,0:T(8,128)(2,1)} %all_to_all.10.own_ref), channel_id=1, source_target_pairs={{0,8},{8,0},{16,24},{24,16},{32,40},{40,32},{48,56},{56,48},{64,72... | collective-permute-start | bytes 3145736 | tf_op jit(solution)/shard_map/ppermute | solution.py:311
  78.5 17.9 %collective-permute-done.8.both_ref = bf16[8,1,32,512]{3,2,1,0:T(8,128)(2,1)} collective-permute-done((bf16[8,1,32,512]{3,2,1,0:T(8,128)(2,1)S(1)}, bf16[8,1,32,512]{3,2,1,0:T(8,128)(2,1)}, u32[]{:S(2)}, u32[]{:S(2)}) %collective-permute-start.8) | collective-permute-done | bytes 262176 | tf_op jit(solution)/shard_map/ppermute | solution.py:294
  96.4 4.0 %collective-permute-start.16 = (bf16[8,4,32,512]{3,2,1,0:T(8,128)(2,1)}, bf16[8,4,32,512]{3,2,1,0:T(8,128)(2,1)}, u32[]{:S(2)}, u32[]{:S(2)}) collective-permute-start(bf16[8,4,32,512]{3,2,1,0:T(8,128)(2,1)} %slice.8.own_ref), channel_id=1, source_target_pairs={{0,8},{8,0},{16,24},{24,16},{32,40},{40,32},{48,56},{56,48},{64,72... | collective-permute-start | bytes 3145736 | tf_op jit(solution)/shard_map/ppermute | solution.py:311
  106.2 1.6 %shard_map.42.refs_1_ = f32[2,512,512]{2,1,0:T(8,128)S(1)} custom-call(s32[2]{0:T(128)S(1)} %copy-done.2, bf16[8,1,32,512]{3,2,1,0:T(8,128)(2,1)S(1)} %slice.9.own_ref, bf16[8,1,32,512]{3,2,1,0:T(8,128)(2,1)} %collective-permute-done.15.first_ref, bf16[8,1,32,512]{3,2,1,0:T(8,128)(2,1)S(1)} %collective-permute-done.7.first_ref.second_ref, ...), custom_call_target="tpu_custom_call" | custom-call | flops 1000 | bytes 1000 | tf_op jit(solution)/shard_map/pallas_call | solution.py:146
  107.8 1.6 %shard_map.41.refs_1_ = f32[2,512,512]{2,1,0:T(8,128)S(1)} custom-call(s32[2]{0:T(128)S(1)} %copy-done.2, bf16[8,1,32,512]{3,2,1,0:T(8,128)(2,1)S(1)} %slice.9.own_ref, bf16[8,1,32,512]{3,2,1,0:T(8,128)(2,1)S(1)} %collective-permute-done.7.first_ref.second_ref, bf16[8,1,32,512]{3,2,1,0:T(8,128)(2,1)} %collective-permute-done.9.second_ref, ...), custom_call_target="tpu_custom_call" | custom-call | flops 1000 | bytes 1000 | tf_op jit(solution)/shard_map/pallas_call | solution.py:146
  109.6 11.3 %shard_map.43.refs_7_ = bf16[4,2,4,512,512]{4,3,2,1,0:T(8,128)(2,1)} custom-call(s32[2]{0:T(128)S(1)} %copy-done.3, f32[2,512,512]{2,1,0:T(8,128)S(1)} %shard_map.42.refs_1_, bf16[2,1024,512]{2,1,0:T(8,128)(2,1)S(1)} %copy-done, bf16[2,1024,512]{2,1,0:T(8,128)(2,1)S(1)} %copy-done.1, bf16[8,4,32,512]{3,2,1,0:T(8,128)(2,1)} %collective-permute-done.3.refs_4_, ...), custom_call_target="tpu_custom_call" | custom-call | flops 1000 | bytes 1000 | tf_op jit(solution)/shard_map/pallas_call | solution.py:230
  120.9 5.4 %shard_map.44.refs_4_ = bf16[4,2,4,512,512]{4,3,2,1,0:T(8,128)(2,1)} custom-call(s32[2]{0:T(128)S(1)} %copy-done.3, f32[2,512,512]{2,1,0:T(8,128)S(1)} %shard_map.41.refs_1_, bf16[2,1024,512]{2,1,0:T(8,128)(2,1)S(1)} %copy-done.1, bf16[8,4,32,512]{3,2,1,0:T(8,128)(2,1)} %collective-permute-done.5.refs_3_, ...), custom_call_target="tpu_custom_call", output_to_operand_aliasing={{}: (7, {})} | custom-call | flops 1000 | bytes 1000 | tf_op jit(solution)/shard_map/pallas_call | solution.py:230
  126.3 3.0 %collective-permute-done.11.refs_3_ = bf16[8,4,32,512]{3,2,1,0:T(8,128)(2,1)S(1)} collective-permute-done((bf16[8,4,32,512]{3,2,1,0:T(8,128)(2,1)}, bf16[8,4,32,512]{3,2,1,0:T(8,128)(2,1)S(1)}, u32[]{:S(2)}, u32[]{:S(2)}) %collective-permute-start.11) | collective-permute-done | bytes 1048608 | tf_op jit(solution)/shard_map/ppermute | solution.py:294
  130.4 3.0 %shard_map.45.refs_5_ = bf16[4,2,4,512,512]{4,3,2,1,0:T(8,128)(2,1)} custom-call(s32[2]{0:T(128)S(1)} %copy-done.3, f32[2,512,512]{2,1,0:T(8,128)S(1)} %shard_map.41.refs_1_, bf16[2,1024,512]{2,1,0:T(8,128)(2,1)S(1)} %copy-done, bf16[8,4,32,512]{3,2,1,0:T(8,128)(2,1)S(1)} %collective-permute-done.11.refs_3_, ...), custom_call_target="tpu_custom_call", output_to_operand_aliasing={{}: (4, {})} | custom-call | flops 1000 | bytes 1000 | tf_op jit(solution)/shard_map/pallas_call | solution.py:230
  133.4 3.1 %shard_map.46 = bf16[4,2,4,512,512]{4,3,2,1,0:T(8,128)(2,1)} custom-call(s32[2]{0:T(128)S(1)} %copy-done.3, f32[2,512,512]{2,1,0:T(8,128)S(1)} %shard_map.41.refs_1_, bf16[2,1024,512]{2,1,0:T(8,128)(2,1)S(1)} %copy-done, bf16[8,4,32,512]{3,2,1,0:T(8,128)(2,1)S(1)} %collective-permute-done.10.refs_6_.refs_3_, ...), custom_call_target="tpu_custom_call", output_to_operand_aliasing={{}: (5, {})} | custom-call | flops 1000 | bytes 1000 | tf_op jit(solution)/shard_map/pallas_call | solution.py:230
  (40 shorter events, 8.0 us)
Async XLA Ops:
  33.5 20.8 %all-to-all-start.1 = ((bf16[8,5,32,512]{3,2,1,0:T(8,128)(2,1)}), bf16[8,5,32,512]{3,2,1,0:T(8,128)(2,1)S(1)}, u32[]{:S(2)}, u32[]{:S(2)}) async-start(bf16[8,5,32,512]{3,2,1,0:T(8,128)(2,1)} %get-tuple-element.24), calls=%async_computation.1 | async-start | bytes 2621440 | tf_op jit(solution)/shard_map/all_to_all | solution.py:324
  37.0 27.3 %collective-permute-start.1 = (bf16[8,4,32,512]{3,2,1,0:T(8,128)(2,1)}, bf16[8,4,32,512]{3,2,1,0:T(8,128)(2,1)}, u32[]{:S(2)}, u32[]{:S(2)}) collective-permute-start(bf16[8,4,32,512]{3,2,1,0:T(8,128)(2,1)} %all_to_all.10.own_ref), channel_id=1, source_target_pairs={{48,0},{56,8},{0,16},{8,24},{16,32},{24,40},{32,48},{40,56},{112,6... | collective-permute-start | bytes 3145736 | tf_op jit(solution)/shard_map/ppermute | solution.py:294
  38.7 25.6 %collective-permute-start = (bf16[8,4,32,512]{3,2,1,0:T(8,128)(2,1)}, bf16[8,4,32,512]{3,2,1,0:T(8,128)(2,1)}, u32[]{:S(2)}, u32[]{:S(2)}) collective-permute-start(bf16[8,4,32,512]{3,2,1,0:T(8,128)(2,1)} %all_to_all.10.own_ref), channel_id=1, source_target_pairs={{16,0},{24,8},{32,16},{40,24},{48,32},{56,40},{0,48},{8,56},{80,64... | collective-permute-start | bytes 3145736 | tf_op jit(solution)/shard_map/ppermute | solution.py:294
  54.2 1.1 copy-start.4
  55.3 12.4 %collective-permute-start.2 = (bf16[8,1,32,512]{3,2,1,0:T(8,128)(2,1)S(1)}, bf16[8,1,32,512]{3,2,1,0:T(8,128)(2,1)S(1)}, u32[]{:S(2)}, u32[]{:S(2)}) collective-permute-start(bf16[8,1,32,512]{3,2,1,0:T(8,128)(2,1)S(1)} %slice.9.own_ref), channel_id=1, source_target_pairs={{48,0},{56,8},{0,16},{8,24},{16,32},{24,40},{32,48},{40,56},{112,6... | collective-permute-start | bytes 786440 | tf_op jit(solution)/shard_map/ppermute | solution.py:294
  59.7 15.1 %collective-permute-start.6 = (bf16[8,1,32,512]{3,2,1,0:T(8,128)(2,1)S(1)}, bf16[8,1,32,512]{3,2,1,0:T(8,128)(2,1)S(1)}, u32[]{:S(2)}, u32[]{:S(2)}) collective-permute-start(bf16[8,1,32,512]{3,2,1,0:T(8,128)(2,1)S(1)} %slice.9.own_ref), channel_id=1, source_target_pairs={{16,0},{24,8},{32,16},{40,24},{48,32},{56,40},{64,48},{72,56},{80,... | collective-permute-start | bytes 786440 | tf_op jit(solution)/shard_map/ppermute | solution.py:294
  67.7 32.7 %collective-permute-start.5 = (bf16[8,4,32,512]{3,2,1,0:T(8,128)(2,1)}, bf16[8,4,32,512]{3,2,1,0:T(8,128)(2,1)}, u32[]{:S(2)}, u32[]{:S(2)}) collective-permute-start(bf16[8,4,32,512]{3,2,1,0:T(8,128)(2,1)} %collective-permute-done.1), channel_id=1, source_target_pairs={{48,0},{56,8},{0,16},{8,24},{80,32},{88,40},{96,48},{104,56},{112,... | collective-permute-start | bytes 3145736 | tf_op jit(solution)/shard_map/ppermute | solution.py:294
  67.7 32.7 %collective-permute-start.3 = (bf16[8,4,32,512]{3,2,1,0:T(8,128)(2,1)}, bf16[8,4,32,512]{3,2,1,0:T(8,128)(2,1)}, u32[]{:S(2)}, u32[]{:S(2)}) collective-permute-start(bf16[8,4,32,512]{3,2,1,0:T(8,128)(2,1)} %slice.8.own_ref), channel_id=1, source_target_pairs={{16,0},{24,8},{32,16},{40,24},{48,32},{56,40},{64,48},{72,56},{80,... | collective-permute-start | bytes 3145736 | tf_op jit(solution)/shard_map/ppermute | solution.py:294
  73.2 27.7 %collective-permute-start.4 = (bf16[8,4,32,512]{3,2,1,0:T(8,128)(2,1)}, bf16[8,4,32,512]{3,2,1,0:T(8,128)(2,1)}, u32[]{:S(2)}, u32[]{:S(2)}) collective-permute-start(bf16[8,4,32,512]{3,2,1,0:T(8,128)(2,1)} %collective-permute-done.refs_7_), channel_id=1, source_target_pairs={{112,48},{120,56},{48,112},{56,120},{113,49},{121,57},{49,113},{57... | collective-permute-start | bytes 3145736 | tf_op jit(solution)/shard_map/ppermute | solution.py:294
  74.8 21.6 %collective-permute-start.8 = (bf16[8,1,32,512]{3,2,1,0:T(8,128)(2,1)S(1)}, bf16[8,1,32,512]{3,2,1,0:T(8,128)(2,1)}, u32[]{:S(2)}, u32[]{:S(2)}) collective-permute-start(bf16[8,1,32,512]{3,2,1,0:T(8,128)(2,1)S(1)} %collective-permute-done.2), channel_id=1, source_target_pairs={{48,0},{56,8},{0,16},{8,24},{80,32},{88,40},{96,48},{104,56},{112,... | collective-permute-start | bytes 786440 | tf_op jit(solution)/shard_map/ppermute | solution.py:294
  74.8 28.0 %collective-permute-start.17 = (bf16[8,4,32,512]{3,2,1,0:T(8,128)(2,1)}, bf16[8,4,32,512]{3,2,1,0:T(8,128)(2,1)}, u32[]{:S(2)}, u32[]{:S(2)}) collective-permute-start(bf16[8,4,32,512]{3,2,1,0:T(8,128)(2,1)} %all_to_all.10.own_ref), channel_id=1, source_target_pairs={{0,8},{8,0},{16,24},{24,16},{32,40},{40,32},{48,56},{56,48},{64,72... | collective-permute-start | bytes 3145736 | tf_op jit(solution)/shard_map/ppermute | solution.py:311
  96.4 8.2 %collective-permute-start.16 = (bf16[8,4,32,512]{3,2,1,0:T(8,128)(2,1)}, bf16[8,4,32,512]{3,2,1,0:T(8,128)(2,1)}, u32[]{:S(2)}, u32[]{:S(2)}) collective-permute-start(bf16[8,4,32,512]{3,2,1,0:T(8,128)(2,1)} %slice.8.own_ref), channel_id=1, source_target_pairs={{0,8},{8,0},{16,24},{24,16},{32,40},{40,32},{48,56},{56,48},{64,72... | collective-permute-start | bytes 3145736 | tf_op jit(solution)/shard_map/ppermute | solution.py:311
  100.4 3.4 %collective-permute-start.15 = (bf16[8,1,32,512]{3,2,1,0:T(8,128)(2,1)S(1)}, bf16[8,1,32,512]{3,2,1,0:T(8,128)(2,1)}, u32[]{:S(2)}, u32[]{:S(2)}) collective-permute-start(bf16[8,1,32,512]{3,2,1,0:T(8,128)(2,1)S(1)} %slice.9.own_ref), channel_id=1, source_target_pairs={{0,8},{8,0},{16,24},{24,16},{32,40},{40,32},{48,56},{56,48},{64,72... | collective-permute-start | bytes 786440 | tf_op jit(solution)/shard_map/ppermute | solution.py:311
  100.4 3.5 %collective-permute-start.7 = (bf16[8,1,32,512]{3,2,1,0:T(8,128)(2,1)S(1)}, bf16[8,1,32,512]{3,2,1,0:T(8,128)(2,1)S(1)}, u32[]{:S(2)}, u32[]{:S(2)}) collective-permute-start(bf16[8,1,32,512]{3,2,1,0:T(8,128)(2,1)S(1)} %collective-permute-done.6.both_ref), channel_id=1, source_target_pairs={{0,8},{8,0},{16,24},{24,16},{32,40},{40,32},{48,56},{56,48},{64,72... | collective-permute-start | bytes 786440 | tf_op jit(solution)/shard_map/ppermute | solution.py:311
  100.9 3.4 %collective-permute-start.9 = (bf16[8,1,32,512]{3,2,1,0:T(8,128)(2,1)}, bf16[8,1,32,512]{3,2,1,0:T(8,128)(2,1)}, u32[]{:S(2)}, u32[]{:S(2)}) collective-permute-start(bf16[8,1,32,512]{3,2,1,0:T(8,128)(2,1)} %collective-permute-done.8.both_ref), channel_id=1, source_target_pairs={{0,8},{8,0},{16,24},{24,16},{32,40},{40,32},{48,56},{56,48},{64,72... | collective-permute-start | bytes 786440 | tf_op jit(solution)/shard_map/ppermute | solution.py:311
  102.9 6.6 %collective-permute-start.12 = (bf16[8,4,32,512]{3,2,1,0:T(8,128)(2,1)}, bf16[8,4,32,512]{3,2,1,0:T(8,128)(2,1)S(1)}, u32[]{:S(2)}, u32[]{:S(2)}) collective-permute-start(bf16[8,4,32,512]{3,2,1,0:T(8,128)(2,1)} %collective-permute-done.refs_7_), channel_id=1, source_target_pairs={{0,8},{8,0},{16,24},{24,16},{32,40},{40,32},{48,56},{56,48},{64,72... | collective-permute-start | bytes 3145736 | tf_op jit(solution)/shard_map/ppermute | solution.py:311
  103.8 5.7 %collective-permute-start.13 = (bf16[8,4,32,512]{3,2,1,0:T(8,128)(2,1)}, bf16[8,4,32,512]{3,2,1,0:T(8,128)(2,1)S(1)}, u32[]{:S(2)}, u32[]{:S(2)}) collective-permute-start(bf16[8,4,32,512]{3,2,1,0:T(8,128)(2,1)} %collective-permute-done.4.refs_8_), channel_id=1, source_target_pairs={{0,8},{8,0},{16,24},{24,16},{32,40},{40,32},{48,56},{56,48},{64,72... | collective-permute-start | bytes 3145736 | tf_op jit(solution)/shard_map/ppermute | solution.py:311
  104.0 5.5 %collective-permute-start.10 = (bf16[8,4,32,512]{3,2,1,0:T(8,128)(2,1)}, bf16[8,4,32,512]{3,2,1,0:T(8,128)(2,1)S(1)}, u32[]{:S(2)}, u32[]{:S(2)}) collective-permute-start(bf16[8,4,32,512]{3,2,1,0:T(8,128)(2,1)} %collective-permute-done.3.refs_4_), channel_id=1, source_target_pairs={{0,8},{8,0},{16,24},{24,16},{32,40},{40,32},{48,56},{56,48},{64,72... | collective-permute-start | bytes 3145736 | tf_op jit(solution)/shard_map/ppermute | solution.py:311
  104.3 16.5 %collective-permute-start.14 = (bf16[8,4,32,512]{3,2,1,0:T(8,128)(2,1)}, bf16[8,4,32,512]{3,2,1,0:T(8,128)(2,1)S(1)}, u32[]{:S(2)}, u32[]{:S(2)}) collective-permute-start(bf16[8,4,32,512]{3,2,1,0:T(8,128)(2,1)} %collective-permute-done.5.refs_3_), channel_id=1, source_target_pairs={{0,8},{8,0},{16,24},{24,16},{32,40},{40,32},{48,56},{56,48},{64,72... | collective-permute-start | bytes 3145736 | tf_op jit(solution)/shard_map/ppermute | solution.py:311
  104.6 24.8 %collective-permute-start.11 = (bf16[8,4,32,512]{3,2,1,0:T(8,128)(2,1)}, bf16[8,4,32,512]{3,2,1,0:T(8,128)(2,1)S(1)}, u32[]{:S(2)}, u32[]{:S(2)}) collective-permute-start(bf16[8,4,32,512]{3,2,1,0:T(8,128)(2,1)} %collective-permute-done.3.refs_4_), channel_id=1, source_target_pairs={{16,0},{24,8},{32,16},{40,24},{48,32},{56,40},{64,48},{72,56},{80,... | collective-permute-start | bytes 3145736 | tf_op jit(solution)/shard_map/ppermute | solution.py:294
  106.2 3.3 %copy-start.1 = (bf16[2,1024,512]{2,1,0:T(8,128)(2,1)S(1)}, bf16[2,1024,512]{2,1,0:T(8,128)(2,1)}, u32[]{:S(2)}) copy-start(bf16[2,1024,512]{2,1,0:T(8,128)(2,1)} %shard_map.38.refs_3_.refs_2_) | copy-start | bytes 6291460
  107.8 1.8 %copy-start = (bf16[2,1024,512]{2,1,0:T(8,128)(2,1)S(1)}, bf16[2,1024,512]{2,1,0:T(8,128)(2,1)}, u32[]{:S(2)}) copy-start(bf16[2,1024,512]{2,1,0:T(8,128)(2,1)} %shard_map.40.refs_2_) | copy-start | bytes 6291460
  107.8 1.8 %copy-start.3 = (s32[2]{0:T(128)S(1)}, s32[2]{0:T(128)}, u32[]{:S(2)}) copy-start(s32[2]{0:T(128)} %shard_map.39.where_ref.refs_0_) | copy-start | bytes 28
  129.3 4.1 %collective-permute-start.18 = (bf16[8,4,32,512]{3,2,1,0:T(8,128)(2,1)S(1)}, bf16[8,4,32,512]{3,2,1,0:T(8,128)(2,1)S(1)}, u32[]{:S(2)}, u32[]{:S(2)}) collective-permute-start(bf16[8,4,32,512]{3,2,1,0:T(8,128)(2,1)S(1)} %collective-permute-done.11.refs_3_), channel_id=1, source_target_pairs={{0,8},{8,0},{16,24},{24,16},{32,40},{40,32},{48,56},{56,48},{64,72... | collective-permute-start | bytes 3145736 | tf_op jit(solution)/shard_map/ppermute | solution.py:311
  (1 other events, 0.6 us)

commit v5 on v4

--- a/solution.py
+++ b/solution.py
@@ -55,14 +55,18 @@
         sums = lax.dot_general(
             band[...], jnp.concatenate([high, low], 1), along, preferred_element_type=jnp.float32
         )
-        both = jnp.concatenate([real.astype(jnp.bfloat16), imag.astype(jnp.bfloat16)], 1)
-        picked = lax.dot_general(picker[...], both, along, preferred_element_type=jnp.float32)
+        picked = [
+            lax.dot_general(
+                picker[:kept, :FB], value.astype(jnp.bfloat16), along, preferred_element_type=jnp.float32
+            )
+            for value in (real, imag)
+        ]
         level = sums[kept:kept + 1] * (0.1 / FB) + 1e-06
         scale = lax.rsqrt(sums[:kept] * (1.0 / (2 * HALF_SPAN + 1)) + level)
         window = step * WIN_STEP + k
         gain = quality[pl.ds(window, 1), :] * scale
         local = lax.rem(window, WIN_GROUP)
-        value = jnp.concatenate([picked[:kept] * gain, picked[kept:] * gain], 0)
+        value = jnp.concatenate([picked[0] * gain, picked[1] * gain], 0)
         for c in range(0, channels, 128):
             staged[c // 128, pl.ds(local, 2 * kept, stride=WIN_GROUP), :] = value[:, c:c + 128]
 

time: 137 us -> 137 us (level)
  no operation moved by 1% of the time
where the time goes in v5:
time: 137 us; the launch traced here: 136 us
  Pallas kernels  43.1 us (31%)
  waiting for transfers between devices  38.1 us (28%)
  starting transfers between devices  27.5 us (20%)
  blocking collectives  22.8 us (17%)
  local copies, waits for them, and re-layouts  4.11 us (3%)
    ppermute x9, waiting for transfers between devices, moved(): lax.ppermute(value, 'blk', [(2 * s + c, 2 * t + c) for s, t in pairs for...  24.3 us
    pallas_call x4, Pallas kernels, cross(): pl.pallas_call(lambda *refs: cross_kernel(*refs, jobs=plan, deep=deep, ro...  22.8 us
    all_to_all x1, blocking collectives, to_bins(): return lax.all_to_all(value, 'bin', split_axis=0, concat_axis=0, tiled=True)  22.8 us
    all_to_all x1, waiting for transfers between devices, to_bins(): return lax.all_to_all(value, 'bin', split_axis=0, concat_axis=0, tiled=True)  13.3 us
    ppermute x9, starting transfers between devices, moved(): lax.ppermute(value, 'blk', [(2 * s + c, 2 * t + c) for s, t in pairs for...  13.3 us
    ppermute x10, starting transfers between devices, swapped(): return lax.ppermute(value, 'blk', [(i, i ^ 1) for i in range(blocks)])  10.6 us
    pallas_call x1, Pallas kernels, whiten(): pl.pallas_call(lambda *refs: whiten_kernel(*refs, channels=channels, kept...  10.4 us
    pallas_call x2, Pallas kernels, turn(): pl.pallas_call(turn_kernel, grid=(deep,), in_specs=[pl.BlockSpec((shares,...  5.41 us
  transfers between devices with their start and end apart: 20, of which 5 were waited for; matrix products, arithmetic and copies ran while one was open for 2% of the time, Pallas kernels for 22%

profile of v5, /device:TPU:1, one launch (start us, length us, event | category | flops | bytes accessed | tf_op | source)
XLA Modules:
  0.0 136.3 jit_solution(14951328978592644735)
XLA Ops:
  0.0 10.4 %shard_map.37 = (bf16[8,4,32,512]{3,2,1,0:T(8,128)(2,1)}, bf16[8,5,32,512]{3,2,1,0:T(8,128)(2,1)}) custom-call(s32[32]{0:T(128)} %refs_0_.1, bf16[32,1024,128]{2,1,0:T(8,128)(2,1)} %bitcast.3, bf16[32,512]{1,0:T(8,128)(2,1)} %refs_2_.1), custom_call_target="tpu_custom_call" | custom-call | flops 11000 | bytes 1000 | tf_op jit(solution)/shard_map/pallas_call | solution.py:93
  10.4 22.8 %all_to_all.10.own_ref = bf16[8,4,32,512]{3,2,1,0:T(8,128)(2,1)} all-to-all(bf16[8,4,32,512]{3,2,1,0:T(8,128)(2,1)} %get-tuple-element.23), channel_id=1, replica_groups=mesh['blk'=16,'bin'=8] {'bin'}, dimensions={0} | all-to-all | bytes 2097152 | tf_op jit(solution)/shard_map/all_to_all | solution.py:328
  33.2 3.6 %all-to-all-start.1 = ((bf16[8,5,32,512]{3,2,1,0:T(8,128)(2,1)}), bf16[8,5,32,512]{3,2,1,0:T(8,128)(2,1)S(1)}, u32[]{:S(2)}, u32[]{:S(2)}) async-start(bf16[8,5,32,512]{3,2,1,0:T(8,128)(2,1)} %get-tuple-element.24), calls=%async_computation.1 | async-start | bytes 2621440 | tf_op jit(solution)/shard_map/all_to_all | solution.py:328
  36.8 1.7 %collective-permute-start.1 = (bf16[8,4,32,512]{3,2,1,0:T(8,128)(2,1)}, bf16[8,4,32,512]{3,2,1,0:T(8,128)(2,1)}, u32[]{:S(2)}, u32[]{:S(2)}) collective-permute-start(bf16[8,4,32,512]{3,2,1,0:T(8,128)(2,1)} %all_to_all.10.own_ref), channel_id=1, source_target_pairs={{48,0},{56,8},{0,16},{8,24},{16,32},{24,40},{32,48},{40,56},{112,6... | collective-permute-start | bytes 3145736 | tf_op jit(solution)/shard_map/ppermute | solution.py:298
  38.5 2.2 %collective-permute-start = (bf16[8,4,32,512]{3,2,1,0:T(8,128)(2,1)}, bf16[8,4,32,512]{3,2,1,0:T(8,128)(2,1)}, u32[]{:S(2)}, u32[]{:S(2)}) collective-permute-start(bf16[8,4,32,512]{3,2,1,0:T(8,128)(2,1)} %all_to_all.10.own_ref), channel_id=1, source_target_pairs={{16,0},{24,8},{32,16},{40,24},{48,32},{56,40},{0,48},{8,56},{80,64... | collective-permute-start | bytes 3145736 | tf_op jit(solution)/shard_map/ppermute | solution.py:298
  40.7 13.3 %all-to-all-done.1 = bf16[8,5,32,512]{3,2,1,0:T(8,128)(2,1)S(1)} async-done(((bf16[8,5,32,512]{3,2,1,0:T(8,128)(2,1)}), bf16[8,5,32,512]{3,2,1,0:T(8,128)(2,1)S(1)}, u32[]{:S(2)}, u32[]{:S(2)}) %all-to-all-start.1) | async-done | bytes 1310752 | tf_op jit(solution)/shard_map/all_to_all | solution.py:328
  55.1 1.7 %collective-permute-start.2 = (bf16[8,1,32,512]{3,2,1,0:T(8,128)(2,1)S(1)}, bf16[8,1,32,512]{3,2,1,0:T(8,128)(2,1)S(1)}, u32[]{:S(2)}, u32[]{:S(2)}) collective-permute-start(bf16[8,1,32,512]{3,2,1,0:T(8,128)(2,1)S(1)} %slice.9.own_ref), channel_id=1, source_target_pairs={{48,0},{56,8},{0,16},{8,24},{16,32},{24,40},{32,48},{40,56},{112,6... | collective-permute-start | bytes 786440 | tf_op jit(solution)/shard_map/ppermute | solution.py:298
  56.8 2.7 %shard_map.38.refs_3_.refs_2_ = bf16[2,1024,512]{2,1,0:T(8,128)(2,1)} custom-call(bf16[8,4,32,512]{3,2,1,0:T(8,128)(2,1)} %all_to_all.10.own_ref), custom_call_target="tpu_custom_call" | custom-call | flops 1500 | bytes 1000 | tf_op jit(solution)/shard_map/pallas_call | solution.py:128
  59.5 2.3 %collective-permute-start.6 = (bf16[8,1,32,512]{3,2,1,0:T(8,128)(2,1)S(1)}, bf16[8,1,32,512]{3,2,1,0:T(8,128)(2,1)S(1)}, u32[]{:S(2)}, u32[]{:S(2)}) collective-permute-start(bf16[8,1,32,512]{3,2,1,0:T(8,128)(2,1)S(1)} %slice.9.own_ref), channel_id=1, source_target_pairs={{16,0},{24,8},{32,16},{40,24},{48,32},{56,40},{64,48},{72,56},{80,... | collective-permute-start | bytes 786440 | tf_op jit(solution)/shard_map/ppermute | solution.py:298
  61.8 2.3 %slice.8.own_ref = bf16[8,4,32,512]{3,2,1,0:T(8,128)(2,1)} slice(bf16[8,5,32,512]{3,2,1,0:T(8,128)(2,1)} %copy-done.4), slice={[0:8], [0:4], [0:32], [0:512]} | slice | bytes 2097152 | tf_op jit(solution)/shard_map/slice | solution.py:336
  64.1 3.4 %collective-permute-done.2 = bf16[8,1,32,512]{3,2,1,0:T(8,128)(2,1)S(1)} collective-permute-done((bf16[8,1,32,512]{3,2,1,0:T(8,128)(2,1)S(1)}, bf16[8,1,32,512]{3,2,1,0:T(8,128)(2,1)S(1)}, u32[]{:S(2)}, u32[]{:S(2)}) %collective-permute-start.2) | collective-permute-done | bytes 262176 | tf_op jit(solution)/shard_map/ppermute | solution.py:298
  67.5 2.8 %collective-permute-start.3 = (bf16[8,4,32,512]{3,2,1,0:T(8,128)(2,1)}, bf16[8,4,32,512]{3,2,1,0:T(8,128)(2,1)}, u32[]{:S(2)}, u32[]{:S(2)}) collective-permute-start(bf16[8,4,32,512]{3,2,1,0:T(8,128)(2,1)} %slice.8.own_ref), channel_id=1, source_target_pairs={{16,0},{24,8},{32,16},{40,24},{48,32},{56,40},{64,48},{72,56},{80,... | collective-permute-start | bytes 3145736 | tf_op jit(solution)/shard_map/ppermute | solution.py:298
  70.3 2.7 %shard_map.40.refs_2_ = bf16[2,1024,512]{2,1,0:T(8,128)(2,1)} custom-call(bf16[8,4,32,512]{3,2,1,0:T(8,128)(2,1)} %slice.8.own_ref), custom_call_target="tpu_custom_call" | custom-call | flops 1500 | bytes 1000 | tf_op jit(solution)/shard_map/pallas_call | solution.py:128
  73.0 1.6 %collective-permute-start.4 = (bf16[8,4,32,512]{3,2,1,0:T(8,128)(2,1)}, bf16[8,4,32,512]{3,2,1,0:T(8,128)(2,1)}, u32[]{:S(2)}, u32[]{:S(2)}) collective-permute-start(bf16[8,4,32,512]{3,2,1,0:T(8,128)(2,1)} %collective-permute-done.refs_7_), channel_id=1, source_target_pairs={{112,48},{120,56},{48,112},{56,120},{113,49},{121,57},{49,113},{57... | collective-permute-start | bytes 3145736 | tf_op jit(solution)/shard_map/ppermute | solution.py:298
  74.6 3.7 %collective-permute-start.17 = (bf16[8,4,32,512]{3,2,1,0:T(8,128)(2,1)}, bf16[8,4,32,512]{3,2,1,0:T(8,128)(2,1)}, u32[]{:S(2)}, u32[]{:S(2)}) collective-permute-start(bf16[8,4,32,512]{3,2,1,0:T(8,128)(2,1)} %all_to_all.10.own_ref), channel_id=1, source_target_pairs={{0,8},{8,0},{16,24},{24,16},{32,40},{40,32},{48,56},{56,48},{64,72... | collective-permute-start | bytes 3145736 | tf_op jit(solution)/shard_map/ppermute | solution.py:315
  78.3 17.9 %collective-permute-done.8.both_ref = bf16[8,1,32,512]{3,2,1,0:T(8,128)(2,1)} collective-permute-done((bf16[8,1,32,512]{3,2,1,0:T(8,128)(2,1)S(1)}, bf16[8,1,32,512]{3,2,1,0:T(8,128)(2,1)}, u32[]{:S(2)}, u32[]{:S(2)}) %collective-permute-start.8) | collective-permute-done | bytes 262176 | tf_op jit(solution)/shard_map/ppermute | solution.py:298
  96.2 4.0 %collective-permute-start.16 = (bf16[8,4,32,512]{3,2,1,0:T(8,128)(2,1)}, bf16[8,4,32,512]{3,2,1,0:T(8,128)(2,1)}, u32[]{:S(2)}, u32[]{:S(2)}) collective-permute-start(bf16[8,4,32,512]{3,2,1,0:T(8,128)(2,1)} %slice.8.own_ref), channel_id=1, source_target_pairs={{0,8},{8,0},{16,24},{24,16},{32,40},{40,32},{48,56},{56,48},{64,72... | collective-permute-start | bytes 3145736 | tf_op jit(solution)/shard_map/ppermute | solution.py:315
  106.0 1.6 %shard_map.42.refs_1_ = f32[2,512,512]{2,1,0:T(8,128)S(1)} custom-call(s32[2]{0:T(128)S(1)} %copy-done.2, bf16[8,1,32,512]{3,2,1,0:T(8,128)(2,1)S(1)} %slice.9.own_ref, bf16[8,1,32,512]{3,2,1,0:T(8,128)(2,1)} %collective-permute-done.15.first_ref, bf16[8,1,32,512]{3,2,1,0:T(8,128)(2,1)S(1)} %collective-permute-done.7.first_ref.second_ref, ...), custom_call_target="tpu_custom_call" | custom-call | flops 1000 | bytes 1000 | tf_op jit(solution)/shard_map/pallas_call | solution.py:150
  107.6 1.6 %shard_map.41.refs_1_ = f32[2,512,512]{2,1,0:T(8,128)S(1)} custom-call(s32[2]{0:T(128)S(1)} %copy-done.2, bf16[8,1,32,512]{3,2,1,0:T(8,128)(2,1)S(1)} %slice.9.own_ref, bf16[8,1,32,512]{3,2,1,0:T(8,128)(2,1)S(1)} %collective-permute-done.7.first_ref.second_ref, bf16[8,1,32,512]{3,2,1,0:T(8,128)(2,1)} %collective-permute-done.9.second_ref, ...), custom_call_target="tpu_custom_call" | custom-call | flops 1000 | bytes 1000 | tf_op jit(solution)/shard_map/pallas_call | solution.py:150
  109.4 11.3 %shard_map.43.refs_7_ = bf16[4,2,4,512,512]{4,3,2,1,0:T(8,128)(2,1)} custom-call(s32[2]{0:T(128)S(1)} %copy-done.3, f32[2,512,512]{2,1,0:T(8,128)S(1)} %shard_map.42.refs_1_, bf16[2,1024,512]{2,1,0:T(8,128)(2,1)S(1)} %copy-done, bf16[2,1024,512]{2,1,0:T(8,128)(2,1)S(1)} %copy-done.1, bf16[8,4,32,512]{3,2,1,0:T(8,128)(2,1)} %collective-permute-done.3.refs_4_, ...), custom_call_target="tpu_custom_call" | custom-call | flops 1000 | bytes 1000 | tf_op jit(solution)/shard_map/pallas_call | solution.py:234
  120.6 5.4 %shard_map.44.refs_4_ = bf16[4,2,4,512,512]{4,3,2,1,0:T(8,128)(2,1)} custom-call(s32[2]{0:T(128)S(1)} %copy-done.3, f32[2,512,512]{2,1,0:T(8,128)S(1)} %shard_map.41.refs_1_, bf16[2,1024,512]{2,1,0:T(8,128)(2,1)S(1)} %copy-done.1, bf16[8,4,32,512]{3,2,1,0:T(8,128)(2,1)} %collective-permute-done.5.refs_3_, ...), custom_call_target="tpu_custom_call", output_to_operand_aliasing={{}: (7, {})} | custom-call | flops 1000 | bytes 1000 | tf_op jit(solution)/shard_map/pallas_call | solution.py:234
  126.1 3.0 %collective-permute-done.11.refs_3_ = bf16[8,4,32,512]{3,2,1,0:T(8,128)(2,1)S(1)} collective-permute-done((bf16[8,4,32,512]{3,2,1,0:T(8,128)(2,1)}, bf16[8,4,32,512]{3,2,1,0:T(8,128)(2,1)S(1)}, u32[]{:S(2)}, u32[]{:S(2)}) %collective-permute-start.11) | collective-permute-done | bytes 1048608 | tf_op jit(solution)/shard_map/ppermute | solution.py:298
  130.2 3.0 %shard_map.45.refs_5_ = bf16[4,2,4,512,512]{4,3,2,1,0:T(8,128)(2,1)} custom-call(s32[2]{0:T(128)S(1)} %copy-done.3, f32[2,512,512]{2,1,0:T(8,128)S(1)} %shard_map.41.refs_1_, bf16[2,1024,512]{2,1,0:T(8,128)(2,1)S(1)} %copy-done, bf16[8,4,32,512]{3,2,1,0:T(8,128)(2,1)S(1)} %collective-permute-done.11.refs_3_, ...), custom_call_target="tpu_custom_call", output_to_operand_aliasing={{}: (4, {})} | custom-call | flops 1000 | bytes 1000 | tf_op jit(solution)/shard_map/pallas_call | solution.py:234
  133.2 3.1 %shard_map.46 = bf16[4,2,4,512,512]{4,3,2,1,0:T(8,128)(2,1)} custom-call(s32[2]{0:T(128)S(1)} %copy-done.3, f32[2,512,512]{2,1,0:T(8,128)S(1)} %shard_map.41.refs_1_, bf16[2,1024,512]{2,1,0:T(8,128)(2,1)S(1)} %copy-done, bf16[8,4,32,512]{3,2,1,0:T(8,128)(2,1)S(1)} %collective-permute-done.10.refs_6_.refs_3_, ...), custom_call_target="tpu_custom_call", output_to_operand_aliasing={{}: (5, {})} | custom-call | flops 1000 | bytes 1000 | tf_op jit(solution)/shard_map/pallas_call | solution.py:234
  (40 shorter events, 8.0 us)
Async XLA Ops:
  33.2 20.8 %all-to-all-start.1 = ((bf16[8,5,32,512]{3,2,1,0:T(8,128)(2,1)}), bf16[8,5,32,512]{3,2,1,0:T(8,128)(2,1)S(1)}, u32[]{:S(2)}, u32[]{:S(2)}) async-start(bf16[8,5,32,512]{3,2,1,0:T(8,128)(2,1)} %get-tuple-element.24), calls=%async_computation.1 | async-start | bytes 2621440 | tf_op jit(solution)/shard_map/all_to_all | solution.py:328
  36.8 27.3 %collective-permute-start.1 = (bf16[8,4,32,512]{3,2,1,0:T(8,128)(2,1)}, bf16[8,4,32,512]{3,2,1,0:T(8,128)(2,1)}, u32[]{:S(2)}, u32[]{:S(2)}) collective-permute-start(bf16[8,4,32,512]{3,2,1,0:T(8,128)(2,1)} %all_to_all.10.own_ref), channel_id=1, source_target_pairs={{48,0},{56,8},{0,16},{8,24},{16,32},{24,40},{32,48},{40,56},{112,6... | collective-permute-start | bytes 3145736 | tf_op jit(solution)/shard_map/ppermute | solution.py:298
  38.5 25.6 %collective-permute-start = (bf16[8,4,32,512]{3,2,1,0:T(8,128)(2,1)}, bf16[8,4,32,512]{3,2,1,0:T(8,128)(2,1)}, u32[]{:S(2)}, u32[]{:S(2)}) collective-permute-start(bf16[8,4,32,512]{3,2,1,0:T(8,128)(2,1)} %all_to_all.10.own_ref), channel_id=1, source_target_pairs={{16,0},{24,8},{32,16},{40,24},{48,32},{56,40},{0,48},{8,56},{80,64... | collective-permute-start | bytes 3145736 | tf_op jit(solution)/shard_map/ppermute | solution.py:298
  54.0 1.1 copy-start.4
  55.1 12.4 %collective-permute-start.2 = (bf16[8,1,32,512]{3,2,1,0:T(8,128)(2,1)S(1)}, bf16[8,1,32,512]{3,2,1,0:T(8,128)(2,1)S(1)}, u32[]{:S(2)}, u32[]{:S(2)}) collective-permute-start(bf16[8,1,32,512]{3,2,1,0:T(8,128)(2,1)S(1)} %slice.9.own_ref), channel_id=1, source_target_pairs={{48,0},{56,8},{0,16},{8,24},{16,32},{24,40},{32,48},{40,56},{112,6... | collective-permute-start | bytes 786440 | tf_op jit(solution)/shard_map/ppermute | solution.py:298
  59.5 15.1 %collective-permute-start.6 = (bf16[8,1,32,512]{3,2,1,0:T(8,128)(2,1)S(1)}, bf16[8,1,32,512]{3,2,1,0:T(8,128)(2,1)S(1)}, u32[]{:S(2)}, u32[]{:S(2)}) collective-permute-start(bf16[8,1,32,512]{3,2,1,0:T(8,128)(2,1)S(1)} %slice.9.own_ref), channel_id=1, source_target_pairs={{16,0},{24,8},{32,16},{40,24},{48,32},{56,40},{64,48},{72,56},{80,... | collective-permute-start | bytes 786440 | tf_op jit(solution)/shard_map/ppermute | solution.py:298
  67.5 32.7 %collective-permute-start.5 = (bf16[8,4,32,512]{3,2,1,0:T(8,128)(2,1)}, bf16[8,4,32,512]{3,2,1,0:T(8,128)(2,1)}, u32[]{:S(2)}, u32[]{:S(2)}) collective-permute-start(bf16[8,4,32,512]{3,2,1,0:T(8,128)(2,1)} %collective-permute-done.1), channel_id=1, source_target_pairs={{48,0},{56,8},{0,16},{8,24},{80,32},{88,40},{96,48},{104,56},{112,... | collective-permute-start | bytes 3145736 | tf_op jit(solution)/shard_map/ppermute | solution.py:298
  67.5 32.7 %collective-permute-start.3 = (bf16[8,4,32,512]{3,2,1,0:T(8,128)(2,1)}, bf16[8,4,32,512]{3,2,1,0:T(8,128)(2,1)}, u32[]{:S(2)}, u32[]{:S(2)}) collective-permute-start(bf16[8,4,32,512]{3,2,1,0:T(8,128)(2,1)} %slice.8.own_ref), channel_id=1, source_target_pairs={{16,0},{24,8},{32,16},{40,24},{48,32},{56,40},{64,48},{72,56},{80,... | collective-permute-start | bytes 3145736 | tf_op jit(solution)/shard_map/ppermute | solution.py:298
  73.0 27.7 %collective-permute-start.4 = (bf16[8,4,32,512]{3,2,1,0:T(8,128)(2,1)}, bf16[8,4,32,512]{3,2,1,0:T(8,128)(2,1)}, u32[]{:S(2)}, u32[]{:S(2)}) collective-permute-start(bf16[8,4,32,512]{3,2,1,0:T(8,128)(2,1)} %collective-permute-done.refs_7_), channel_id=1, source_target_pairs={{112,48},{120,56},{48,112},{56,120},{113,49},{121,57},{49,113},{57... | collective-permute-start | bytes 3145736 | tf_op jit(solution)/shard_map/ppermute | solution.py:298
  74.6 21.6 %collective-permute-start.8 = (bf16[8,1,32,512]{3,2,1,0:T(8,128)(2,1)S(1)}, bf16[8,1,32,512]{3,2,1,0:T(8,128)(2,1)}, u32[]{:S(2)}, u32[]{:S(2)}) collective-permute-start(bf16[8,1,32,512]{3,2,1,0:T(8,128)(2,1)S(1)} %collective-permute-done.2), channel_id=1, source_target_pairs={{48,0},{56,8},{0,16},{8,24},{80,32},{88,40},{96,48},{104,56},{112,... | collective-permute-start | bytes 786440 | tf_op jit(solution)/shard_map/ppermute | solution.py:298
  74.6 28.0 %collective-permute-start.17 = (bf16[8,4,32,512]{3,2,1,0:T(8,128)(2,1)}, bf16[8,4,32,512]{3,2,1,0:T(8,128)(2,1)}, u32[]{:S(2)}, u32[]{:S(2)}) collective-permute-start(bf16[8,4,32,512]{3,2,1,0:T(8,128)(2,1)} %all_to_all.10.own_ref), channel_id=1, source_target_pairs={{0,8},{8,0},{16,24},{24,16},{32,40},{40,32},{48,56},{56,48},{64,72... | collective-permute-start | bytes 3145736 | tf_op jit(solution)/shard_map/ppermute | solution.py:315
  96.2 8.2 %collective-permute-start.16 = (bf16[8,4,32,512]{3,2,1,0:T(8,128)(2,1)}, bf16[8,4,32,512]{3,2,1,0:T(8,128)(2,1)}, u32[]{:S(2)}, u32[]{:S(2)}) collective-permute-start(bf16[8,4,32,512]{3,2,1,0:T(8,128)(2,1)} %slice.8.own_ref), channel_id=1, source_target_pairs={{0,8},{8,0},{16,24},{24,16},{32,40},{40,32},{48,56},{56,48},{64,72... | collective-permute-start | bytes 3145736 | tf_op jit(solution)/shard_map/ppermute | solution.py:315
  100.2 3.4 %collective-permute-start.15 = (bf16[8,1,32,512]{3,2,1,0:T(8,128)(2,1)S(1)}, bf16[8,1,32,512]{3,2,1,0:T(8,128)(2,1)}, u32[]{:S(2)}, u32[]{:S(2)}) collective-permute-start(bf16[8,1,32,512]{3,2,1,0:T(8,128)(2,1)S(1)} %slice.9.own_ref), channel_id=1, source_target_pairs={{0,8},{8,0},{16,24},{24,16},{32,40},{40,32},{48,56},{56,48},{64,72... | collective-permute-start | bytes 786440 | tf_op jit(solution)/shard_map/ppermute | solution.py:315
  100.2 3.5 %collective-permute-start.7 = (bf16[8,1,32,512]{3,2,1,0:T(8,128)(2,1)S(1)}, bf16[8,1,32,512]{3,2,1,0:T(8,128)(2,1)S(1)}, u32[]{:S(2)}, u32[]{:S(2)}) collective-permute-start(bf16[8,1,32,512]{3,2,1,0:T(8,128)(2,1)S(1)} %collective-permute-done.6.both_ref), channel_id=1, source_target_pairs={{0,8},{8,0},{16,24},{24,16},{32,40},{40,32},{48,56},{56,48},{64,72... | collective-permute-start | bytes 786440 | tf_op jit(solution)/shard_map/ppermute | solution.py:315
  100.7 3.4 %collective-permute-start.9 = (bf16[8,1,32,512]{3,2,1,0:T(8,128)(2,1)}, bf16[8,1,32,512]{3,2,1,0:T(8,128)(2,1)}, u32[]{:S(2)}, u32[]{:S(2)}) collective-permute-start(bf16[8,1,32,512]{3,2,1,0:T(8,128)(2,1)} %collective-permute-done.8.both_ref), channel_id=1, source_target_pairs={{0,8},{8,0},{16,24},{24,16},{32,40},{40,32},{48,56},{56,48},{64,72... | collective-permute-start | bytes 786440 | tf_op jit(solution)/shard_map/ppermute | solution.py:315
  102.7 6.6 %collective-permute-start.12 = (bf16[8,4,32,512]{3,2,1,0:T(8,128)(2,1)}, bf16[8,4,32,512]{3,2,1,0:T(8,128)(2,1)S(1)}, u32[]{:S(2)}, u32[]{:S(2)}) collective-permute-start(bf16[8,4,32,512]{3,2,1,0:T(8,128)(2,1)} %collective-permute-done.refs_7_), channel_id=1, source_target_pairs={{0,8},{8,0},{16,24},{24,16},{32,40},{40,32},{48,56},{56,48},{64,72... | collective-permute-start | bytes 3145736 | tf_op jit(solution)/shard_map/ppermute | solution.py:315
  103.6 5.7 %collective-permute-start.13 = (bf16[8,4,32,512]{3,2,1,0:T(8,128)(2,1)}, bf16[8,4,32,512]{3,2,1,0:T(8,128)(2,1)S(1)}, u32[]{:S(2)}, u32[]{:S(2)}) collective-permute-start(bf16[8,4,32,512]{3,2,1,0:T(8,128)(2,1)} %collective-permute-done.4.refs_8_), channel_id=1, source_target_pairs={{0,8},{8,0},{16,24},{24,16},{32,40},{40,32},{48,56},{56,48},{64,72... | collective-permute-start | bytes 3145736 | tf_op jit(solution)/shard_map/ppermute | solution.py:315
  103.7 5.5 %collective-permute-start.10 = (bf16[8,4,32,512]{3,2,1,0:T(8,128)(2,1)}, bf16[8,4,32,512]{3,2,1,0:T(8,128)(2,1)S(1)}, u32[]{:S(2)}, u32[]{:S(2)}) collective-permute-start(bf16[8,4,32,512]{3,2,1,0:T(8,128)(2,1)} %collective-permute-done.3.refs_4_), channel_id=1, source_target_pairs={{0,8},{8,0},{16,24},{24,16},{32,40},{40,32},{48,56},{56,48},{64,72... | collective-permute-start | bytes 3145736 | tf_op jit(solution)/shard_map/ppermute | solution.py:315
  104.1 16.5 %collective-permute-start.14 = (bf16[8,4,32,512]{3,2,1,0:T(8,128)(2,1)}, bf16[8,4,32,512]{3,2,1,0:T(8,128)(2,1)S(1)}, u32[]{:S(2)}, u32[]{:S(2)}) collective-permute-start(bf16[8,4,32,512]{3,2,1,0:T(8,128)(2,1)} %collective-permute-done.5.refs_3_), channel_id=1, source_target_pairs={{0,8},{8,0},{16,24},{24,16},{32,40},{40,32},{48,56},{56,48},{64,72... | collective-permute-start | bytes 3145736 | tf_op jit(solution)/shard_map/ppermute | solution.py:315
  104.3 24.8 %collective-permute-start.11 = (bf16[8,4,32,512]{3,2,1,0:T(8,128)(2,1)}, bf16[8,4,32,512]{3,2,1,0:T(8,128)(2,1)S(1)}, u32[]{:S(2)}, u32[]{:S(2)}) collective-permute-start(bf16[8,4,32,512]{3,2,1,0:T(8,128)(2,1)} %collective-permute-done.3.refs_4_), channel_id=1, source_target_pairs={{16,0},{24,8},{32,16},{40,24},{48,32},{56,40},{64,48},{72,56},{80,... | collective-permute-start | bytes 3145736 | tf_op jit(solution)/shard_map/ppermute | solution.py:298
  106.0 3.3 %copy-start.1 = (bf16[2,1024,512]{2,1,0:T(8,128)(2,1)S(1)}, bf16[2,1024,512]{2,1,0:T(8,128)(2,1)}, u32[]{:S(2)}) copy-start(bf16[2,1024,512]{2,1,0:T(8,128)(2,1)} %shard_map.38.refs_3_.refs_2_) | copy-start | bytes 6291460
  107.6 1.8 %copy-start = (bf16[2,1024,512]{2,1,0:T(8,128)(2,1)S(1)}, bf16[2,1024,512]{2,1,0:T(8,128)(2,1)}, u32[]{:S(2)}) copy-start(bf16[2,1024,512]{2,1,0:T(8,128)(2,1)} %shard_map.40.refs_2_) | copy-start | bytes 6291460
  107.6 1.8 %copy-start.3 = (s32[2]{0:T(128)S(1)}, s32[2]{0:T(128)}, u32[]{:S(2)}) copy-start(s32[2]{0:T(128)} %shard_map.39.where_ref.refs_0_) | copy-start | bytes 28
  129.1 4.1 %collective-permute-start.18 = (bf16[8,4,32,512]{3,2,1,0:T(8,128)(2,1)S(1)}, bf16[8,4,32,512]{3,2,1,0:T(8,128)(2,1)S(1)}, u32[]{:S(2)}, u32[]{:S(2)}) collective-permute-start(bf16[8,4,32,512]{3,2,1,0:T(8,128)(2,1)S(1)} %collective-permute-done.11.refs_3_), channel_id=1, source_target_pairs={{0,8},{8,0},{16,24},{24,16},{32,40},{40,32},{48,56},{56,48},{64,72... | collective-permute-start | bytes 3145736 | tf_op jit(solution)/shard_map/ppermute | solution.py:315
  (1 other events, 0.6 us)
